TPU v7x, 32 devices: a whole 2x2x4 slice. The times are simulated.
32 devices in a mesh: chan: 4 (over z), lag: 8 (over y, x, core).
Axes of the slice: x: 2, y: 2, z: 4, core: 2. Of those that a mesh axis runs over, the one named last changes fastest.
Arguments:
- raw_samples: bfloat16 [8, 512, 800], P(None, 'chan', 'lag'), may hold values from -6 to 6
- decimation_taps: float32 [16], replicated, may hold values from -1.5 to 1.5
- bandpass_taps: float32 [65], replicated, may hold values from -0.75 to 0.75
Outputs:
- correlations: float32 [512, 3, 512, 128], P('chan', None, 'lag')
All inputs are finite; a program needn't handle non-finite values.
Results may differ from a plain program's by a relative error of at most 0.0055.
Values may be sent and summed in bfloat16 or wider, within the bound.
No kernel may reach another device: no remote copies, remote signals or barrier semaphores. Data moves between devices by JAX's collectives and lax.ppermute only.
A program may use at most 128 MiB of HBM per device.

v0:
```python
import functools
import math

import jax
import jax.numpy as jnp
from jax import lax
from jax.experimental import pallas as pl
from jax.experimental.pallas import tpu as pltpu
from jax.sharding import PartitionSpec as P

NLAG = 512
SUB = 8
LANES = 128
F32 = jnp.float32
BF16 = jnp.bfloat16


def ceil_to(value, unit):
    return -(-value // unit) * unit


class Plan:
    def __init__(self, shape, lag_total, dec_taps, bp_taps):
        self.windows, self.channels, self.raw = shape
        self.lag_total = lag_total
        self.dec_taps, self.bp_taps = dec_taps, bp_taps
        self.dec = self.raw // 2
        self.head = dec_taps // 2
        self.whole = self.dec - self.head
        self.edge = dec_taps - 1
        self.rows = ceil_to(self.whole + 2 * self.edge, SUB)
        self.slot = ceil_to(self.rows, 16)
        self.wide = self.windows * self.channels
        self.total = self.dec * lag_total
        self.half = self.total // 2
        self.depth = ceil_to(self.half + SUB, 16)
        self.deep = self.windows * self.depth
        self.lags = NLAG // lag_total
        self.shifts = self.lags // 2 // SUB
        self.held = lag_total * self.slot
        self.joined = self.held + ceil_to(lag_total * self.head, 16)
        self.pad = NLAG // 4
        self.padded = ceil_to(self.pad + self.depth + NLAG // 4, SUB)


def rounded_tap(taps, index):
    return jnp.full((SUB, LANES), taps[index], F32).astype(BF16).astype(F32)[0:1, 0:1]


def local_kernel(plan, taps_ref, raw_ref, out_ref):
    row = lax.broadcasted_iota(jnp.int32, (plan.rows, plan.raw), 0)
    time = lax.broadcasted_iota(jnp.int32, (plan.rows, plan.raw), 1)
    tap = 2 * (row + plan.head) - time
    table = jnp.zeros((plan.rows, plan.raw), F32)
    for k in range(plan.dec_taps):
        table = jnp.where(tap == k, rounded_tap(taps_ref, k), table)
    last = time - (plan.raw - plan.edge) == row - plan.whole
    first = time == row - plan.whole - plan.edge
    is_last = (row >= plan.whole) & (row < plan.whole + plan.edge)
    is_first = (row >= plan.whole + plan.edge) & (row < plan.whole + 2 * plan.edge)
    picked = jnp.where(is_last & last | is_first & first, 1.0, 0.0)
    table = jnp.where(row < plan.whole, table, picked).astype(BF16)
    for w in range(plan.windows):
        out_ref[:, w * plan.channels : (w + 1) * plan.channels] = lax.dot_general(
            table, raw_ref[w], (((1,), (1,)), ((), ())), preferred_element_type=F32
        ).astype(BF16)


def local_rows(plan, raw, taps):
    return pl.pallas_call(
        functools.partial(local_kernel, plan),
        out_shape=jax.ShapeDtypeStruct((plan.rows, plan.wide), BF16),
        in_specs=[pl.BlockSpec(memory_space=pltpu.SMEM), pl.BlockSpec(memory_space=pltpu.VMEM)],
        out_specs=pl.BlockSpec(memory_space=pltpu.VMEM),
    )(taps, raw)


def table_kernel(plan, dec_ref, bp_ref, even_ref, odd_ref, edge_ref):
    span = ceil_to(plan.total + plan.bp_taps, LANES)
    lane = lax.broadcasted_iota(jnp.int32, (1, span), 1)
    base = jnp.zeros((1, span), F32)
    for k in range(plan.bp_taps):
        base = jnp.where(lane == (span - k) % span, rounded_tap(bp_ref, k), base)
    col = lax.broadcasted_iota(jnp.int32, (span, plan.joined), 1)
    time = lax.broadcasted_iota(jnp.int32, (span, plan.joined), 0)
    at = jnp.full((span, plan.joined), -1, jnp.int32)
    for p in range(plan.lag_total):
        start = col - p * plan.slot
        at = jnp.where((start >= 0) & (start < plan.whole), start + p * plan.dec + plan.head, at)
        start = col - plan.held - p * plan.head
        at = jnp.where((start >= 0) & (start < plan.head), start + p * plan.dec, at)
    order = jnp.where(time == at, 1.0, 0.0).astype(BF16)
    for parity, ref in ((0, even_ref), (1, odd_ref)):
        spread = jnp.broadcast_to(base, (plan.half, span))
        taps = pltpu.roll(spread, parity, 1, stride=2, stride_axis=0)
        ref[...] = jnp.dot(taps.astype(BF16), order, preferred_element_type=F32).astype(BF16)
    rows = plan.joined - plan.held
    row = lax.broadcasted_iota(jnp.int32, (rows, plan.held), 0)
    col = lax.broadcasted_iota(jnp.int32, (rows, plan.held), 1)
    tap = jnp.full((rows, plan.held), -1, jnp.int32)
    for p in range(plan.lag_total):
        j = row - p * plan.head
        mine = (j >= 0) & (j < plan.head)
        r = col - p * plan.slot - plan.whole - plan.edge
        tap = jnp.where(mine & (r >= 0) & (r < plan.edge), 2 * j - r, tap)
        r = col - (p - 1) * plan.slot - plan.whole
        tap = jnp.where(mine & (r >= 0) & (r < plan.edge), 2 * j + plan.edge - r, tap)
    table = jnp.zeros((rows, plan.held), F32)
    for k in range(plan.dec_taps):
        table = jnp.where(tap == k, rounded_tap(dec_ref, k), table)
    edge_ref[...] = table.astype(BF16)


def tables(plan, dec_taps, bp_taps):
    smem, vmem = pl.BlockSpec(memory_space=pltpu.SMEM), pl.BlockSpec(memory_space=pltpu.VMEM)
    return pl.pallas_call(
        functools.partial(table_kernel, plan),
        out_shape=(
            jax.ShapeDtypeStruct((plan.half, plan.joined), BF16),
            jax.ShapeDtypeStruct((plan.half, plan.joined), BF16),
            jax.ShapeDtypeStruct((plan.joined - plan.held, plan.held), BF16),
        ),
        in_specs=[smem, smem],
        out_specs=(vmem, vmem, vmem),
        compiler_params=pltpu.CompilerParams(vmem_limit_bytes=32 * 2**20),
        cost_estimate=pl.CostEstimate(flops=500_000_000, bytes_accessed=2_000_000, transcendentals=0),
    )(dec_taps, bp_taps)


def make_series(plan, place_ref, pieces, tables_refs, held, even, odd, ahead, right):
    even_ref, odd_ref, edge_ref = tables_refs
    place = place_ref[0]
    if plan.slot > plan.rows:
        for p in range(plan.lag_total):
            held[(p + 1) * plan.slot - 16 : (p + 1) * plan.slot, :] = jnp.zeros((16, plan.wide), BF16)
    for p, piece in enumerate(pieces):
        at = pl.multiple_of(lax.bitwise_xor(place, p) * plan.slot, 16)
        held[pl.ds(at, plan.rows), :] = piece[...]
    held[plan.held : plan.joined, :] = jnp.dot(
        edge_ref[...], held[0 : plan.held, :], preferred_element_type=F32
    ).astype(BF16)
    for ref in (even, odd, ahead):
        ref[0 : plan.pad, :] = jnp.zeros((plan.pad, plan.wide), F32)
        ref[plan.pad + plan.half - SUB :, :] = jnp.zeros(
            (plan.padded - plan.pad - plan.half + SUB, plan.wide), F32
        )
    step = 2 * LANES
    for c in range(0, plan.wide, step):
        cols = slice(c, c + step)
        block = held[:, cols]
        a = jnp.dot(even_ref[...], block, preferred_element_type=F32)
        b = jnp.dot(odd_ref[...], block, preferred_element_type=F32)
        power = jnp.sum(a * a + b * b, axis=0, keepdims=True) * (1.0 / plan.total)
        scale = lax.rsqrt(power + 1e-06)
        a = (a * scale).astype(BF16).astype(F32)
        b = (b * scale).astype(BF16).astype(F32)
        even[plan.pad : plan.pad + plan.half, cols] = a
        odd[plan.pad : plan.pad + plan.half, cols] = b
        ahead[plan.pad - 1 : plan.pad - 1 + plan.half, cols] = a
    base = place * (plan.lags // 2)
    for w in range(plan.windows):
        cols = slice(w * plan.channels, (w + 1) * plan.channels)
        rows = slice(w * plan.depth, (w + 1) * plan.depth)
        for s in range(plan.shifts):
            at = pl.ds(pl.multiple_of(base + s * SUB, SUB), plan.depth)
            a, b, c = even[at, cols], odd[at, cols], ahead[at, cols]
            to = slice(s * plan.channels, (s + 1) * plan.channels)
            right[0, rows, to] = b.astype(BF16)
            right[1, rows, to] = (a - b).astype(BF16)
            right[2, rows, to] = (c - b).astype(BF16)


def make_left(plan, even, odd, stack, turned):
    for k, ref in enumerate((even, odd)):
        for w in range(plan.windows):
            stack[w * plan.depth : (w + 1) * plan.depth, :] = ref[
                plan.pad : plan.pad + plan.depth, w * plan.channels : (w + 1) * plan.channels
            ]
        turned[k] = stack[...].T


def shift_left(plan, count, turned, left):
    start = pl.program_id(0) * count

    def pair(k, carry):
        parts = []
        for n in range(2):
            i = start + 2 * k + n
            spread = [jnp.broadcast_to(turned[e, pl.ds(i, 1), :], (SUB, plan.deep)) for e in range(2)]
            parts.append([pltpu.roll(x, 0, 1, stride=1, stride_axis=0) for x in spread])
        a = jnp.concatenate([parts[0][0], parts[1][0]], axis=0)
        b = jnp.concatenate([parts[0][1], parts[1][1]], axis=0)
        rows = pl.ds(pl.multiple_of(k * 16, 16), 16)
        left[0, rows, :] = (a + b).astype(BF16)
        left[1, rows, :] = a.astype(BF16)
        left[2, rows, :] = b.astype(BF16)
        return carry

    lax.fori_loop(0, count // 2, pair, 0)


def correlate(plan, count, left, right, out_ref):
    factor = 1.0 / math.sqrt(plan.windows * plan.total)
    step = min(2 * LANES, plan.shifts * plan.channels)
    for c in range(0, plan.shifts * plan.channels, step):
        cols = slice(c, c + step)
        both, even, odd = (
            jnp.dot(left[k], right[k, :, cols], preferred_element_type=F32) for k in range(3)
        )
        for parity, value in ((0, even), (1, odd)):
            value = (both + value) * factor
            for n in range(step // plan.channels):
                s = c // plan.channels + n
                part = value[:, n * plan.channels : (n + 1) * plan.channels]
                out_ref[:, 0, pl.ds(2 * SUB * s + parity, SUB, stride=2), :] = part.reshape(
                    count, SUB, plan.channels
                )


def own_kernel(plan, count, place_ref, *refs):
    n = plan.lag_total
    pieces, tabs, (out_ref, left_ref) = refs[:n], refs[n : n + 3], refs[n + 3 : n + 5]
    held, even, odd, ahead, right, stack, turned = refs[n + 5 :]

    @pl.when(pl.program_id(0) == 0)
    def _():
        make_series(plan, place_ref, pieces, tabs, held, even, odd, ahead, right)
        make_left(plan, even, odd, stack, turned)

    shift_left(plan, count, turned, left_ref)
    correlate(plan, count, left_ref, right, out_ref)


def other_kernel(plan, count, place_ref, *refs):
    n = plan.lag_total
    pieces, tabs, left_ref, out_ref = refs[:n], refs[n : n + 3], refs[n + 3], refs[n + 5]
    held, even, odd, ahead, right = refs[n + 6 :]

    @pl.when(pl.program_id(0) == 0)
    def _():
        make_series(plan, place_ref, pieces, tabs, held, even, odd, ahead, right)

    correlate(plan, count, left_ref, right, out_ref)


def block_call(plan, count, pairs, distance, place, pieces, tabs, left=None, out=None):
    whole = lambda shape: pl.BlockSpec(shape, lambda i: (0,) * len(shape))
    out_shape = jax.ShapeDtypeStruct((plan.channels, pairs, plan.lags, plan.channels), F32)
    left_shape = jax.ShapeDtypeStruct((3, plan.channels * SUB, plan.deep), BF16)
    out_spec = pl.BlockSpec((count, 1, plan.lags, plan.channels), lambda i: (i, distance, 0, 0))
    left_spec = pl.BlockSpec((3, count * SUB, plan.deep), lambda i: (0, i, 0))
    vmem = pl.BlockSpec(memory_space=pltpu.VMEM)
    in_specs = [pl.BlockSpec(memory_space=pltpu.SMEM)] + [vmem] * (plan.lag_total + 3)
    scratch = [
        pltpu.VMEM((plan.joined, plan.wide), BF16),
        pltpu.VMEM((plan.padded, plan.wide), F32),
        pltpu.VMEM((plan.padded, plan.wide), F32),
        pltpu.VMEM((plan.padded, plan.wide), F32),
        pltpu.VMEM((3, plan.deep, plan.shifts * plan.channels), BF16),
    ]
    flops = 2 * 3 * plan.channels * SUB * plan.deep * plan.shifts * plan.channels
    cost = pl.CostEstimate(flops=flops, bytes_accessed=16 * 2**20, transcendentals=0)
    params = pltpu.CompilerParams(vmem_limit_bytes=48 * 2**20)
    if left is None:
        return pl.pallas_call(
            functools.partial(own_kernel, plan, count),
            grid=(plan.channels // count,),
            out_shape=(out_shape, left_shape),
            in_specs=in_specs,
            out_specs=(out_spec, left_spec),
            scratch_shapes=scratch
            + [pltpu.VMEM((plan.deep, plan.channels), F32), pltpu.VMEM((2, plan.channels, plan.deep), F32)],
            compiler_params=params,
            cost_estimate=cost,
            name="own_block",
        )(place, *pieces, *tabs)
    return pl.pallas_call(
        functools.partial(other_kernel, plan, count),
        grid=(plan.channels // count,),
        out_shape=out_shape,
        in_specs=in_specs + [left_spec, pl.BlockSpec(memory_space=pl.ANY)],
        out_specs=out_spec,
        scratch_shapes=scratch,
        input_output_aliases={len(in_specs) + 1: 0},
        compiler_params=params,
        cost_estimate=cost,
        name="other_block",
    )(place, *pieces, *tabs, left, out)


def swap(piece, mask):
    count = lax.axis_size("lag")
    return lax.ppermute(piece, "lag", [(i ^ mask, i) for i in range(count)])


def from_ahead(piece, distance):
    count = lax.axis_size("chan")
    return lax.ppermute(piece, "chan", [((i + distance) % count, i) for i in range(count)])


def gather_pieces(piece):
    count = lax.axis_size("lag")
    mine = {0: piece}
    for mask in range(2, count, 2):
        mine[mask] = swap(piece, mask)
    for mask in range(0, count, 2):
        mine[mask + 1] = swap(mine[mask], 1)
    return [mine[p] for p in range(count)]


def shards(raw_samples, decimation_taps, bandpass_taps):
    plan = Plan(raw_samples.shape, lax.axis_size("lag"), decimation_taps.shape[0], bandpass_taps.shape[0])
    pairs = lax.axis_size("chan") // 2 + 1
    place = lax.axis_index("lag").astype(jnp.int32).reshape(1)
    piece = local_rows(plan, raw_samples, decimation_taps)
    tabs = tables(plan, decimation_taps, bandpass_taps)
    count = 32
    out, left = block_call(plan, count, pairs, 0, place, gather_pieces(piece), tabs)
    for distance in range(1, pairs):
        pieces = gather_pieces(from_ahead(piece, distance))
        out = block_call(plan, count, pairs, distance, place, pieces, tabs, left, out)
    return out


def solution(mesh):
    placed = (P(None, "chan", "lag"), P(), P())
    return jax.shard_map(
        shards, mesh=mesh, in_specs=placed, out_specs=P("chan", None, "lag", None), check_vma=False
    )
```

profile of v0, /device:TPU:0, one launch (start us, length us, event | category | flops | bytes accessed | tf_op | source)
XLA Modules:
  0.0 81.1 jit_solution(14582775347586192398)
XLA Ops:
  0.0 1.8 %copy.6.raw_ref = bf16[8,128,100]{2,1,0:T(8,128)(2,1)} copy(bf16[8,128,100]{1,0,2:T(8,128)(2,1)} %param.3) | data formatting | bytes 409600 | tf_op args[0]
  1.8 1.9 %shard_map.37.refs_0_ = bf16[72,1024]{1,0:T(8,128)(2,1)} custom-call(f32[16]{0:T(128)} %dec_ref.1, bf16[8,128,100]{2,1,0:T(8,128)(2,1)} %copy.6.raw_ref), custom_call_target="tpu_custom_call" | custom-call | tf_op jit(solution)/shard_map/pallas_call | solution.py:70
  3.8 2.9 %collective-permute-start.9 = (bf16[72,1024]{1,0:T(8,128)(2,1)}, bf16[72,1024]{1,0:T(8,128)(2,1)S(1)}, u32[]{:S(2)}, u32[]{:S(2)}) collective-permute-start(bf16[72,1024]{1,0:T(8,128)(2,1)} %shard_map.37.refs_0_), channel_id=1, source_target_pairs={{2,0},{3,1},{0,2},{1,3},{6,4},{7,5},{4,6},{5,7},{10,8},{11,9},{8,1... | collective-permute-start | bytes 442376 | tf_op jit(solution)/shard_map/ppermute | solution.py:293
  6.7 1.5 %collective-permute-start.11 = (bf16[72,1024]{1,0:T(8,128)(2,1)}, bf16[72,1024]{1,0:T(8,128)(2,1)S(1)}, u32[]{:S(2)}, u32[]{:S(2)}) collective-permute-start(bf16[72,1024]{1,0:T(8,128)(2,1)} %shard_map.37.refs_0_), channel_id=1, source_target_pairs={{4,0},{5,1},{6,2},{7,3},{0,4},{1,5},{2,6},{3,7},{12,8},{13,9},{14,... | collective-permute-start | bytes 442376 | tf_op jit(solution)/shard_map/ppermute | solution.py:293
  8.2 0.0 collective-permute-start.13
  8.2 4.1 %collective-permute-start.15 = (bf16[72,1024]{1,0:T(8,128)(2,1)}, bf16[72,1024]{1,0:T(8,128)(2,1)S(1)}, u32[]{:S(2)}, u32[]{:S(2)}) collective-permute-start(bf16[72,1024]{1,0:T(8,128)(2,1)} %shard_map.37.refs_0_), channel_id=1, source_target_pairs={{8,0},{16,8},{24,16},{0,24},{9,1},{17,9},{25,17},{1,25},{10,2},{18... | collective-permute-start | bytes 442376 | tf_op jit(solution)/shard_map/ppermute | solution.py:298
  12.3 2.0 %collective-permute-start = (bf16[72,1024]{1,0:T(8,128)(2,1)}, bf16[72,1024]{1,0:T(8,128)(2,1)S(1)}, u32[]{:S(2)}, u32[]{:S(2)}) collective-permute-start(bf16[72,1024]{1,0:T(8,128)(2,1)} %shard_map.37.refs_0_), channel_id=1, source_target_pairs={{16,0},{24,8},{0,16},{8,24},{17,1},{25,9},{1,17},{9,25},{18,2},{26... | collective-permute-start | bytes 442376 | tf_op jit(solution)/shard_map/ppermute | solution.py:298
  14.3 1.1 %collective-permute-done.11.refs_4_ = bf16[72,1024]{1,0:T(8,128)(2,1)S(1)} collective-permute-done((bf16[72,1024]{1,0:T(8,128)(2,1)}, bf16[72,1024]{1,0:T(8,128)(2,1)S(1)}, u32[]{:S(2)}, u32[]{:S(2)}) %collective-permute-start.11) | collective-permute-done | bytes 147488 | tf_op jit(solution)/shard_map/ppermute | solution.py:293
  15.4 0.5 collective-permute-start.12
  15.9 0.1 collective-permute-start.14
  16.0 0.9 %collective-permute-done.15.refs_0_ = bf16[72,1024]{1,0:T(8,128)(2,1)S(1)} collective-permute-done((bf16[72,1024]{1,0:T(8,128)(2,1)}, bf16[72,1024]{1,0:T(8,128)(2,1)S(1)}, u32[]{:S(2)}, u32[]{:S(2)}) %collective-permute-start.15) | collective-permute-done | bytes 147488 | tf_op jit(solution)/shard_map/ppermute | solution.py:298
  16.8 1.5 %collective-permute-start.17 = (bf16[72,1024]{1,0:T(8,128)(2,1)S(1)}, bf16[72,1024]{1,0:T(8,128)(2,1)S(1)}, u32[]{:S(2)}, u32[]{:S(2)}) collective-permute-start(bf16[72,1024]{1,0:T(8,128)(2,1)S(1)} %collective-permute-done.15.refs_0_), channel_id=1, source_target_pairs={{2,0},{3,1},{0,2},{1,3},{6,4},{7,5},{4,6},{5,7},{10,8},{11,9},{8,1... | collective-permute-start | bytes 442376 | tf_op jit(solution)/shard_map/ppermute | solution.py:293
  18.3 4.2 %collective-permute-done.refs_0_ = bf16[72,1024]{1,0:T(8,128)(2,1)S(1)} collective-permute-done((bf16[72,1024]{1,0:T(8,128)(2,1)}, bf16[72,1024]{1,0:T(8,128)(2,1)S(1)}, u32[]{:S(2)}, u32[]{:S(2)}) %collective-permute-start) | collective-permute-done | bytes 147488 | tf_op jit(solution)/shard_map/ppermute | solution.py:298
  22.5 1.5 %collective-permute-start.19 = (bf16[72,1024]{1,0:T(8,128)(2,1)S(1)}, bf16[72,1024]{1,0:T(8,128)(2,1)S(1)}, u32[]{:S(2)}, u32[]{:S(2)}) collective-permute-start(bf16[72,1024]{1,0:T(8,128)(2,1)S(1)} %collective-permute-done.15.refs_0_), channel_id=1, source_target_pairs={{4,0},{5,1},{6,2},{7,3},{0,4},{1,5},{2,6},{3,7},{12,8},{13,9},{14,... | collective-permute-start | bytes 442376 | tf_op jit(solution)/shard_map/ppermute | solution.py:293
  24.1 1.4 %collective-permute-start.21 = (bf16[72,1024]{1,0:T(8,128)(2,1)S(1)}, bf16[72,1024]{1,0:T(8,128)(2,1)S(1)}, u32[]{:S(2)}, u32[]{:S(2)}) collective-permute-start(bf16[72,1024]{1,0:T(8,128)(2,1)S(1)} %collective-permute-done.15.refs_0_), channel_id=1, source_target_pairs={{6,0},{7,1},{4,2},{5,3},{2,4},{3,5},{0,6},{1,7},{14,8},{15,9},{12,... | collective-permute-start | bytes 442376 | tf_op jit(solution)/shard_map/ppermute | solution.py:293
  25.5 0.6 collective-permute-start.2
  26.1 0.7 copy-done.1
  26.8 0.7 copy-done.2
  27.4 1.4 %shard_map.38 = (bf16[200,704]{1,0:T(8,128)(2,1)S(1)}, bf16[200,704]{1,0:T(8,128)(2,1)S(1)}, bf16[64,640]{1,0:T(8,128)(2,1)S(1)}) custom-call(f32[16]{0:T(128)S(1)} %copy-done.1, f32[65]{0:T(128)S(1)} %copy-done.2), custom_call_target="tpu_custom_call" | custom-call | flops 500000000 | bytes 2000000 | tf_op jit(solution)/shard_map/pallas_call | solution.py:116
  28.8 1.6 %collective-permute-start.4 = (bf16[72,1024]{1,0:T(8,128)(2,1)S(1)}, bf16[72,1024]{1,0:T(8,128)(2,1)S(1)}, u32[]{:S(2)}, u32[]{:S(2)}) collective-permute-start(bf16[72,1024]{1,0:T(8,128)(2,1)S(1)} %collective-permute-done.refs_0_), channel_id=1, source_target_pairs={{4,0},{5,1},{6,2},{7,3},{0,4},{1,5},{2,6},{3,7},{12,8},{13,9},{14,... | collective-permute-start | bytes 442376 | tf_op jit(solution)/shard_map/ppermute | solution.py:293
  30.4 0.5 collective-permute-done.19.refs_4_
  31.0 2.5 %collective-permute-start.6 = (bf16[72,1024]{1,0:T(8,128)(2,1)S(1)}, bf16[72,1024]{1,0:T(8,128)(2,1)S(1)}, u32[]{:S(2)}, u32[]{:S(2)}) collective-permute-start(bf16[72,1024]{1,0:T(8,128)(2,1)S(1)} %collective-permute-done.refs_0_), channel_id=1, source_target_pairs={{6,0},{7,1},{4,2},{5,3},{2,4},{3,5},{0,6},{1,7},{14,8},{15,9},{12,... | collective-permute-start | bytes 442376 | tf_op jit(solution)/shard_map/ppermute | solution.py:293
  33.4 0.5 collective-permute-start.20
  33.9 0.1 collective-permute-start.22
  34.0 0.9 %copy-done = bf16[72,1024]{1,0:T(8,128)(2,1)S(1)} copy-done((bf16[72,1024]{1,0:T(8,128)(2,1)S(1)}, bf16[72,1024]{1,0:T(8,128)(2,1)}, u32[]{:S(2)}) %copy-start) | copy-done | bytes 147480
  34.9 19.6 %own_block.1 = (f32[128,3,64,128]{3,2,1,0:T(8,128)}, bf16[3,1024,1664]{2,1,0:T(8,128)(2,1)}) custom-call(s32[1]{0:T(128)} %bitcast.place_ref, bf16[72,1024]{1,0:T(8,128)(2,1)S(1)} %copy-done, bf16[72,1024]{1,0:T(8,128)(2,1)S(1)} %collective-permute-done.8.refs_1_, bf16[72,1024]{1,0:T(8,128)(2,1)S(1)} %collective-permute-done.9.refs_2_, ...), custom_call_target="tpu_custom_call" | custom-call | flops 5234491392 | bytes 16777216 | tf_op jit(solution)/shard_map/own_block/pallas_call | solution.py:265
  54.6 0.4 collective-permute-start.1
  55.0 0.1 collective-permute-start.3
  55.1 0.4 collective-permute-start.5
  55.5 0.1 collective-permute-start.7
  55.6 12.7 %other_block.2.refs_12_ = f32[128,3,64,128]{3,2,1,0:T(8,128)} custom-call(s32[1]{0:T(128)} %bitcast.place_ref, bf16[72,1024]{1,0:T(8,128)(2,1)S(1)} %collective-permute-done.15.refs_0_, bf16[72,1024]{1,0:T(8,128)(2,1)S(1)} %collective-permute-done.16.refs_1_, bf16[72,1024]{1,0:T(8,128)(2,1)S(1)} %collective-permute-done.17.refs_2_, ...), custom_call_target="tpu_custom_call", output_to_operand_aliasing={{}: (13, {})} | custom-call | flops 5234491392 | bytes 16777216 | tf_op jit(solution)/shard_map/other_block/pallas_call | solution.py:277
  68.4 12.8 %other_block.3 = f32[128,3,64,128]{3,2,1,0:T(8,128)} custom-call(s32[1]{0:T(128)} %bitcast.place_ref, bf16[72,1024]{1,0:T(8,128)(2,1)S(1)} %collective-permute-done.refs_0_, bf16[72,1024]{1,0:T(8,128)(2,1)S(1)} %collective-permute-done.1.refs_1_, bf16[72,1024]{1,0:T(8,128)(2,1)S(1)} %collective-permute-done.2.refs_2_, ...), custom_call_target="tpu_custom_call", output_to_operand_aliasing={{}: (13, {})} | custom-call | flops 5234491392 | bytes 16777216 | tf_op jit(solution)/shard_map/other_block/pallas_call | solution.py:277
  (26 shorter events, 0.1 us)
Async XLA Ops:
  3.8 8.5 %collective-permute-start.9 = (bf16[72,1024]{1,0:T(8,128)(2,1)}, bf16[72,1024]{1,0:T(8,128)(2,1)S(1)}, u32[]{:S(2)}, u32[]{:S(2)}) collective-permute-start(bf16[72,1024]{1,0:T(8,128)(2,1)} %shard_map.37.refs_0_), channel_id=1, source_target_pairs={{2,0},{3,1},{0,2},{1,3},{6,4},{7,5},{4,6},{5,7},{10,8},{11,9},{8,1... | collective-permute-start | bytes 442376 | tf_op jit(solution)/shard_map/ppermute | solution.py:293
  6.7 8.7 %collective-permute-start.11 = (bf16[72,1024]{1,0:T(8,128)(2,1)}, bf16[72,1024]{1,0:T(8,128)(2,1)S(1)}, u32[]{:S(2)}, u32[]{:S(2)}) collective-permute-start(bf16[72,1024]{1,0:T(8,128)(2,1)} %shard_map.37.refs_0_), channel_id=1, source_target_pairs={{4,0},{5,1},{6,2},{7,3},{0,4},{1,5},{2,6},{3,7},{12,8},{13,9},{14,... | collective-permute-start | bytes 442376 | tf_op jit(solution)/shard_map/ppermute | solution.py:293
  8.2 7.2 %collective-permute-start.13 = (bf16[72,1024]{1,0:T(8,128)(2,1)}, bf16[72,1024]{1,0:T(8,128)(2,1)S(1)}, u32[]{:S(2)}, u32[]{:S(2)}) collective-permute-start(bf16[72,1024]{1,0:T(8,128)(2,1)} %shard_map.37.refs_0_), channel_id=1, source_target_pairs={{6,0},{7,1},{4,2},{5,3},{2,4},{3,5},{0,6},{1,7},{14,8},{15,9},{12,... | collective-permute-start | bytes 442376 | tf_op jit(solution)/shard_map/ppermute | solution.py:293
  8.2 7.7 %collective-permute-start.8 = (bf16[72,1024]{1,0:T(8,128)(2,1)}, bf16[72,1024]{1,0:T(8,128)(2,1)S(1)}, u32[]{:S(2)}, u32[]{:S(2)}) collective-permute-start(bf16[72,1024]{1,0:T(8,128)(2,1)} %shard_map.37.refs_0_), channel_id=1, source_target_pairs={{1,0},{0,1},{3,2},{2,3},{5,4},{4,5},{7,6},{6,7},{9,8},{8,9},{11,10... | collective-permute-start | bytes 442376 | tf_op jit(solution)/shard_map/ppermute | solution.py:293
  8.2 8.6 %collective-permute-start.15 = (bf16[72,1024]{1,0:T(8,128)(2,1)}, bf16[72,1024]{1,0:T(8,128)(2,1)S(1)}, u32[]{:S(2)}, u32[]{:S(2)}) collective-permute-start(bf16[72,1024]{1,0:T(8,128)(2,1)} %shard_map.37.refs_0_), channel_id=1, source_target_pairs={{8,0},{16,8},{24,16},{0,24},{9,1},{17,9},{25,17},{1,25},{10,2},{18... | collective-permute-start | bytes 442376 | tf_op jit(solution)/shard_map/ppermute | solution.py:298
  12.3 10.3 %collective-permute-start = (bf16[72,1024]{1,0:T(8,128)(2,1)}, bf16[72,1024]{1,0:T(8,128)(2,1)S(1)}, u32[]{:S(2)}, u32[]{:S(2)}) collective-permute-start(bf16[72,1024]{1,0:T(8,128)(2,1)} %shard_map.37.refs_0_), channel_id=1, source_target_pairs={{16,0},{24,8},{0,16},{8,24},{17,1},{25,9},{1,17},{9,25},{18,2},{26... | collective-permute-start | bytes 442376 | tf_op jit(solution)/shard_map/ppermute | solution.py:298
  15.4 8.7 %collective-permute-start.10 = (bf16[72,1024]{1,0:T(8,128)(2,1)S(1)}, bf16[72,1024]{1,0:T(8,128)(2,1)S(1)}, u32[]{:S(2)}, u32[]{:S(2)}) collective-permute-start(bf16[72,1024]{1,0:T(8,128)(2,1)S(1)} %collective-permute-done.9.refs_2_), channel_id=1, source_target_pairs={{1,0},{0,1},{3,2},{2,3},{5,4},{4,5},{7,6},{6,7},{9,8},{8,9},{11,10... | collective-permute-start | bytes 442376 | tf_op jit(solution)/shard_map/ppermute | solution.py:293
  15.4 10.1 %collective-permute-start.12 = (bf16[72,1024]{1,0:T(8,128)(2,1)S(1)}, bf16[72,1024]{1,0:T(8,128)(2,1)S(1)}, u32[]{:S(2)}, u32[]{:S(2)}) collective-permute-start(bf16[72,1024]{1,0:T(8,128)(2,1)S(1)} %collective-permute-done.11.refs_4_), channel_id=1, source_target_pairs={{1,0},{0,1},{3,2},{2,3},{5,4},{4,5},{7,6},{6,7},{9,8},{8,9},{11,10... | collective-permute-start | bytes 442376 | tf_op jit(solution)/shard_map/ppermute | solution.py:293
  15.9 9.6 %collective-permute-start.14 = (bf16[72,1024]{1,0:T(8,128)(2,1)S(1)}, bf16[72,1024]{1,0:T(8,128)(2,1)S(1)}, u32[]{:S(2)}, u32[]{:S(2)}) collective-permute-start(bf16[72,1024]{1,0:T(8,128)(2,1)S(1)} %collective-permute-done.13.refs_6_), channel_id=1, source_target_pairs={{1,0},{0,1},{3,2},{2,3},{5,4},{4,5},{7,6},{6,7},{9,8},{8,9},{11,10... | collective-permute-start | bytes 442376 | tf_op jit(solution)/shard_map/ppermute | solution.py:293
  16.8 12.0 %collective-permute-start.17 = (bf16[72,1024]{1,0:T(8,128)(2,1)S(1)}, bf16[72,1024]{1,0:T(8,128)(2,1)S(1)}, u32[]{:S(2)}, u32[]{:S(2)}) collective-permute-start(bf16[72,1024]{1,0:T(8,128)(2,1)S(1)} %collective-permute-done.15.refs_0_), channel_id=1, source_target_pairs={{2,0},{3,1},{0,2},{1,3},{6,4},{7,5},{4,6},{5,7},{10,8},{11,9},{8,1... | collective-permute-start | bytes 442376 | tf_op jit(solution)/shard_map/ppermute | solution.py:293
  22.5 8.4 %collective-permute-start.19 = (bf16[72,1024]{1,0:T(8,128)(2,1)S(1)}, bf16[72,1024]{1,0:T(8,128)(2,1)S(1)}, u32[]{:S(2)}, u32[]{:S(2)}) collective-permute-start(bf16[72,1024]{1,0:T(8,128)(2,1)S(1)} %collective-permute-done.15.refs_0_), channel_id=1, source_target_pairs={{4,0},{5,1},{6,2},{7,3},{0,4},{1,5},{2,6},{3,7},{12,8},{13,9},{14,... | collective-permute-start | bytes 442376 | tf_op jit(solution)/shard_map/ppermute | solution.py:293
  24.1 9.3 %collective-permute-start.21 = (bf16[72,1024]{1,0:T(8,128)(2,1)S(1)}, bf16[72,1024]{1,0:T(8,128)(2,1)S(1)}, u32[]{:S(2)}, u32[]{:S(2)}) collective-permute-start(bf16[72,1024]{1,0:T(8,128)(2,1)S(1)} %collective-permute-done.15.refs_0_), channel_id=1, source_target_pairs={{6,0},{7,1},{4,2},{5,3},{2,4},{3,5},{0,6},{1,7},{14,8},{15,9},{12,... | collective-permute-start | bytes 442376 | tf_op jit(solution)/shard_map/ppermute | solution.py:293
  25.5 7.9 %collective-permute-start.16 = (bf16[72,1024]{1,0:T(8,128)(2,1)S(1)}, bf16[72,1024]{1,0:T(8,128)(2,1)S(1)}, u32[]{:S(2)}, u32[]{:S(2)}) collective-permute-start(bf16[72,1024]{1,0:T(8,128)(2,1)S(1)} %collective-permute-done.15.refs_0_), channel_id=1, source_target_pairs={{1,0},{0,1},{3,2},{2,3},{5,4},{4,5},{7,6},{6,7},{9,8},{8,9},{11,10... | collective-permute-start | bytes 442376 | tf_op jit(solution)/shard_map/ppermute | solution.py:293
  25.5 8.4 %collective-permute-start.2 = (bf16[72,1024]{1,0:T(8,128)(2,1)S(1)}, bf16[72,1024]{1,0:T(8,128)(2,1)S(1)}, u32[]{:S(2)}, u32[]{:S(2)}) collective-permute-start(bf16[72,1024]{1,0:T(8,128)(2,1)S(1)} %collective-permute-done.refs_0_), channel_id=1, source_target_pairs={{2,0},{3,1},{0,2},{1,3},{6,4},{7,5},{4,6},{5,7},{10,8},{11,9},{8,1... | collective-permute-start | bytes 442376 | tf_op jit(solution)/shard_map/ppermute | solution.py:293
  26.1 0.7 copy-start.1
  26.8 0.7 copy-start.2
  28.8 25.7 %collective-permute-start.4 = (bf16[72,1024]{1,0:T(8,128)(2,1)S(1)}, bf16[72,1024]{1,0:T(8,128)(2,1)S(1)}, u32[]{:S(2)}, u32[]{:S(2)}) collective-permute-start(bf16[72,1024]{1,0:T(8,128)(2,1)S(1)} %collective-permute-done.refs_0_), channel_id=1, source_target_pairs={{4,0},{5,1},{6,2},{7,3},{0,4},{1,5},{2,6},{3,7},{12,8},{13,9},{14,... | collective-permute-start | bytes 442376 | tf_op jit(solution)/shard_map/ppermute | solution.py:293
  31.0 24.0 %collective-permute-start.6 = (bf16[72,1024]{1,0:T(8,128)(2,1)S(1)}, bf16[72,1024]{1,0:T(8,128)(2,1)S(1)}, u32[]{:S(2)}, u32[]{:S(2)}) collective-permute-start(bf16[72,1024]{1,0:T(8,128)(2,1)S(1)} %collective-permute-done.refs_0_), channel_id=1, source_target_pairs={{6,0},{7,1},{4,2},{5,3},{2,4},{3,5},{0,6},{1,7},{14,8},{15,9},{12,... | collective-permute-start | bytes 442376 | tf_op jit(solution)/shard_map/ppermute | solution.py:293
  33.4 21.7 %collective-permute-start.18 = (bf16[72,1024]{1,0:T(8,128)(2,1)S(1)}, bf16[72,1024]{1,0:T(8,128)(2,1)S(1)}, u32[]{:S(2)}, u32[]{:S(2)}) collective-permute-start(bf16[72,1024]{1,0:T(8,128)(2,1)S(1)} %collective-permute-done.17.refs_2_), channel_id=1, source_target_pairs={{1,0},{0,1},{3,2},{2,3},{5,4},{4,5},{7,6},{6,7},{9,8},{8,9},{11,10... | collective-permute-start | bytes 442376 | tf_op jit(solution)/shard_map/ppermute | solution.py:293
  33.4 22.1 %collective-permute-start.20 = (bf16[72,1024]{1,0:T(8,128)(2,1)S(1)}, bf16[72,1024]{1,0:T(8,128)(2,1)S(1)}, u32[]{:S(2)}, u32[]{:S(2)}) collective-permute-start(bf16[72,1024]{1,0:T(8,128)(2,1)S(1)} %collective-permute-done.19.refs_4_), channel_id=1, source_target_pairs={{1,0},{0,1},{3,2},{2,3},{5,4},{4,5},{7,6},{6,7},{9,8},{8,9},{11,10... | collective-permute-start | bytes 442376 | tf_op jit(solution)/shard_map/ppermute | solution.py:293
  33.9 21.7 %collective-permute-start.22 = (bf16[72,1024]{1,0:T(8,128)(2,1)S(1)}, bf16[72,1024]{1,0:T(8,128)(2,1)S(1)}, u32[]{:S(2)}, u32[]{:S(2)}) collective-permute-start(bf16[72,1024]{1,0:T(8,128)(2,1)S(1)} %collective-permute-done.21.refs_6_), channel_id=1, source_target_pairs={{1,0},{0,1},{3,2},{2,3},{5,4},{4,5},{7,6},{6,7},{9,8},{8,9},{11,10... | collective-permute-start | bytes 442376 | tf_op jit(solution)/shard_map/ppermute | solution.py:293
  34.0 0.9 %copy-start = (bf16[72,1024]{1,0:T(8,128)(2,1)S(1)}, bf16[72,1024]{1,0:T(8,128)(2,1)}, u32[]{:S(2)}) copy-start(bf16[72,1024]{1,0:T(8,128)(2,1)} %shard_map.37.refs_0_) | copy-start | bytes 442372
  54.6 13.8 %collective-permute-start.1 = (bf16[72,1024]{1,0:T(8,128)(2,1)S(1)}, bf16[72,1024]{1,0:T(8,128)(2,1)S(1)}, u32[]{:S(2)}, u32[]{:S(2)}) collective-permute-start(bf16[72,1024]{1,0:T(8,128)(2,1)S(1)} %collective-permute-done.refs_0_), channel_id=1, source_target_pairs={{1,0},{0,1},{3,2},{2,3},{5,4},{4,5},{7,6},{6,7},{9,8},{8,9},{11,10... | collective-permute-start | bytes 442376 | tf_op jit(solution)/shard_map/ppermute | solution.py:293
  55.0 13.4 %collective-permute-start.3 = (bf16[72,1024]{1,0:T(8,128)(2,1)S(1)}, bf16[72,1024]{1,0:T(8,128)(2,1)S(1)}, u32[]{:S(2)}, u32[]{:S(2)}) collective-permute-start(bf16[72,1024]{1,0:T(8,128)(2,1)S(1)} %collective-permute-done.2.refs_2_), channel_id=1, source_target_pairs={{1,0},{0,1},{3,2},{2,3},{5,4},{4,5},{7,6},{6,7},{9,8},{8,9},{11,10... | collective-permute-start | bytes 442376 | tf_op jit(solution)/shard_map/ppermute | solution.py:293
  55.1 13.3 %collective-permute-start.5 = (bf16[72,1024]{1,0:T(8,128)(2,1)S(1)}, bf16[72,1024]{1,0:T(8,128)(2,1)S(1)}, u32[]{:S(2)}, u32[]{:S(2)}) collective-permute-start(bf16[72,1024]{1,0:T(8,128)(2,1)S(1)} %collective-permute-done.4.refs_4_), channel_id=1, source_target_pairs={{1,0},{0,1},{3,2},{2,3},{5,4},{4,5},{7,6},{6,7},{9,8},{8,9},{11,10... | collective-permute-start | bytes 442376 | tf_op jit(solution)/shard_map/ppermute | solution.py:293
  55.5 12.8 %collective-permute-start.7 = (bf16[72,1024]{1,0:T(8,128)(2,1)S(1)}, bf16[72,1024]{1,0:T(8,128)(2,1)S(1)}, u32[]{:S(2)}, u32[]{:S(2)}) collective-permute-start(bf16[72,1024]{1,0:T(8,128)(2,1)S(1)} %collective-permute-done.6.refs_6_), channel_id=1, source_target_pairs={{1,0},{0,1},{3,2},{2,3},{5,4},{4,5},{7,6},{6,7},{9,8},{8,9},{11,10... | collective-permute-start | bytes 442376 | tf_op jit(solution)/shard_map/ppermute | solution.py:293
where the time goes:
time: 81.6 us; the launch traced here: 81.1 us
  Pallas kernels  48.5 us (59%)
  starting transfers between devices  21.8 us (27%)
  waiting for transfers between devices  6.73 us (8%)
  local copies, waits for them, and re-layouts  4.04 us (5%)
    pallas_call x2, Pallas kernels, block_call(): pl.pallas_call(functools.partial(other_kernel, plan, count), grid=(plan.c...  25.5 us
    pallas_call x1, Pallas kernels, block_call(): pl.pallas_call(functools.partial(own_kernel, plan, count), grid=(plan.cha...  19.6 us
    ppermute x21, starting transfers between devices, swap(): return lax.ppermute(piece, 'lag', [(i ^ mask, i) for i in range(count)])  15.7 us
    ppermute x2, starting transfers between devices, from_ahead(): lax.ppermute(piece, 'chan', [((i + distance) % count, i) for i in range(c...  6.09 us
    ppermute x2, waiting for transfers between devices, from_ahead(): lax.ppermute(piece, 'chan', [((i + distance) % count, i) for i in range(c...  5.09 us
    unnamed x7, local copies, waits for them, and re-layouts  4.04 us
    pallas_call x1, Pallas kernels, local_rows(): pl.pallas_call(functools.partial(local_kernel, plan), out_shape=jax.Shape...  1.93 us
    ppermute x21, waiting for transfers between devices, swap(): return lax.ppermute(piece, 'lag', [(i ^ mask, i) for i in range(count)])  1.64 us
  transfers between devices with their start and end apart: 23, of which 4 were waited for; matrix products, arithmetic and copies ran while one was open for 0% of the time, Pallas kernels for 42%

commit v1 on v0

--- a/solution.py
+++ b/solution.py
@@ -13,6 +13,8 @@
 LANES = 128
 F32 = jnp.float32
 BF16 = jnp.bfloat16
+SMEM = pl.BlockSpec(memory_space=pltpu.SMEM)
+VMEM = pl.BlockSpec(memory_space=pltpu.VMEM)
 
 
 def ceil_to(value, unit):
@@ -44,10 +46,10 @@
 
 
 def rounded_tap(taps, index):
-    return jnp.full((SUB, LANES), taps[index], F32).astype(BF16).astype(F32)[0:1, 0:1]
-
-
-def local_kernel(plan, taps_ref, raw_ref, out_ref):
+    return taps[0:1, index : index + 1].astype(BF16).astype(F32)
+
+
+def local_kernel(plan, taps_ref, raw_ref, out_ref, spread):
     row = lax.broadcasted_iota(jnp.int32, (plan.rows, plan.raw), 0)
     time = lax.broadcasted_iota(jnp.int32, (plan.rows, plan.raw), 1)
     tap = 2 * (row + plan.head) - time
@@ -60,9 +62,11 @@
     is_first = (row >= plan.whole + plan.edge) & (row < plan.whole + 2 * plan.edge)
     picked = jnp.where(is_last & last | is_first & first, 1.0, 0.0)
     table = jnp.where(row < plan.whole, table, picked).astype(BF16)
+    spread[...] = raw_ref[...].astype(F32).reshape(plan.raw * plan.windows, plan.channels)
     for w in range(plan.windows):
-        out_ref[:, w * plan.channels : (w + 1) * plan.channels] = lax.dot_general(
-            table, raw_ref[w], (((1,), (1,)), ((), ())), preferred_element_type=F32
+        series = spread[pl.ds(w, plan.raw, stride=plan.windows), :].astype(BF16)
+        out_ref[:, w * plan.channels : (w + 1) * plan.channels] = jnp.dot(
+            table, series, preferred_element_type=F32
         ).astype(BF16)
 
 
@@ -70,9 +74,11 @@
     return pl.pallas_call(
         functools.partial(local_kernel, plan),
         out_shape=jax.ShapeDtypeStruct((plan.rows, plan.wide), BF16),
-        in_specs=[pl.BlockSpec(memory_space=pltpu.SMEM), pl.BlockSpec(memory_space=pltpu.VMEM)],
-        out_specs=pl.BlockSpec(memory_space=pltpu.VMEM),
-    )(taps, raw)
+        in_specs=[VMEM, VMEM],
+        out_specs=VMEM,
+        scratch_shapes=[pltpu.VMEM((plan.raw * plan.windows, plan.channels), F32)],
+        name="local_rows",
+    )(taps, jnp.transpose(raw, (2, 0, 1)))
 
 
 def table_kernel(plan, dec_ref, bp_ref, even_ref, odd_ref, edge_ref):
@@ -112,7 +118,6 @@
 
 
 def tables(plan, dec_taps, bp_taps):
-    smem, vmem = pl.BlockSpec(memory_space=pltpu.SMEM), pl.BlockSpec(memory_space=pltpu.VMEM)
     return pl.pallas_call(
         functools.partial(table_kernel, plan),
         out_shape=(
@@ -120,22 +125,28 @@
             jax.ShapeDtypeStruct((plan.half, plan.joined), BF16),
             jax.ShapeDtypeStruct((plan.joined - plan.held, plan.held), BF16),
         ),
-        in_specs=[smem, smem],
-        out_specs=(vmem, vmem, vmem),
-        compiler_params=pltpu.CompilerParams(vmem_limit_bytes=32 * 2**20),
+        in_specs=[VMEM, VMEM],
+        out_specs=(VMEM, VMEM, VMEM),
+        compiler_params=pltpu.CompilerParams(vmem_limit_bytes=20 * 2**20),
         cost_estimate=pl.CostEstimate(flops=500_000_000, bytes_accessed=2_000_000, transcendentals=0),
+        name="tables",
     )(dec_taps, bp_taps)
 
 
 def make_series(plan, place_ref, pieces, tables_refs, held, even, odd, ahead, right):
-    even_ref, odd_ref, edge_ref = tables_refs
     place = place_ref[0]
     if plan.slot > plan.rows:
         for p in range(plan.lag_total):
             held[(p + 1) * plan.slot - 16 : (p + 1) * plan.slot, :] = jnp.zeros((16, plan.wide), BF16)
-    for p, piece in enumerate(pieces):
+    for p in range(plan.lag_total):
         at = pl.multiple_of(lax.bitwise_xor(place, p) * plan.slot, 16)
-        held[pl.ds(at, plan.rows), :] = piece[...]
+        held[pl.ds(at, plan.rows), :] = pieces[p][...]
+    filter_block(plan, tables_refs, held, even, odd, ahead)
+    lay_right(plan, place, even, odd, ahead, right)
+
+
+def filter_block(plan, tables_refs, held, even, odd, ahead):
+    even_ref, odd_ref, edge_ref = tables_refs
     held[plan.held : plan.joined, :] = jnp.dot(
         edge_ref[...], held[0 : plan.held, :], preferred_element_type=F32
     ).astype(BF16)
@@ -157,6 +168,9 @@
         even[plan.pad : plan.pad + plan.half, cols] = a
         odd[plan.pad : plan.pad + plan.half, cols] = b
         ahead[plan.pad - 1 : plan.pad - 1 + plan.half, cols] = a
+
+
+def lay_right(plan, place, even, odd, ahead, right):
     base = place * (plan.lags // 2)
     for w in range(plan.windows):
         cols = slice(w * plan.channels, (w + 1) * plan.channels)
@@ -170,33 +184,23 @@
             right[2, rows, to] = (c - b).astype(BF16)
 
 
-def make_left(plan, even, odd, stack, turned):
-    for k, ref in enumerate((even, odd)):
+def make_left(plan, even, odd, stacks, mixes, left):
+    for ref, stack in zip((even, odd), stacks, strict=True):
+        stack[0:SUB, :] = jnp.zeros((SUB, plan.channels), F32)
         for w in range(plan.windows):
-            stack[w * plan.depth : (w + 1) * plan.depth, :] = ref[
+            stack[SUB + w * plan.depth : SUB + (w + 1) * plan.depth, :] = ref[
                 plan.pad : plan.pad + plan.depth, w * plan.channels : (w + 1) * plan.channels
             ]
-        turned[k] = stack[...].T
-
-
-def shift_left(plan, count, turned, left):
-    start = pl.program_id(0) * count
-
-    def pair(k, carry):
-        parts = []
-        for n in range(2):
-            i = start + 2 * k + n
-            spread = [jnp.broadcast_to(turned[e, pl.ds(i, 1), :], (SUB, plan.deep)) for e in range(2)]
-            parts.append([pltpu.roll(x, 0, 1, stride=1, stride_axis=0) for x in spread])
-        a = jnp.concatenate([parts[0][0], parts[1][0]], axis=0)
-        b = jnp.concatenate([parts[0][1], parts[1][1]], axis=0)
-        rows = pl.ds(pl.multiple_of(k * 16, 16), 16)
-        left[0, rows, :] = (a + b).astype(BF16)
-        left[1, rows, :] = a.astype(BF16)
-        left[2, rows, :] = b.astype(BF16)
-        return carry
-
-    lax.fori_loop(0, count // 2, pair, 0)
+    for n, c in enumerate(range(0, plan.deep, LANES)):
+        mixed = mixes[n % 2]
+        for delay in range(SUB):
+            rows = slice(SUB - delay + c, SUB - delay + c + LANES)
+            for e, stack in enumerate(stacks):
+                mixed[e, pl.ds(delay, plan.channels, stride=SUB), :] = stack[rows, :].T
+        for r in range(0, plan.channels * SUB, LANES):
+            a, b = (mixed[e, r : r + LANES, :] for e in range(2))
+            for k, value in enumerate((a + b, a, b)):
+                left[k, r : r + LANES, c : c + LANES] = value.astype(BF16)
 
 
 def correlate(plan, count, left, right, out_ref):
@@ -204,8 +208,9 @@
     step = min(2 * LANES, plan.shifts * plan.channels)
     for c in range(0, plan.shifts * plan.channels, step):
         cols = slice(c, c + step)
+        rows = pl.ds(pl.multiple_of(pl.program_id(0) * count * SUB, count * SUB), count * SUB)
         both, even, odd = (
-            jnp.dot(left[k], right[k, :, cols], preferred_element_type=F32) for k in range(3)
+            jnp.dot(left[k, rows, :], right[k, :, cols], preferred_element_type=F32) for k in range(3)
         )
         for parity, value in ((0, even), (1, odd)):
             value = (both + value) * factor
@@ -217,18 +222,16 @@
                 )
 
 
-def own_kernel(plan, count, place_ref, *refs):
+def own_kernel(plan, place_ref, *refs):
     n = plan.lag_total
-    pieces, tabs, (out_ref, left_ref) = refs[:n], refs[n : n + 3], refs[n + 3 : n + 5]
-    held, even, odd, ahead, right, stack, turned = refs[n + 5 :]
-
-    @pl.when(pl.program_id(0) == 0)
-    def _():
-        make_series(plan, place_ref, pieces, tabs, held, even, odd, ahead, right)
-        make_left(plan, even, odd, stack, turned)
-
-    shift_left(plan, count, turned, left_ref)
-    correlate(plan, count, left_ref, right, out_ref)
+    pieces, tabs, (left_ref, right_ref) = refs[:n], refs[n : n + 3], refs[n + 3 : n + 5]
+    held, even, odd, ahead, *rest = refs[n + 5 :]
+    make_series(plan, place_ref, pieces, tabs, held, even, odd, ahead, right_ref)
+    make_left(plan, even, odd, rest[:2], rest[2:], left_ref)
+
+
+def first_kernel(plan, count, left_ref, right_ref, out_ref):
+    correlate(plan, count, left_ref, right_ref, out_ref)
 
 
 def other_kernel(plan, count, place_ref, *refs):
@@ -243,48 +246,65 @@
     correlate(plan, count, left_ref, right, out_ref)
 
 
-def block_call(plan, count, pairs, distance, place, pieces, tabs, left=None, out=None):
-    whole = lambda shape: pl.BlockSpec(shape, lambda i: (0,) * len(shape))
+def series_scratch(plan):
+    return [pltpu.VMEM((plan.joined, plan.wide), BF16)] + [pltpu.VMEM((plan.padded, plan.wide), F32)] * 3
+
+
+def prepare_own(plan, place, pieces, tabs):
+    return pl.pallas_call(
+        functools.partial(own_kernel, plan),
+        out_shape=(
+            jax.ShapeDtypeStruct((3, plan.channels * SUB, plan.deep), BF16),
+            jax.ShapeDtypeStruct((3, plan.deep, plan.shifts * plan.channels), BF16),
+        ),
+        in_specs=[SMEM] + [VMEM] * (plan.lag_total + 3),
+        out_specs=(VMEM, VMEM),
+        scratch_shapes=series_scratch(plan)
+        + [pltpu.VMEM((SUB + plan.deep, plan.channels), F32)] * 2
+        + [pltpu.VMEM((2, plan.channels * SUB, LANES), F32)] * 2,
+        compiler_params=pltpu.CompilerParams(vmem_limit_bytes=33 * 2**20),
+        cost_estimate=pl.CostEstimate(flops=5_000_000_000, bytes_accessed=2**20, transcendentals=0),
+        name="prepare_own",
+    )(place, *pieces, *tabs)
+
+
+def correlation_parts(plan, count, pairs, distance):
     out_shape = jax.ShapeDtypeStruct((plan.channels, pairs, plan.lags, plan.channels), F32)
-    left_shape = jax.ShapeDtypeStruct((3, plan.channels * SUB, plan.deep), BF16)
     out_spec = pl.BlockSpec((count, 1, plan.lags, plan.channels), lambda i: (i, distance, 0, 0))
-    left_spec = pl.BlockSpec((3, count * SUB, plan.deep), lambda i: (0, i, 0))
-    vmem = pl.BlockSpec(memory_space=pltpu.VMEM)
-    in_specs = [pl.BlockSpec(memory_space=pltpu.SMEM)] + [vmem] * (plan.lag_total + 3)
-    scratch = [
-        pltpu.VMEM((plan.joined, plan.wide), BF16),
-        pltpu.VMEM((plan.padded, plan.wide), F32),
-        pltpu.VMEM((plan.padded, plan.wide), F32),
-        pltpu.VMEM((plan.padded, plan.wide), F32),
-        pltpu.VMEM((3, plan.deep, plan.shifts * plan.channels), BF16),
-    ]
     flops = 2 * 3 * plan.channels * SUB * plan.deep * plan.shifts * plan.channels
-    cost = pl.CostEstimate(flops=flops, bytes_accessed=16 * 2**20, transcendentals=0)
-    params = pltpu.CompilerParams(vmem_limit_bytes=48 * 2**20)
-    if left is None:
-        return pl.pallas_call(
-            functools.partial(own_kernel, plan, count),
-            grid=(plan.channels // count,),
-            out_shape=(out_shape, left_shape),
-            in_specs=in_specs,
-            out_specs=(out_spec, left_spec),
-            scratch_shapes=scratch
-            + [pltpu.VMEM((plan.deep, plan.channels), F32), pltpu.VMEM((2, plan.channels, plan.deep), F32)],
-            compiler_params=params,
-            cost_estimate=cost,
-            name="own_block",
-        )(place, *pieces, *tabs)
+    cost = pl.CostEstimate(flops=flops, bytes_accessed=8 * 2**20, transcendentals=0)
+    return out_shape, out_spec, cost
+
+
+def own_correlation(plan, count, pairs, left, right):
+    out_shape, out_spec, cost = correlation_parts(plan, count, pairs, 0)
+    return pl.pallas_call(
+        functools.partial(first_kernel, plan, count),
+        grid=(plan.channels // count,),
+        out_shape=out_shape,
+        in_specs=[VMEM, VMEM],
+        out_specs=out_spec,
+        compiler_params=pltpu.CompilerParams(vmem_limit_bytes=24 * 2**20),
+        cost_estimate=cost,
+        name="own_correlation",
+    )(left, right)
+
+
+def other_correlation(plan, count, pairs, distance, place, pieces, tabs, left, out):
+    out_shape, out_spec, cost = correlation_parts(plan, count, pairs, distance)
+    in_specs = [SMEM] + [VMEM] * (plan.lag_total + 4) + [pl.BlockSpec(memory_space=pl.ANY)]
     return pl.pallas_call(
         functools.partial(other_kernel, plan, count),
         grid=(plan.channels // count,),
         out_shape=out_shape,
-        in_specs=in_specs + [left_spec, pl.BlockSpec(memory_space=pl.ANY)],
+        in_specs=in_specs,
         out_specs=out_spec,
-        scratch_shapes=scratch,
-        input_output_aliases={len(in_specs) + 1: 0},
-        compiler_params=params,
+        scratch_shapes=series_scratch(plan)
+        + [pltpu.VMEM((3, plan.deep, plan.shifts * plan.channels), BF16)],
+        input_output_aliases={len(in_specs) - 1: 0},
+        compiler_params=pltpu.CompilerParams(vmem_limit_bytes=30 * 2**20),
         cost_estimate=cost,
-        name="other_block",
+        name="other_correlation",
     )(place, *pieces, *tabs, left, out)
 
 
@@ -298,27 +318,36 @@
     return lax.ppermute(piece, "chan", [((i + distance) % count, i) for i in range(count)])
 
 
-def gather_pieces(piece):
-    count = lax.axis_size("lag")
-    mine = {0: piece}
-    for mask in range(2, count, 2):
-        mine[mask] = swap(piece, mask)
-    for mask in range(0, count, 2):
-        mine[mask + 1] = swap(mine[mask], 1)
-    return [mine[p] for p in range(count)]
+def same_core(piece):
+    return [swap(piece, mask) if mask else piece for mask in range(0, lax.axis_size("lag"), 2)]
+
+
+def both_cores(held):
+    return [x for piece in held for x in (piece, swap(piece, 1))]
 
 
 def shards(raw_samples, decimation_taps, bandpass_taps):
     plan = Plan(raw_samples.shape, lax.axis_size("lag"), decimation_taps.shape[0], bandpass_taps.shape[0])
     pairs = lax.axis_size("chan") // 2 + 1
     place = lax.axis_index("lag").astype(jnp.int32).reshape(1)
-    piece = local_rows(plan, raw_samples, decimation_taps)
-    tabs = tables(plan, decimation_taps, bandpass_taps)
+    dec_taps = decimation_taps.reshape(1, -1)
+    piece = local_rows(plan, raw_samples, dec_taps)
+    tabs = tables(plan, dec_taps, bandpass_taps.reshape(1, -1))
     count = 32
-    out, left = block_call(plan, count, pairs, 0, place, gather_pieces(piece), tabs)
+    held = same_core(piece)
+    tabs, held[1:] = lax.optimization_barrier((tabs, held[1:]))
+    left, right = prepare_own(plan, place, both_cores(held), tabs)
+    ahead = [from_ahead(x, 1) for x in held]
+    left, ahead = lax.optimization_barrier((left, ahead))
+    out = own_correlation(plan, count, pairs, left, right)
     for distance in range(1, pairs):
-        pieces = gather_pieces(from_ahead(piece, distance))
-        out = block_call(plan, count, pairs, distance, place, pieces, tabs, left, out)
+        pieces = both_cores(ahead)
+        if distance + 1 < pairs:
+            ahead = [from_ahead(x, 1) for x in ahead]
+        out_next = other_correlation(plan, count, pairs, distance, place, pieces, tabs, left, out)
+        if distance + 1 < pairs:
+            out_next, ahead = lax.optimization_barrier((out_next, ahead))
+        out = out_next
     return out
 
 

time: 81.6 us -> 68.6 us (0.84)
  Pallas kernels: 48.5 us -> 38.1 us
  starting transfers between devices: 21.8 us -> 16.7 us
  waiting for transfers between devices: 6.73 us -> 11.4 us
  local copies, waits for them, and re-layouts: 4.04 us -> 2.22 us
    pallas_call x3 -> x4, Pallas kernels: 45.2 us -> 35.3 us  [the longest x2 20.9 us: other_correlation(): pl.pallas_call(functools.partial(other_kernel, plan, count), grid=(plan.c...]
    ppermute x21 -> x15, starting transfers between devices: 15.7 us -> 6.74 us  [swap(): return lax.ppermute(piece, 'lag', [(i ^ mask, i) for i in range(count)])]
    ppermute x21 -> x15, waiting for transfers between devices: 1.64 us -> 6.04 us  [swap(): return lax.ppermute(piece, 'lag', [(i ^ mask, i) for i in range(count)])]
    ppermute x2 -> x8, starting transfers between devices: 6.09 us -> 9.91 us  [from_ahead(): lax.ppermute(piece, 'chan', [((i + distance) % count, i) for i in range(c...]
    unnamed x7 -> x6, local copies, waits for them, and re-layouts: 4.04 us -> 2.22 us
    ppermute x2 -> x8, waiting for transfers between devices: 5.09 us -> 5.37 us  [from_ahead(): lax.ppermute(piece, 'chan', [((i + distance) % count, i) for i in range(c...]
  transfers between devices with their start and end apart: 23 -> 23, of which waited for: 4 -> 9; matrix products, arithmetic and copies ran while one was open for 0% -> 0% of each run, Pallas kernels for 42% -> 38%
where the time goes in v1:
time: 68.6 us; the launch traced here: 68.5 us
  Pallas kernels  38.1 us (56%)
  starting transfers between devices  16.7 us (24%)
  waiting for transfers between devices  11.4 us (17%)
  local copies, waits for them, and re-layouts  2.22 us (3%)
    pallas_call x2, Pallas kernels, other_correlation(): pl.pallas_call(functools.partial(other_kernel, plan, count), grid=(plan.c...  20.9 us
    ppermute x8, starting transfers between devices, from_ahead(): lax.ppermute(piece, 'chan', [((i + distance) % count, i) for i in range(c...  9.91 us
    pallas_call x1, Pallas kernels, own_correlation(): pl.pallas_call(functools.partial(first_kernel, plan, count), grid=(plan.c...  7.37 us
    pallas_call x1, Pallas kernels, prepare_own(): pl.pallas_call(functools.partial(own_kernel, plan), out_shape=(jax.ShapeD...  7 us
    ppermute x15, starting transfers between devices, swap(): return lax.ppermute(piece, 'lag', [(i ^ mask, i) for i in range(count)])  6.74 us
    ppermute x15, waiting for transfers between devices, swap(): return lax.ppermute(piece, 'lag', [(i ^ mask, i) for i in range(count)])  6.04 us
    ppermute x8, waiting for transfers between devices, from_ahead(): lax.ppermute(piece, 'chan', [((i + distance) % count, i) for i in range(c...  5.37 us
    unnamed x6, local copies, waits for them, and re-layouts  2.22 us
  transfers between devices with their start and end apart: 23, of which 9 were waited for; matrix products, arithmetic and copies ran while one was open for 0% of the time, Pallas kernels for 38%

profile of v1, /device:TPU:0, one launch (start us, length us, event | category | flops | bytes accessed | tf_op | source)
XLA Modules:
  0.0 68.5 jit_solution(3342456338577736429)
XLA Ops:
  0.0 2.0 %local_rows.1.refs_0_ = bf16[72,1024]{1,0:T(8,128)(2,1)} custom-call(f32[1,16]{1,0:T(1,128)} %bitcast.4, bf16[100,8,128]{2,1,0:T(8,128)(2,1)} %bitcast.7), custom_call_target="tpu_custom_call" | custom-call | tf_op jit(solution)/shard_map/local_rows/pallas_call | solution.py:74
  2.0 2.9 %collective-permute-start.1 = (bf16[72,1024]{1,0:T(8,128)(2,1)}, bf16[72,1024]{1,0:T(8,128)(2,1)S(1)}, u32[]{:S(2)}, u32[]{:S(2)}) collective-permute-start(bf16[72,1024]{1,0:T(8,128)(2,1)} %local_rows.1.refs_0_), channel_id=1, source_target_pairs={{2,0},{3,1},{0,2},{1,3},{6,4},{7,5},{4,6},{5,7},{10,8},{11,9},{8,1... | collective-permute-start | bytes 442376 | tf_op jit(solution)/shard_map/ppermute | solution.py:313
  4.9 1.5 %collective-permute-start.2 = (bf16[72,1024]{1,0:T(8,128)(2,1)}, bf16[72,1024]{1,0:T(8,128)(2,1)S(1)}, u32[]{:S(2)}, u32[]{:S(2)}) collective-permute-start(bf16[72,1024]{1,0:T(8,128)(2,1)} %local_rows.1.refs_0_), channel_id=1, source_target_pairs={{4,0},{5,1},{6,2},{7,3},{0,4},{1,5},{2,6},{3,7},{12,8},{13,9},{14,... | collective-permute-start | bytes 442376 | tf_op jit(solution)/shard_map/ppermute | solution.py:313
  6.4 0.7 copy-done.1
  7.1 0.7 copy-done.2
  7.7 0.9 %tables.1 = (bf16[200,704]{1,0:T(8,128)(2,1)S(1)}, bf16[200,704]{1,0:T(8,128)(2,1)S(1)}, bf16[64,640]{1,0:T(8,128)(2,1)S(1)}) custom-call(f32[1,16]{1,0:T(1,128)S(1)} %bitcast.5, f32[1,65]{1,0:T(1,128)S(1)} %bitcast.6), custom_call_target="tpu_custom_call" | custom-call | flops 500000000 | bytes 2000000 | tf_op jit(solution)/shard_map/tables/pallas_call | solution.py:121
  8.6 0.8 %collective-permute-done.1.refs_2_ = bf16[72,1024]{1,0:T(8,128)(2,1)S(1)} collective-permute-done((bf16[72,1024]{1,0:T(8,128)(2,1)}, bf16[72,1024]{1,0:T(8,128)(2,1)S(1)}, u32[]{:S(2)}, u32[]{:S(2)}) %collective-permute-start.1) | collective-permute-done | bytes 147488 | tf_op jit(solution)/shard_map/ppermute | solution.py:313
  9.5 4.1 %collective-permute-done.2.refs_4_ = bf16[72,1024]{1,0:T(8,128)(2,1)S(1)} collective-permute-done((bf16[72,1024]{1,0:T(8,128)(2,1)}, bf16[72,1024]{1,0:T(8,128)(2,1)S(1)}, u32[]{:S(2)}, u32[]{:S(2)}) %collective-permute-start.2) | collective-permute-done | bytes 147488 | tf_op jit(solution)/shard_map/ppermute | solution.py:313
  13.6 0.5 collective-permute-start.5
  14.1 3.6 %collective-permute-start.7 = (bf16[72,1024]{1,0:T(8,128)(2,1)}, bf16[72,1024]{1,0:T(8,128)(2,1)S(1)}, u32[]{:S(2)}, u32[]{:S(2)}) collective-permute-start(bf16[72,1024]{1,0:T(8,128)(2,1)} %local_rows.1.refs_0_), channel_id=1, source_target_pairs={{8,0},{16,8},{24,16},{0,24},{9,1},{17,9},{25,17},{1,25},{10,2},{18... | collective-permute-start | bytes 442376 | tf_op jit(solution)/shard_map/ppermute | solution.py:318
  17.7 0.4 collective-permute-start.10
  18.2 0.5 collective-permute-start.8
  18.6 0.5 collective-permute-start.9
  19.1 0.9 %copy-done = bf16[72,1024]{1,0:T(8,128)(2,1)S(1)} copy-done((bf16[72,1024]{1,0:T(8,128)(2,1)S(1)}, bf16[72,1024]{1,0:T(8,128)(2,1)}, u32[]{:S(2)}) %copy-start) | copy-done | bytes 147480
  20.0 7.0 %prepare_own.1 = (bf16[3,1024,1664]{2,1,0:T(8,128)(2,1)S(1)}, bf16[3,1664,512]{2,1,0:T(8,128)(2,1)S(1)}) custom-call(s32[1]{0:T(128)} %bitcast.place_ref, bf16[72,1024]{1,0:T(8,128)(2,1)S(1)} %copy-done, bf16[72,1024]{1,0:T(8,128)(2,1)S(1)} %collective-permute-done.refs_1_, bf16[72,1024]{1,0:T(8,128)(2,1)S(1)} %collective-permute-done.1.refs_2_, ...), custom_call_target="tpu_custom_call" | custom-call | flops 5000000000 | bytes 1048576 | tf_op jit(solution)/shard_map/prepare_own/pallas_call | solution.py:254
  27.0 1.4 %collective-permute-done.8.refs_2_ = bf16[72,1024]{1,0:T(8,128)(2,1)S(1)} collective-permute-done((bf16[72,1024]{1,0:T(8,128)(2,1)S(1)}, bf16[72,1024]{1,0:T(8,128)(2,1)S(1)}, u32[]{:S(2)}, u32[]{:S(2)}) %collective-permute-start.8) | collective-permute-done | bytes 147488 | tf_op jit(solution)/shard_map/ppermute | solution.py:318
  28.4 2.8 %collective-permute-done.9.refs_4_ = bf16[72,1024]{1,0:T(8,128)(2,1)S(1)} collective-permute-done((bf16[72,1024]{1,0:T(8,128)(2,1)S(1)}, bf16[72,1024]{1,0:T(8,128)(2,1)S(1)}, u32[]{:S(2)}, u32[]{:S(2)}) %collective-permute-start.9) | collective-permute-done | bytes 147488 | tf_op jit(solution)/shard_map/ppermute | solution.py:318
  31.2 4.3 %collective-permute-start.15 = (bf16[72,1024]{1,0:T(8,128)(2,1)S(1)}, bf16[72,1024]{1,0:T(8,128)(2,1)S(1)}, u32[]{:S(2)}, u32[]{:S(2)}) collective-permute-start(bf16[72,1024]{1,0:T(8,128)(2,1)S(1)} %collective-permute-done.7.refs_0_), channel_id=1, source_target_pairs={{8,0},{16,8},{24,16},{0,24},{9,1},{17,9},{25,17},{1,25},{10,2},{18... | collective-permute-start | bytes 442376 | tf_op jit(solution)/shard_map/ppermute | solution.py:318
  35.5 0.2 collective-permute-start.12
  35.7 0.3 collective-permute-start.13
  36.0 0.2 collective-permute-start.14
  36.2 7.4 %own_correlation.1.refs_12_ = f32[128,3,64,128]{3,2,1,0:T(8,128)} custom-call(bf16[3,1024,1664]{2,1,0:T(8,128)(2,1)S(1)} %get-tuple-element.40.left_ref.refs_11_, bf16[3,1664,512]{2,1,0:T(8,128)(2,1)S(1)} %get-tuple-element.41.right_ref), custom_call_target="tpu_custom_call" | custom-call | flops 5234491392 | bytes 8388608 | tf_op jit(solution)/shard_map/own_correlation/pallas_call | solution.py:281
  43.6 0.3 collective-permute-start.16
  43.9 0.3 collective-permute-start.18
  44.3 10.5 %other_correlation.2.refs_12_ = f32[128,3,64,128]{3,2,1,0:T(8,128)} custom-call(s32[1]{0:T(128)} %bitcast.place_ref, bf16[72,1024]{1,0:T(8,128)(2,1)S(1)} %collective-permute-done.7.refs_0_, bf16[72,1024]{1,0:T(8,128)(2,1)S(1)} %collective-permute-done.11.refs_1_, ...), custom_call_target="tpu_custom_call", output_to_operand_aliasing={{}: (13, {})} | custom-call | flops 5234491392 | bytes 8388608 | tf_op jit(solution)/shard_map/other_correlation/pallas_call | solution.py:296
  54.7 1.2 %collective-permute-done.18.refs_6_ = bf16[72,1024]{1,0:T(8,128)(2,1)S(1)} collective-permute-done((bf16[72,1024]{1,0:T(8,128)(2,1)S(1)}, bf16[72,1024]{1,0:T(8,128)(2,1)S(1)}, u32[]{:S(2)}, u32[]{:S(2)}) %collective-permute-start.18) | collective-permute-done | bytes 147488 | tf_op jit(solution)/shard_map/ppermute | solution.py:318
  55.9 0.5 collective-permute-start.20
  56.4 0.5 collective-permute-start.22
  56.9 0.3 collective-permute-done.19.refs_1_
  57.3 0.2 collective-permute-done.20.refs_3_
  57.5 0.3 collective-permute-done.21.refs_5_
  58.0 10.5 %other_correlation.3 = f32[128,3,64,128]{3,2,1,0:T(8,128)} custom-call(s32[1]{0:T(128)} %bitcast.place_ref, bf16[72,1024]{1,0:T(8,128)(2,1)S(1)} %collective-permute-done.15.refs_0_, bf16[72,1024]{1,0:T(8,128)(2,1)S(1)} %collective-permute-done.19.refs_1_, bf16[72,1024]{1,0:T(8,128)(2,1)S(1)} %collective-permute-done.16.refs_2_, ...), custom_call_target="tpu_custom_call", output_to_operand_aliasing={{}: (13, {})} | custom-call | flops 5234491392 | bytes 8388608 | tf_op jit(solution)/shard_map/other_correlation/pallas_call | solution.py:296
  (26 shorter events, 0.3 us)
Async XLA Ops:
  2.0 7.5 %collective-permute-start.1 = (bf16[72,1024]{1,0:T(8,128)(2,1)}, bf16[72,1024]{1,0:T(8,128)(2,1)S(1)}, u32[]{:S(2)}, u32[]{:S(2)}) collective-permute-start(bf16[72,1024]{1,0:T(8,128)(2,1)} %local_rows.1.refs_0_), channel_id=1, source_target_pairs={{2,0},{3,1},{0,2},{1,3},{6,4},{7,5},{4,6},{5,7},{10,8},{11,9},{8,1... | collective-permute-start | bytes 442376 | tf_op jit(solution)/shard_map/ppermute | solution.py:313
  4.9 8.7 %collective-permute-start.2 = (bf16[72,1024]{1,0:T(8,128)(2,1)}, bf16[72,1024]{1,0:T(8,128)(2,1)S(1)}, u32[]{:S(2)}, u32[]{:S(2)}) collective-permute-start(bf16[72,1024]{1,0:T(8,128)(2,1)} %local_rows.1.refs_0_), channel_id=1, source_target_pairs={{4,0},{5,1},{6,2},{7,3},{0,4},{1,5},{2,6},{3,7},{12,8},{13,9},{14,... | collective-permute-start | bytes 442376 | tf_op jit(solution)/shard_map/ppermute | solution.py:313
  6.4 7.2 %collective-permute-start.3 = (bf16[72,1024]{1,0:T(8,128)(2,1)}, bf16[72,1024]{1,0:T(8,128)(2,1)S(1)}, u32[]{:S(2)}, u32[]{:S(2)}) collective-permute-start(bf16[72,1024]{1,0:T(8,128)(2,1)} %local_rows.1.refs_0_), channel_id=1, source_target_pairs={{6,0},{7,1},{4,2},{5,3},{2,4},{3,5},{0,6},{1,7},{14,8},{15,9},{12,... | collective-permute-start | bytes 442376 | tf_op jit(solution)/shard_map/ppermute | solution.py:313
  6.4 11.3 %collective-permute-start = (bf16[72,1024]{1,0:T(8,128)(2,1)}, bf16[72,1024]{1,0:T(8,128)(2,1)S(1)}, u32[]{:S(2)}, u32[]{:S(2)}) collective-permute-start(bf16[72,1024]{1,0:T(8,128)(2,1)} %local_rows.1.refs_0_), channel_id=1, source_target_pairs={{1,0},{0,1},{3,2},{2,3},{5,4},{4,5},{7,6},{6,7},{9,8},{8,9},{11,10... | collective-permute-start | bytes 442376 | tf_op jit(solution)/shard_map/ppermute | solution.py:313
  6.4 0.7 copy-start.1
  7.1 0.7 copy-start.2
  13.6 4.6 %collective-permute-start.4 = (bf16[72,1024]{1,0:T(8,128)(2,1)S(1)}, bf16[72,1024]{1,0:T(8,128)(2,1)S(1)}, u32[]{:S(2)}, u32[]{:S(2)}) collective-permute-start(bf16[72,1024]{1,0:T(8,128)(2,1)S(1)} %collective-permute-done.1.refs_2_), channel_id=1, source_target_pairs={{1,0},{0,1},{3,2},{2,3},{5,4},{4,5},{7,6},{6,7},{9,8},{8,9},{11,10... | collective-permute-start | bytes 442376 | tf_op jit(solution)/shard_map/ppermute | solution.py:313
  13.6 5.0 %collective-permute-start.5 = (bf16[72,1024]{1,0:T(8,128)(2,1)S(1)}, bf16[72,1024]{1,0:T(8,128)(2,1)S(1)}, u32[]{:S(2)}, u32[]{:S(2)}) collective-permute-start(bf16[72,1024]{1,0:T(8,128)(2,1)S(1)} %collective-permute-done.2.refs_4_), channel_id=1, source_target_pairs={{1,0},{0,1},{3,2},{2,3},{5,4},{4,5},{7,6},{6,7},{9,8},{8,9},{11,10... | collective-permute-start | bytes 442376 | tf_op jit(solution)/shard_map/ppermute | solution.py:313
  14.1 5.0 %collective-permute-start.6 = (bf16[72,1024]{1,0:T(8,128)(2,1)S(1)}, bf16[72,1024]{1,0:T(8,128)(2,1)S(1)}, u32[]{:S(2)}, u32[]{:S(2)}) collective-permute-start(bf16[72,1024]{1,0:T(8,128)(2,1)S(1)} %collective-permute-done.3.refs_6_), channel_id=1, source_target_pairs={{1,0},{0,1},{3,2},{2,3},{5,4},{4,5},{7,6},{6,7},{9,8},{8,9},{11,10... | collective-permute-start | bytes 442376 | tf_op jit(solution)/shard_map/ppermute | solution.py:313
  14.1 12.9 %collective-permute-start.7 = (bf16[72,1024]{1,0:T(8,128)(2,1)}, bf16[72,1024]{1,0:T(8,128)(2,1)S(1)}, u32[]{:S(2)}, u32[]{:S(2)}) collective-permute-start(bf16[72,1024]{1,0:T(8,128)(2,1)} %local_rows.1.refs_0_), channel_id=1, source_target_pairs={{8,0},{16,8},{24,16},{0,24},{9,1},{17,9},{25,17},{1,25},{10,2},{18... | collective-permute-start | bytes 442376 | tf_op jit(solution)/shard_map/ppermute | solution.py:318
  17.7 9.3 %collective-permute-start.10 = (bf16[72,1024]{1,0:T(8,128)(2,1)S(1)}, bf16[72,1024]{1,0:T(8,128)(2,1)S(1)}, u32[]{:S(2)}, u32[]{:S(2)}) collective-permute-start(bf16[72,1024]{1,0:T(8,128)(2,1)S(1)} %collective-permute-done.3.refs_6_), channel_id=1, source_target_pairs={{8,0},{16,8},{24,16},{0,24},{9,1},{17,9},{25,17},{1,25},{10,2},{18... | collective-permute-start | bytes 442376 | tf_op jit(solution)/shard_map/ppermute | solution.py:318
  18.2 10.2 %collective-permute-start.8 = (bf16[72,1024]{1,0:T(8,128)(2,1)S(1)}, bf16[72,1024]{1,0:T(8,128)(2,1)S(1)}, u32[]{:S(2)}, u32[]{:S(2)}) collective-permute-start(bf16[72,1024]{1,0:T(8,128)(2,1)S(1)} %collective-permute-done.1.refs_2_), channel_id=1, source_target_pairs={{8,0},{16,8},{24,16},{0,24},{9,1},{17,9},{25,17},{1,25},{10,2},{18... | collective-permute-start | bytes 442376 | tf_op jit(solution)/shard_map/ppermute | solution.py:318
  18.6 12.6 %collective-permute-start.9 = (bf16[72,1024]{1,0:T(8,128)(2,1)S(1)}, bf16[72,1024]{1,0:T(8,128)(2,1)S(1)}, u32[]{:S(2)}, u32[]{:S(2)}) collective-permute-start(bf16[72,1024]{1,0:T(8,128)(2,1)S(1)} %collective-permute-done.2.refs_4_), channel_id=1, source_target_pairs={{8,0},{16,8},{24,16},{0,24},{9,1},{17,9},{25,17},{1,25},{10,2},{18... | collective-permute-start | bytes 442376 | tf_op jit(solution)/shard_map/ppermute | solution.py:318
  19.1 0.9 %copy-start = (bf16[72,1024]{1,0:T(8,128)(2,1)S(1)}, bf16[72,1024]{1,0:T(8,128)(2,1)}, u32[]{:S(2)}) copy-start(bf16[72,1024]{1,0:T(8,128)(2,1)} %local_rows.1.refs_0_) | copy-start | bytes 442372
  31.2 12.4 %collective-permute-start.11 = (bf16[72,1024]{1,0:T(8,128)(2,1)S(1)}, bf16[72,1024]{1,0:T(8,128)(2,1)S(1)}, u32[]{:S(2)}, u32[]{:S(2)}) collective-permute-start(bf16[72,1024]{1,0:T(8,128)(2,1)S(1)} %collective-permute-done.7.refs_0_), channel_id=1, source_target_pairs={{1,0},{0,1},{3,2},{2,3},{5,4},{4,5},{7,6},{6,7},{9,8},{8,9},{11,10... | collective-permute-start | bytes 442376 | tf_op jit(solution)/shard_map/ppermute | solution.py:313
  31.2 23.6 %collective-permute-start.15 = (bf16[72,1024]{1,0:T(8,128)(2,1)S(1)}, bf16[72,1024]{1,0:T(8,128)(2,1)S(1)}, u32[]{:S(2)}, u32[]{:S(2)}) collective-permute-start(bf16[72,1024]{1,0:T(8,128)(2,1)S(1)} %collective-permute-done.7.refs_0_), channel_id=1, source_target_pairs={{8,0},{16,8},{24,16},{0,24},{9,1},{17,9},{25,17},{1,25},{10,2},{18... | collective-permute-start | bytes 442376 | tf_op jit(solution)/shard_map/ppermute | solution.py:318
  35.5 8.4 %collective-permute-start.12 = (bf16[72,1024]{1,0:T(8,128)(2,1)S(1)}, bf16[72,1024]{1,0:T(8,128)(2,1)S(1)}, u32[]{:S(2)}, u32[]{:S(2)}) collective-permute-start(bf16[72,1024]{1,0:T(8,128)(2,1)S(1)} %collective-permute-done.8.refs_2_), channel_id=1, source_target_pairs={{1,0},{0,1},{3,2},{2,3},{5,4},{4,5},{7,6},{6,7},{9,8},{8,9},{11,10... | collective-permute-start | bytes 442376 | tf_op jit(solution)/shard_map/ppermute | solution.py:313
  35.7 8.2 %collective-permute-start.13 = (bf16[72,1024]{1,0:T(8,128)(2,1)S(1)}, bf16[72,1024]{1,0:T(8,128)(2,1)S(1)}, u32[]{:S(2)}, u32[]{:S(2)}) collective-permute-start(bf16[72,1024]{1,0:T(8,128)(2,1)S(1)} %collective-permute-done.9.refs_4_), channel_id=1, source_target_pairs={{1,0},{0,1},{3,2},{2,3},{5,4},{4,5},{7,6},{6,7},{9,8},{8,9},{11,10... | collective-permute-start | bytes 442376 | tf_op jit(solution)/shard_map/ppermute | solution.py:313
  36.0 8.3 %collective-permute-start.14 = (bf16[72,1024]{1,0:T(8,128)(2,1)S(1)}, bf16[72,1024]{1,0:T(8,128)(2,1)S(1)}, u32[]{:S(2)}, u32[]{:S(2)}) collective-permute-start(bf16[72,1024]{1,0:T(8,128)(2,1)S(1)} %collective-permute-done.10.refs_6_), channel_id=1, source_target_pairs={{1,0},{0,1},{3,2},{2,3},{5,4},{4,5},{7,6},{6,7},{9,8},{8,9},{11,10... | collective-permute-start | bytes 442376 | tf_op jit(solution)/shard_map/ppermute | solution.py:313
  43.6 11.2 %collective-permute-start.16 = (bf16[72,1024]{1,0:T(8,128)(2,1)S(1)}, bf16[72,1024]{1,0:T(8,128)(2,1)S(1)}, u32[]{:S(2)}, u32[]{:S(2)}) collective-permute-start(bf16[72,1024]{1,0:T(8,128)(2,1)S(1)} %collective-permute-done.8.refs_2_), channel_id=1, source_target_pairs={{8,0},{16,8},{24,16},{0,24},{9,1},{17,9},{25,17},{1,25},{10,2},{18... | collective-permute-start | bytes 442376 | tf_op jit(solution)/shard_map/ppermute | solution.py:318
  43.9 10.9 %collective-permute-start.17 = (bf16[72,1024]{1,0:T(8,128)(2,1)S(1)}, bf16[72,1024]{1,0:T(8,128)(2,1)S(1)}, u32[]{:S(2)}, u32[]{:S(2)}) collective-permute-start(bf16[72,1024]{1,0:T(8,128)(2,1)S(1)} %collective-permute-done.9.refs_4_), channel_id=1, source_target_pairs={{8,0},{16,8},{24,16},{0,24},{9,1},{17,9},{25,17},{1,25},{10,2},{18... | collective-permute-start | bytes 442376 | tf_op jit(solution)/shard_map/ppermute | solution.py:318
  43.9 12.0 %collective-permute-start.18 = (bf16[72,1024]{1,0:T(8,128)(2,1)S(1)}, bf16[72,1024]{1,0:T(8,128)(2,1)S(1)}, u32[]{:S(2)}, u32[]{:S(2)}) collective-permute-start(bf16[72,1024]{1,0:T(8,128)(2,1)S(1)} %collective-permute-done.10.refs_6_), channel_id=1, source_target_pairs={{8,0},{16,8},{24,16},{0,24},{9,1},{17,9},{25,17},{1,25},{10,2},{18... | collective-permute-start | bytes 442376 | tf_op jit(solution)/shard_map/ppermute | solution.py:318
  55.9 1.4 %collective-permute-start.19 = (bf16[72,1024]{1,0:T(8,128)(2,1)S(1)}, bf16[72,1024]{1,0:T(8,128)(2,1)S(1)}, u32[]{:S(2)}, u32[]{:S(2)}) collective-permute-start(bf16[72,1024]{1,0:T(8,128)(2,1)S(1)} %collective-permute-done.15.refs_0_), channel_id=1, source_target_pairs={{1,0},{0,1},{3,2},{2,3},{5,4},{4,5},{7,6},{6,7},{9,8},{8,9},{11,10... | collective-permute-start | bytes 442376 | tf_op jit(solution)/shard_map/ppermute | solution.py:313
  55.9 1.6 %collective-permute-start.20 = (bf16[72,1024]{1,0:T(8,128)(2,1)S(1)}, bf16[72,1024]{1,0:T(8,128)(2,1)S(1)}, u32[]{:S(2)}, u32[]{:S(2)}) collective-permute-start(bf16[72,1024]{1,0:T(8,128)(2,1)S(1)} %collective-permute-done.16.refs_2_), channel_id=1, source_target_pairs={{1,0},{0,1},{3,2},{2,3},{5,4},{4,5},{7,6},{6,7},{9,8},{8,9},{11,10... | collective-permute-start | bytes 442376 | tf_op jit(solution)/shard_map/ppermute | solution.py:313
  56.4 1.4 %collective-permute-start.21 = (bf16[72,1024]{1,0:T(8,128)(2,1)S(1)}, bf16[72,1024]{1,0:T(8,128)(2,1)S(1)}, u32[]{:S(2)}, u32[]{:S(2)}) collective-permute-start(bf16[72,1024]{1,0:T(8,128)(2,1)S(1)} %collective-permute-done.17.refs_4_), channel_id=1, source_target_pairs={{1,0},{0,1},{3,2},{2,3},{5,4},{4,5},{7,6},{6,7},{9,8},{8,9},{11,10... | collective-permute-start | bytes 442376 | tf_op jit(solution)/shard_map/ppermute | solution.py:313
  56.4 1.6 %collective-permute-start.22 = (bf16[72,1024]{1,0:T(8,128)(2,1)S(1)}, bf16[72,1024]{1,0:T(8,128)(2,1)S(1)}, u32[]{:S(2)}, u32[]{:S(2)}) collective-permute-start(bf16[72,1024]{1,0:T(8,128)(2,1)S(1)} %collective-permute-done.18.refs_6_), channel_id=1, source_target_pairs={{1,0},{0,1},{3,2},{2,3},{5,4},{4,5},{7,6},{6,7},{9,8},{8,9},{11,10... | collective-permute-start | bytes 442376 | tf_op jit(solution)/shard_map/ppermute | solution.py:313

commit v2 on v1

--- a/solution.py
+++ b/solution.py
@@ -49,7 +49,7 @@
     return taps[0:1, index : index + 1].astype(BF16).astype(F32)
 
 
-def local_kernel(plan, taps_ref, raw_ref, out_ref, spread):
+def local_kernel(plan, taps_ref, raw_ref, sent_ref, kept_ref, spread):
     row = lax.broadcasted_iota(jnp.int32, (plan.rows, plan.raw), 0)
     time = lax.broadcasted_iota(jnp.int32, (plan.rows, plan.raw), 1)
     tap = 2 * (row + plan.head) - time
@@ -65,17 +65,17 @@
     spread[...] = raw_ref[...].astype(F32).reshape(plan.raw * plan.windows, plan.channels)
     for w in range(plan.windows):
         series = spread[pl.ds(w, plan.raw, stride=plan.windows), :].astype(BF16)
-        out_ref[:, w * plan.channels : (w + 1) * plan.channels] = jnp.dot(
-            table, series, preferred_element_type=F32
-        ).astype(BF16)
+        rows = jnp.dot(table, series, preferred_element_type=F32).astype(BF16)
+        for ref in (sent_ref, kept_ref):
+            ref[:, w * plan.channels : (w + 1) * plan.channels] = rows
 
 
 def local_rows(plan, raw, taps):
     return pl.pallas_call(
         functools.partial(local_kernel, plan),
-        out_shape=jax.ShapeDtypeStruct((plan.rows, plan.wide), BF16),
+        out_shape=[jax.ShapeDtypeStruct((plan.rows, plan.wide), BF16)] * 2,
         in_specs=[VMEM, VMEM],
-        out_specs=VMEM,
+        out_specs=[VMEM, VMEM],
         scratch_shapes=[pltpu.VMEM((plan.raw * plan.windows, plan.channels), F32)],
         name="local_rows",
     )(taps, jnp.transpose(raw, (2, 0, 1)))
@@ -263,7 +263,7 @@
         + [pltpu.VMEM((SUB + plan.deep, plan.channels), F32)] * 2
         + [pltpu.VMEM((2, plan.channels * SUB, LANES), F32)] * 2,
         compiler_params=pltpu.CompilerParams(vmem_limit_bytes=33 * 2**20),
-        cost_estimate=pl.CostEstimate(flops=5_000_000_000, bytes_accessed=2**20, transcendentals=0),
+        cost_estimate=pl.CostEstimate(flops=100_000_000, bytes_accessed=2**18, transcendentals=0),
         name="prepare_own",
     )(place, *pieces, *tabs)
 
@@ -318,8 +318,9 @@
     return lax.ppermute(piece, "chan", [((i + distance) % count, i) for i in range(count)])
 
 
-def same_core(piece):
-    return [swap(piece, mask) if mask else piece for mask in range(0, lax.axis_size("lag"), 2)]
+def same_core(piece, start=None, stop=None):
+    masks = list(range(0, lax.axis_size("lag"), 2))[start:stop]
+    return [swap(piece, mask) if mask else piece for mask in masks]
 
 
 def both_cores(held):
@@ -331,23 +332,24 @@
     pairs = lax.axis_size("chan") // 2 + 1
     place = lax.axis_index("lag").astype(jnp.int32).reshape(1)
     dec_taps = decimation_taps.reshape(1, -1)
-    piece = local_rows(plan, raw_samples, dec_taps)
+    piece, kept = local_rows(plan, raw_samples, dec_taps)
     tabs = tables(plan, dec_taps, bandpass_taps.reshape(1, -1))
     count = 32
-    held = same_core(piece)
-    tabs, held[1:] = lax.optimization_barrier((tabs, held[1:]))
-    left, right = prepare_own(plan, place, both_cores(held), tabs)
-    ahead = [from_ahead(x, 1) for x in held]
-    left, ahead = lax.optimization_barrier((left, ahead))
+    own = same_core(piece)
+    far = [from_ahead(piece, distance) for distance in range(1, pairs)]
+    tabs, own[1:] = lax.optimization_barrier((tabs, own[1:]))
+    pieces, far[0] = lax.optimization_barrier((both_cores(own), far[0]))
+    left, right = prepare_own(plan, place, [kept, *pieces[1:]], tabs)
+    left, far = lax.optimization_barrier((left, far))
+    held = same_core(far[0])
+    early = same_core(far[1], stop=-1) if pairs > 2 else None
     out = own_correlation(plan, count, pairs, left, right)
     for distance in range(1, pairs):
-        pieces = both_cores(ahead)
+        out, held, far = lax.optimization_barrier((out, held, far))
+        pieces = both_cores(held)
         if distance + 1 < pairs:
-            ahead = [from_ahead(x, 1) for x in ahead]
-        out_next = other_correlation(plan, count, pairs, distance, place, pieces, tabs, left, out)
-        if distance + 1 < pairs:
-            out_next, ahead = lax.optimization_barrier((out_next, ahead))
-        out = out_next
+            held = early + same_core(far[distance], start=-1) if distance == 1 else same_core(far[distance])
+        out = other_correlation(plan, count, pairs, distance, place, pieces, tabs, left, out)
     return out
 
 

time: 68.6 us -> 63.9 us (0.931)
  waiting for transfers between devices: 11.4 us -> 1.97 us
  starting transfers between devices: 16.7 us -> 20.8 us
    ppermute x15 -> x21, starting transfers between devices: 6.74 us -> 14.2 us  [swap(): return lax.ppermute(piece, 'lag', [(i ^ mask, i) for i in range(count)])]
    ppermute x8 -> x2, waiting for transfers between devices: 5.37 us -> 0.01 us  [from_ahead(): lax.ppermute(piece, 'chan', [((i + distance) % count, i) for i in range(c...]
    ppermute x15 -> x21, waiting for transfers between devices: 6.04 us -> 1.97 us  [swap(): return lax.ppermute(piece, 'lag', [(i ^ mask, i) for i in range(count)])]
    ppermute x8 -> x2, starting transfers between devices: 9.91 us -> 6.67 us  [from_ahead(): lax.ppermute(piece, 'chan', [((i + distance) % count, i) for i in range(c...]
  transfers between devices with their start and end apart: 23 -> 23, of which waited for: 9 -> 5; matrix products, arithmetic and copies ran while one was open for 0% -> 0% of each run, Pallas kernels for 38% -> 41%
where the time goes in v2:
time: 63.9 us; the launch traced here: 63.8 us
  Pallas kernels  38.6 us (60%)
  starting transfers between devices  20.8 us (33%)
  local copies, waits for them, and re-layouts  2.21 us (3%)
  waiting for transfers between devices  1.97 us (3%)
    pallas_call x2, Pallas kernels, other_correlation(): pl.pallas_call(functools.partial(other_kernel, plan, count), grid=(plan.c...  21.4 us
    ppermute x21, starting transfers between devices, swap(): return lax.ppermute(piece, 'lag', [(i ^ mask, i) for i in range(count)])  14.2 us
    pallas_call x1, Pallas kernels, own_correlation(): pl.pallas_call(functools.partial(first_kernel, plan, count), grid=(plan.c...  7.38 us
    pallas_call x1, Pallas kernels, prepare_own(): pl.pallas_call(functools.partial(own_kernel, plan), out_shape=(jax.ShapeD...  7 us
    ppermute x2, starting transfers between devices, from_ahead(): lax.ppermute(piece, 'chan', [((i + distance) % count, i) for i in range(c...  6.67 us
    unnamed x6, local copies, waits for them, and re-layouts  2.21 us
    pallas_call x1, Pallas kernels, local_rows(): pl.pallas_call(functools.partial(local_kernel, plan), out_shape=[jax.Shap...  2.01 us
    ppermute x21, waiting for transfers between devices, swap(): return lax.ppermute(piece, 'lag', [(i ^ mask, i) for i in range(count)])  1.97 us
  transfers between devices with their start and end apart: 23, of which 5 were waited for; matrix products, arithmetic and copies ran while one was open for 0% of the time, Pallas kernels for 41%

profile of v2, /device:TPU:0, one launch (start us, length us, event | category | flops | bytes accessed | tf_op | source)
XLA Modules:
  0.0 63.8 jit_solution(1037020644512984811)
XLA Ops:
  0.0 2.0 %local_rows.1 = (bf16[72,1024]{1,0:T(8,128)(2,1)}, bf16[72,1024]{1,0:T(8,128)(2,1)}) custom-call(f32[1,16]{1,0:T(1,128)} %bitcast.4, bf16[100,8,128]{2,1,0:T(8,128)(2,1)} %bitcast.7), custom_call_target="tpu_custom_call" | custom-call | tf_op jit(solution)/shard_map/local_rows/pallas_call | solution.py:74
  2.0 2.9 %collective-permute-start.1 = (bf16[72,1024]{1,0:T(8,128)(2,1)}, bf16[72,1024]{1,0:T(8,128)(2,1)S(1)}, u32[]{:S(2)}, u32[]{:S(2)}) collective-permute-start(bf16[72,1024]{1,0:T(8,128)(2,1)} %get-tuple-element.41), channel_id=1, source_target_pairs={{2,0},{3,1},{0,2},{1,3},{6,4},{7,5},{4,6},{5,7},{10,8},{11,9},{8,1... | collective-permute-start | bytes 442376 | tf_op jit(solution)/shard_map/ppermute | solution.py:313
  5.0 1.5 %collective-permute-start.2 = (bf16[72,1024]{1,0:T(8,128)(2,1)}, bf16[72,1024]{1,0:T(8,128)(2,1)S(1)}, u32[]{:S(2)}, u32[]{:S(2)}) collective-permute-start(bf16[72,1024]{1,0:T(8,128)(2,1)} %get-tuple-element.41), channel_id=1, source_target_pairs={{4,0},{5,1},{6,2},{7,3},{0,4},{1,5},{2,6},{3,7},{12,8},{13,9},{14,... | collective-permute-start | bytes 442376 | tf_op jit(solution)/shard_map/ppermute | solution.py:313
  6.5 4.1 %collective-permute-start.7 = (bf16[72,1024]{1,0:T(8,128)(2,1)}, bf16[72,1024]{1,0:T(8,128)(2,1)S(1)}, u32[]{:S(2)}, u32[]{:S(2)}) collective-permute-start(bf16[72,1024]{1,0:T(8,128)(2,1)} %get-tuple-element.41), channel_id=1, source_target_pairs={{8,0},{16,8},{24,16},{0,24},{9,1},{17,9},{25,17},{1,25},{10,2},{18... | collective-permute-start | bytes 442376 | tf_op jit(solution)/shard_map/ppermute | solution.py:318
  10.6 0.7 %copy-done.1 = f32[16]{0:T(128)S(1)} copy-done((f32[16]{0:T(128)S(1)}, f32[16]{0:T(128)}, u32[]{:S(2)}) %copy-start.1) | copy-done | bytes 88
  11.2 0.7 %copy-done.2 = f32[65]{0:T(128)S(1)} copy-done((f32[65]{0:T(128)S(1)}, f32[65]{0:T(128)}, u32[]{:S(2)}) %copy-start.2) | copy-done | bytes 284
  11.9 0.9 %tables.1 = (bf16[200,704]{1,0:T(8,128)(2,1)S(1)}, bf16[200,704]{1,0:T(8,128)(2,1)S(1)}, bf16[64,640]{1,0:T(8,128)(2,1)S(1)}) custom-call(f32[1,16]{1,0:T(1,128)S(1)} %bitcast.5, f32[1,65]{1,0:T(1,128)S(1)} %bitcast.6), custom_call_target="tpu_custom_call" | custom-call | flops 500000000 | bytes 2000000 | tf_op jit(solution)/shard_map/tables/pallas_call | solution.py:121
  12.8 0.9 %collective-permute-done.2.refs_4_ = bf16[72,1024]{1,0:T(8,128)(2,1)S(1)} collective-permute-done((bf16[72,1024]{1,0:T(8,128)(2,1)}, bf16[72,1024]{1,0:T(8,128)(2,1)S(1)}, u32[]{:S(2)}, u32[]{:S(2)}) %collective-permute-start.2) | collective-permute-done | bytes 147488 | tf_op jit(solution)/shard_map/ppermute | solution.py:313
  13.6 0.5 collective-permute-start.5
  14.2 2.6 %collective-permute-start.8 = (bf16[72,1024]{1,0:T(8,128)(2,1)}, bf16[72,1024]{1,0:T(8,128)(2,1)S(1)}, u32[]{:S(2)}, u32[]{:S(2)}) collective-permute-start(bf16[72,1024]{1,0:T(8,128)(2,1)} %get-tuple-element.41), channel_id=1, source_target_pairs={{16,0},{24,8},{0,16},{8,24},{17,1},{25,9},{1,17},{9,25},{18,2},{26... | collective-permute-start | bytes 442376 | tf_op jit(solution)/shard_map/ppermute | solution.py:318
  16.8 0.9 %copy-done = bf16[72,1024]{1,0:T(8,128)(2,1)S(1)} copy-done((bf16[72,1024]{1,0:T(8,128)(2,1)S(1)}, bf16[72,1024]{1,0:T(8,128)(2,1)}, u32[]{:S(2)}) %copy-start) | copy-done | bytes 147480
  17.7 7.0 %prepare_own.1 = (bf16[3,1024,1664]{2,1,0:T(8,128)(2,1)S(1)}, bf16[3,1664,512]{2,1,0:T(8,128)(2,1)S(1)}) custom-call(s32[1]{0:T(128)} %bitcast.place_ref, bf16[72,1024]{1,0:T(8,128)(2,1)S(1)} %copy-done, bf16[72,1024]{1,0:T(8,128)(2,1)S(1)} %collective-permute-done.refs_1_, bf16[72,1024]{1,0:T(8,128)(2,1)S(1)} %collective-permute-done.1.refs_2_, ...), custom_call_target="tpu_custom_call" | custom-call | flops 100000000 | bytes 262144 | tf_op jit(solution)/shard_map/prepare_own/pallas_call | solution.py:254
  24.7 1.6 %collective-permute-start.10 = (bf16[72,1024]{1,0:T(8,128)(2,1)S(1)}, bf16[72,1024]{1,0:T(8,128)(2,1)S(1)}, u32[]{:S(2)}, u32[]{:S(2)}) collective-permute-start(bf16[72,1024]{1,0:T(8,128)(2,1)S(1)} %collective-permute-done.7.refs_0_), channel_id=1, source_target_pairs={{4,0},{5,1},{6,2},{7,3},{0,4},{1,5},{2,6},{3,7},{12,8},{13,9},{14,... | collective-permute-start | bytes 442376 | tf_op jit(solution)/shard_map/ppermute | solution.py:313
  26.3 1.2 %collective-permute-start.11 = (bf16[72,1024]{1,0:T(8,128)(2,1)S(1)}, bf16[72,1024]{1,0:T(8,128)(2,1)S(1)}, u32[]{:S(2)}, u32[]{:S(2)}) collective-permute-start(bf16[72,1024]{1,0:T(8,128)(2,1)S(1)} %collective-permute-done.7.refs_0_), channel_id=1, source_target_pairs={{6,0},{7,1},{4,2},{5,3},{2,4},{3,5},{0,6},{1,7},{14,8},{15,9},{12,... | collective-permute-start | bytes 442376 | tf_op jit(solution)/shard_map/ppermute | solution.py:313
  27.5 0.8 %collective-permute-start.9 = (bf16[72,1024]{1,0:T(8,128)(2,1)S(1)}, bf16[72,1024]{1,0:T(8,128)(2,1)S(1)}, u32[]{:S(2)}, u32[]{:S(2)}) collective-permute-start(bf16[72,1024]{1,0:T(8,128)(2,1)S(1)} %collective-permute-done.7.refs_0_), channel_id=1, source_target_pairs={{2,0},{3,1},{0,2},{1,3},{6,4},{7,5},{4,6},{5,7},{10,8},{11,9},{8,1... | collective-permute-start | bytes 442376 | tf_op jit(solution)/shard_map/ppermute | solution.py:313
  28.2 7.4 %own_correlation.1.refs_12_ = f32[128,3,64,128]{3,2,1,0:T(8,128)} custom-call(bf16[3,1024,1664]{2,1,0:T(8,128)(2,1)S(1)} %get-tuple-element.60.left_ref.refs_11_, bf16[3,1664,512]{2,1,0:T(8,128)(2,1)S(1)} %get-tuple-element.61.right_ref), custom_call_target="tpu_custom_call" | custom-call | flops 5234491392 | bytes 8388608 | tf_op jit(solution)/shard_map/own_correlation/pallas_call | solution.py:281
  35.6 0.1 collective-permute-start.12
  35.7 0.5 collective-permute-start.13
  36.2 0.1 collective-permute-start.14
  36.3 0.4 collective-permute-start.15
  36.7 1.2 %collective-permute-start.16 = (bf16[72,1024]{1,0:T(8,128)(2,1)S(1)}, bf16[72,1024]{1,0:T(8,128)(2,1)S(1)}, u32[]{:S(2)}, u32[]{:S(2)}) collective-permute-start(bf16[72,1024]{1,0:T(8,128)(2,1)S(1)} %collective-permute-done.8.refs_0_), channel_id=1, source_target_pairs={{2,0},{3,1},{0,2},{1,3},{6,4},{7,5},{4,6},{5,7},{10,8},{11,9},{8,1... | collective-permute-start | bytes 442376 | tf_op jit(solution)/shard_map/ppermute | solution.py:313
  38.0 0.9 %collective-permute-start.17 = (bf16[72,1024]{1,0:T(8,128)(2,1)S(1)}, bf16[72,1024]{1,0:T(8,128)(2,1)S(1)}, u32[]{:S(2)}, u32[]{:S(2)}) collective-permute-start(bf16[72,1024]{1,0:T(8,128)(2,1)S(1)} %collective-permute-done.8.refs_0_), channel_id=1, source_target_pairs={{4,0},{5,1},{6,2},{7,3},{0,4},{1,5},{2,6},{3,7},{12,8},{13,9},{14,... | collective-permute-start | bytes 442376 | tf_op jit(solution)/shard_map/ppermute | solution.py:313
  38.9 1.3 %collective-permute-start.18 = (bf16[72,1024]{1,0:T(8,128)(2,1)S(1)}, bf16[72,1024]{1,0:T(8,128)(2,1)S(1)}, u32[]{:S(2)}, u32[]{:S(2)}) collective-permute-start(bf16[72,1024]{1,0:T(8,128)(2,1)S(1)} %collective-permute-done.8.refs_0_), channel_id=1, source_target_pairs={{6,0},{7,1},{4,2},{5,3},{2,4},{3,5},{0,6},{1,7},{14,8},{15,9},{12,... | collective-permute-start | bytes 442376 | tf_op jit(solution)/shard_map/ppermute | solution.py:313
  40.2 10.7 %other_correlation.2.refs_12_ = f32[128,3,64,128]{3,2,1,0:T(8,128)} custom-call(s32[1]{0:T(128)} %bitcast.place_ref, bf16[72,1024]{1,0:T(8,128)(2,1)S(1)} %collective-permute-done.7.refs_0_, bf16[72,1024]{1,0:T(8,128)(2,1)S(1)} %collective-permute-done.12.refs_1_, ...), custom_call_target="tpu_custom_call", output_to_operand_aliasing={{}: (13, {})} | custom-call | flops 5234491392 | bytes 8388608 | tf_op jit(solution)/shard_map/other_correlation/pallas_call | solution.py:296
  51.0 0.5 collective-permute-start.20
  51.5 0.1 collective-permute-start.21
  51.6 0.4 collective-permute-start.22
  52.0 0.3 collective-permute-done.19.refs_1_
  52.4 0.2 collective-permute-done.20.refs_3_
  52.6 0.3 collective-permute-done.21.refs_5_
  52.9 0.2 collective-permute-done.22.refs_7_
  53.1 10.7 %other_correlation.3 = f32[128,3,64,128]{3,2,1,0:T(8,128)} custom-call(s32[1]{0:T(128)} %bitcast.place_ref, bf16[72,1024]{1,0:T(8,128)(2,1)S(1)} %collective-permute-done.8.refs_0_, bf16[72,1024]{1,0:T(8,128)(2,1)S(1)} %collective-permute-done.19.refs_1_, bf16[72,1024]{1,0:T(8,128)(2,1)S(1)} %collective-permute-done.16.refs_2_, ...), custom_call_target="tpu_custom_call", output_to_operand_aliasing={{}: (13, {})} | custom-call | flops 5234491392 | bytes 8388608 | tf_op jit(solution)/shard_map/other_correlation/pallas_call | solution.py:296
  (26 shorter events, 0.1 us)
Async XLA Ops:
  2.0 10.8 %collective-permute-start.1 = (bf16[72,1024]{1,0:T(8,128)(2,1)}, bf16[72,1024]{1,0:T(8,128)(2,1)S(1)}, u32[]{:S(2)}, u32[]{:S(2)}) collective-permute-start(bf16[72,1024]{1,0:T(8,128)(2,1)} %get-tuple-element.41), channel_id=1, source_target_pairs={{2,0},{3,1},{0,2},{1,3},{6,4},{7,5},{4,6},{5,7},{10,8},{11,9},{8,1... | collective-permute-start | bytes 442376 | tf_op jit(solution)/shard_map/ppermute | solution.py:313
  5.0 8.7 %collective-permute-start.2 = (bf16[72,1024]{1,0:T(8,128)(2,1)}, bf16[72,1024]{1,0:T(8,128)(2,1)S(1)}, u32[]{:S(2)}, u32[]{:S(2)}) collective-permute-start(bf16[72,1024]{1,0:T(8,128)(2,1)} %get-tuple-element.41), channel_id=1, source_target_pairs={{4,0},{5,1},{6,2},{7,3},{0,4},{1,5},{2,6},{3,7},{12,8},{13,9},{14,... | collective-permute-start | bytes 442376 | tf_op jit(solution)/shard_map/ppermute | solution.py:313
  6.5 7.2 %collective-permute-start.3 = (bf16[72,1024]{1,0:T(8,128)(2,1)}, bf16[72,1024]{1,0:T(8,128)(2,1)S(1)}, u32[]{:S(2)}, u32[]{:S(2)}) collective-permute-start(bf16[72,1024]{1,0:T(8,128)(2,1)} %get-tuple-element.41), channel_id=1, source_target_pairs={{6,0},{7,1},{4,2},{5,3},{2,4},{3,5},{0,6},{1,7},{14,8},{15,9},{12,... | collective-permute-start | bytes 442376 | tf_op jit(solution)/shard_map/ppermute | solution.py:313
  6.5 7.7 %collective-permute-start = (bf16[72,1024]{1,0:T(8,128)(2,1)}, bf16[72,1024]{1,0:T(8,128)(2,1)S(1)}, u32[]{:S(2)}, u32[]{:S(2)}) collective-permute-start(bf16[72,1024]{1,0:T(8,128)(2,1)} %get-tuple-element.41), channel_id=1, source_target_pairs={{1,0},{0,1},{3,2},{2,3},{5,4},{4,5},{7,6},{6,7},{9,8},{8,9},{11,10... | collective-permute-start | bytes 442376 | tf_op jit(solution)/shard_map/ppermute | solution.py:313
  6.5 10.3 %collective-permute-start.7 = (bf16[72,1024]{1,0:T(8,128)(2,1)}, bf16[72,1024]{1,0:T(8,128)(2,1)S(1)}, u32[]{:S(2)}, u32[]{:S(2)}) collective-permute-start(bf16[72,1024]{1,0:T(8,128)(2,1)} %get-tuple-element.41), channel_id=1, source_target_pairs={{8,0},{16,8},{24,16},{0,24},{9,1},{17,9},{25,17},{1,25},{10,2},{18... | collective-permute-start | bytes 442376 | tf_op jit(solution)/shard_map/ppermute | solution.py:318
  10.6 0.7 %copy-start.1 = (f32[16]{0:T(128)S(1)}, f32[16]{0:T(128)}, u32[]{:S(2)}) copy-start(f32[16]{0:T(128)} %param.4) | copy-start | bytes 196
  11.2 0.7 %copy-start.2 = (f32[65]{0:T(128)S(1)}, f32[65]{0:T(128)}, u32[]{:S(2)}) copy-start(f32[65]{0:T(128)} %param.5) | copy-start | bytes 784
  13.6 3.1 %collective-permute-start.4 = (bf16[72,1024]{1,0:T(8,128)(2,1)S(1)}, bf16[72,1024]{1,0:T(8,128)(2,1)S(1)}, u32[]{:S(2)}, u32[]{:S(2)}) collective-permute-start(bf16[72,1024]{1,0:T(8,128)(2,1)S(1)} %collective-permute-done.1.refs_2_), channel_id=1, source_target_pairs={{1,0},{0,1},{3,2},{2,3},{5,4},{4,5},{7,6},{6,7},{9,8},{8,9},{11,10... | collective-permute-start | bytes 442376 | tf_op jit(solution)/shard_map/ppermute | solution.py:313
  13.6 3.1 %collective-permute-start.5 = (bf16[72,1024]{1,0:T(8,128)(2,1)S(1)}, bf16[72,1024]{1,0:T(8,128)(2,1)S(1)}, u32[]{:S(2)}, u32[]{:S(2)}) collective-permute-start(bf16[72,1024]{1,0:T(8,128)(2,1)S(1)} %collective-permute-done.2.refs_4_), channel_id=1, source_target_pairs={{1,0},{0,1},{3,2},{2,3},{5,4},{4,5},{7,6},{6,7},{9,8},{8,9},{11,10... | collective-permute-start | bytes 442376 | tf_op jit(solution)/shard_map/ppermute | solution.py:313
  14.1 2.6 %collective-permute-start.6 = (bf16[72,1024]{1,0:T(8,128)(2,1)S(1)}, bf16[72,1024]{1,0:T(8,128)(2,1)S(1)}, u32[]{:S(2)}, u32[]{:S(2)}) collective-permute-start(bf16[72,1024]{1,0:T(8,128)(2,1)S(1)} %collective-permute-done.3.refs_6_), channel_id=1, source_target_pairs={{1,0},{0,1},{3,2},{2,3},{5,4},{4,5},{7,6},{6,7},{9,8},{8,9},{11,10... | collective-permute-start | bytes 442376 | tf_op jit(solution)/shard_map/ppermute | solution.py:313
  14.2 10.5 %collective-permute-start.8 = (bf16[72,1024]{1,0:T(8,128)(2,1)}, bf16[72,1024]{1,0:T(8,128)(2,1)S(1)}, u32[]{:S(2)}, u32[]{:S(2)}) collective-permute-start(bf16[72,1024]{1,0:T(8,128)(2,1)} %get-tuple-element.41), channel_id=1, source_target_pairs={{16,0},{24,8},{0,16},{8,24},{17,1},{25,9},{1,17},{9,25},{18,2},{26... | collective-permute-start | bytes 442376 | tf_op jit(solution)/shard_map/ppermute | solution.py:318
  16.8 0.9 %copy-start = (bf16[72,1024]{1,0:T(8,128)(2,1)S(1)}, bf16[72,1024]{1,0:T(8,128)(2,1)}, u32[]{:S(2)}) copy-start(bf16[72,1024]{1,0:T(8,128)(2,1)} %get-tuple-element.40.refs_0_) | copy-start | bytes 442372
  24.7 10.9 %collective-permute-start.10 = (bf16[72,1024]{1,0:T(8,128)(2,1)S(1)}, bf16[72,1024]{1,0:T(8,128)(2,1)S(1)}, u32[]{:S(2)}, u32[]{:S(2)}) collective-permute-start(bf16[72,1024]{1,0:T(8,128)(2,1)S(1)} %collective-permute-done.7.refs_0_), channel_id=1, source_target_pairs={{4,0},{5,1},{6,2},{7,3},{0,4},{1,5},{2,6},{3,7},{12,8},{13,9},{14,... | collective-permute-start | bytes 442376 | tf_op jit(solution)/shard_map/ppermute | solution.py:313
  26.3 9.4 %collective-permute-start.11 = (bf16[72,1024]{1,0:T(8,128)(2,1)S(1)}, bf16[72,1024]{1,0:T(8,128)(2,1)S(1)}, u32[]{:S(2)}, u32[]{:S(2)}) collective-permute-start(bf16[72,1024]{1,0:T(8,128)(2,1)S(1)} %collective-permute-done.7.refs_0_), channel_id=1, source_target_pairs={{6,0},{7,1},{4,2},{5,3},{2,4},{3,5},{0,6},{1,7},{14,8},{15,9},{12,... | collective-permute-start | bytes 442376 | tf_op jit(solution)/shard_map/ppermute | solution.py:313
  27.5 8.2 %collective-permute-start.9 = (bf16[72,1024]{1,0:T(8,128)(2,1)S(1)}, bf16[72,1024]{1,0:T(8,128)(2,1)S(1)}, u32[]{:S(2)}, u32[]{:S(2)}) collective-permute-start(bf16[72,1024]{1,0:T(8,128)(2,1)S(1)} %collective-permute-done.7.refs_0_), channel_id=1, source_target_pairs={{2,0},{3,1},{0,2},{1,3},{6,4},{7,5},{4,6},{5,7},{10,8},{11,9},{8,1... | collective-permute-start | bytes 442376 | tf_op jit(solution)/shard_map/ppermute | solution.py:313
  35.6 2.3 %collective-permute-start.12 = (bf16[72,1024]{1,0:T(8,128)(2,1)S(1)}, bf16[72,1024]{1,0:T(8,128)(2,1)S(1)}, u32[]{:S(2)}, u32[]{:S(2)}) collective-permute-start(bf16[72,1024]{1,0:T(8,128)(2,1)S(1)} %collective-permute-done.7.refs_0_), channel_id=1, source_target_pairs={{1,0},{0,1},{3,2},{2,3},{5,4},{4,5},{7,6},{6,7},{9,8},{8,9},{11,10... | collective-permute-start | bytes 442376 | tf_op jit(solution)/shard_map/ppermute | solution.py:313
  35.7 3.2 %collective-permute-start.13 = (bf16[72,1024]{1,0:T(8,128)(2,1)S(1)}, bf16[72,1024]{1,0:T(8,128)(2,1)S(1)}, u32[]{:S(2)}, u32[]{:S(2)}) collective-permute-start(bf16[72,1024]{1,0:T(8,128)(2,1)S(1)} %collective-permute-done.9.refs_2_), channel_id=1, source_target_pairs={{1,0},{0,1},{3,2},{2,3},{5,4},{4,5},{7,6},{6,7},{9,8},{8,9},{11,10... | collective-permute-start | bytes 442376 | tf_op jit(solution)/shard_map/ppermute | solution.py:313
  36.2 4.0 %collective-permute-start.14 = (bf16[72,1024]{1,0:T(8,128)(2,1)S(1)}, bf16[72,1024]{1,0:T(8,128)(2,1)S(1)}, u32[]{:S(2)}, u32[]{:S(2)}) collective-permute-start(bf16[72,1024]{1,0:T(8,128)(2,1)S(1)} %collective-permute-done.10.refs_4_), channel_id=1, source_target_pairs={{1,0},{0,1},{3,2},{2,3},{5,4},{4,5},{7,6},{6,7},{9,8},{8,9},{11,10... | collective-permute-start | bytes 442376 | tf_op jit(solution)/shard_map/ppermute | solution.py:313
  36.3 3.9 %collective-permute-start.15 = (bf16[72,1024]{1,0:T(8,128)(2,1)S(1)}, bf16[72,1024]{1,0:T(8,128)(2,1)S(1)}, u32[]{:S(2)}, u32[]{:S(2)}) collective-permute-start(bf16[72,1024]{1,0:T(8,128)(2,1)S(1)} %collective-permute-done.11.refs_6_), channel_id=1, source_target_pairs={{1,0},{0,1},{3,2},{2,3},{5,4},{4,5},{7,6},{6,7},{9,8},{8,9},{11,10... | collective-permute-start | bytes 442376 | tf_op jit(solution)/shard_map/ppermute | solution.py:313
  36.7 14.2 %collective-permute-start.16 = (bf16[72,1024]{1,0:T(8,128)(2,1)S(1)}, bf16[72,1024]{1,0:T(8,128)(2,1)S(1)}, u32[]{:S(2)}, u32[]{:S(2)}) collective-permute-start(bf16[72,1024]{1,0:T(8,128)(2,1)S(1)} %collective-permute-done.8.refs_0_), channel_id=1, source_target_pairs={{2,0},{3,1},{0,2},{1,3},{6,4},{7,5},{4,6},{5,7},{10,8},{11,9},{8,1... | collective-permute-start | bytes 442376 | tf_op jit(solution)/shard_map/ppermute | solution.py:313
  38.0 12.9 %collective-permute-start.17 = (bf16[72,1024]{1,0:T(8,128)(2,1)S(1)}, bf16[72,1024]{1,0:T(8,128)(2,1)S(1)}, u32[]{:S(2)}, u32[]{:S(2)}) collective-permute-start(bf16[72,1024]{1,0:T(8,128)(2,1)S(1)} %collective-permute-done.8.refs_0_), channel_id=1, source_target_pairs={{4,0},{5,1},{6,2},{7,3},{0,4},{1,5},{2,6},{3,7},{12,8},{13,9},{14,... | collective-permute-start | bytes 442376 | tf_op jit(solution)/shard_map/ppermute | solution.py:313
  38.9 12.0 %collective-permute-start.18 = (bf16[72,1024]{1,0:T(8,128)(2,1)S(1)}, bf16[72,1024]{1,0:T(8,128)(2,1)S(1)}, u32[]{:S(2)}, u32[]{:S(2)}) collective-permute-start(bf16[72,1024]{1,0:T(8,128)(2,1)S(1)} %collective-permute-done.8.refs_0_), channel_id=1, source_target_pairs={{6,0},{7,1},{4,2},{5,3},{2,4},{3,5},{0,6},{1,7},{14,8},{15,9},{12,... | collective-permute-start | bytes 442376 | tf_op jit(solution)/shard_map/ppermute | solution.py:313
  50.9 1.4 %collective-permute-start.19 = (bf16[72,1024]{1,0:T(8,128)(2,1)S(1)}, bf16[72,1024]{1,0:T(8,128)(2,1)S(1)}, u32[]{:S(2)}, u32[]{:S(2)}) collective-permute-start(bf16[72,1024]{1,0:T(8,128)(2,1)S(1)} %collective-permute-done.8.refs_0_), channel_id=1, source_target_pairs={{1,0},{0,1},{3,2},{2,3},{5,4},{4,5},{7,6},{6,7},{9,8},{8,9},{11,10... | collective-permute-start | bytes 442376 | tf_op jit(solution)/shard_map/ppermute | solution.py:313
  51.0 1.6 %collective-permute-start.20 = (bf16[72,1024]{1,0:T(8,128)(2,1)S(1)}, bf16[72,1024]{1,0:T(8,128)(2,1)S(1)}, u32[]{:S(2)}, u32[]{:S(2)}) collective-permute-start(bf16[72,1024]{1,0:T(8,128)(2,1)S(1)} %collective-permute-done.16.refs_2_), channel_id=1, source_target_pairs={{1,0},{0,1},{3,2},{2,3},{5,4},{4,5},{7,6},{6,7},{9,8},{8,9},{11,10... | collective-permute-start | bytes 442376 | tf_op jit(solution)/shard_map/ppermute | solution.py:313
  51.5 1.4 %collective-permute-start.21 = (bf16[72,1024]{1,0:T(8,128)(2,1)S(1)}, bf16[72,1024]{1,0:T(8,128)(2,1)S(1)}, u32[]{:S(2)}, u32[]{:S(2)}) collective-permute-start(bf16[72,1024]{1,0:T(8,128)(2,1)S(1)} %collective-permute-done.17.refs_4_), channel_id=1, source_target_pairs={{1,0},{0,1},{3,2},{2,3},{5,4},{4,5},{7,6},{6,7},{9,8},{8,9},{11,10... | collective-permute-start | bytes 442376 | tf_op jit(solution)/shard_map/ppermute | solution.py:313
  51.6 1.5 %collective-permute-start.22 = (bf16[72,1024]{1,0:T(8,128)(2,1)S(1)}, bf16[72,1024]{1,0:T(8,128)(2,1)S(1)}, u32[]{:S(2)}, u32[]{:S(2)}) collective-permute-start(bf16[72,1024]{1,0:T(8,128)(2,1)S(1)} %collective-permute-done.18.refs_6_), channel_id=1, source_target_pairs={{1,0},{0,1},{3,2},{2,3},{5,4},{4,5},{7,6},{6,7},{9,8},{8,9},{11,10... | collective-permute-start | bytes 442376 | tf_op jit(solution)/shard_map/ppermute | solution.py:313

commit v3 on v2

--- a/solution.py
+++ b/solution.py
@@ -10,6 +10,7 @@
 
 NLAG = 512
 SUB = 8
+PITCH = SUB + 1
 LANES = 128
 F32 = jnp.float32
 BF16 = jnp.bfloat16
@@ -37,6 +38,8 @@
         self.half = self.total // 2
         self.depth = ceil_to(self.half + SUB, 16)
         self.deep = self.windows * self.depth
+        self.even = self.deep // (2 * LANES) * 2 * LANES
+        self.full = 2 * self.deep - self.even
         self.lags = NLAG // lag_total
         self.shifts = self.lags // 2 // SUB
         self.held = lag_total * self.slot
@@ -49,7 +52,7 @@
     return taps[0:1, index : index + 1].astype(BF16).astype(F32)
 
 
-def local_kernel(plan, taps_ref, raw_ref, sent_ref, kept_ref, spread):
+def local_kernel(plan, taps_ref, raw_ref, out_ref, spread):
     row = lax.broadcasted_iota(jnp.int32, (plan.rows, plan.raw), 0)
     time = lax.broadcasted_iota(jnp.int32, (plan.rows, plan.raw), 1)
     tap = 2 * (row + plan.head) - time
@@ -63,25 +66,27 @@
     picked = jnp.where(is_last & last | is_first & first, 1.0, 0.0)
     table = jnp.where(row < plan.whole, table, picked).astype(BF16)
     spread[...] = raw_ref[...].astype(F32).reshape(plan.raw * plan.windows, plan.channels)
-    for w in range(plan.windows):
-        series = spread[pl.ds(w, plan.raw, stride=plan.windows), :].astype(BF16)
-        rows = jnp.dot(table, series, preferred_element_type=F32).astype(BF16)
-        for ref in (sent_ref, kept_ref):
-            ref[:, w * plan.channels : (w + 1) * plan.channels] = rows
+    series = [
+        spread[pl.ds(w, plan.raw, stride=plan.windows), :].astype(BF16) for w in range(plan.windows)
+    ]
+    out_ref[...] = jnp.dot(
+        table, jnp.concatenate(series, axis=1), preferred_element_type=F32
+    ).astype(BF16)
 
 
 def local_rows(plan, raw, taps):
     return pl.pallas_call(
         functools.partial(local_kernel, plan),
-        out_shape=[jax.ShapeDtypeStruct((plan.rows, plan.wide), BF16)] * 2,
+        out_shape=jax.ShapeDtypeStruct((plan.rows, plan.wide), BF16),
         in_specs=[VMEM, VMEM],
-        out_specs=[VMEM, VMEM],
+        out_specs=VMEM,
         scratch_shapes=[pltpu.VMEM((plan.raw * plan.windows, plan.channels), F32)],
         name="local_rows",
     )(taps, jnp.transpose(raw, (2, 0, 1)))
 
 
-def table_kernel(plan, dec_ref, bp_ref, even_ref, odd_ref, edge_ref):
+def table_kernel(plan, dec_ref, bp_ref, piece_ref, band_ref, edge_ref, kept_ref):
+    kept_ref[...] = piece_ref[...]
     span = ceil_to(plan.total + plan.bp_taps, LANES)
     lane = lax.broadcasted_iota(jnp.int32, (1, span), 1)
     base = jnp.zeros((1, span), F32)
@@ -96,10 +101,10 @@
         start = col - plan.held - p * plan.head
         at = jnp.where((start >= 0) & (start < plan.head), start + p * plan.dec, at)
     order = jnp.where(time == at, 1.0, 0.0).astype(BF16)
-    for parity, ref in ((0, even_ref), (1, odd_ref)):
+    for parity in range(2):
         spread = jnp.broadcast_to(base, (plan.half, span))
         taps = pltpu.roll(spread, parity, 1, stride=2, stride_axis=0)
-        ref[...] = jnp.dot(taps.astype(BF16), order, preferred_element_type=F32).astype(BF16)
+        band_ref[parity * plan.half : (parity + 1) * plan.half, :] = jnp.dot(taps.astype(BF16), order, preferred_element_type=F32).astype(BF16)
     rows = plan.joined - plan.held
     row = lax.broadcasted_iota(jnp.int32, (rows, plan.held), 0)
     col = lax.broadcasted_iota(jnp.int32, (rows, plan.held), 1)
@@ -117,20 +122,20 @@
     edge_ref[...] = table.astype(BF16)
 
 
-def tables(plan, dec_taps, bp_taps):
+def tables(plan, dec_taps, bp_taps, piece):
     return pl.pallas_call(
         functools.partial(table_kernel, plan),
         out_shape=(
-            jax.ShapeDtypeStruct((plan.half, plan.joined), BF16),
-            jax.ShapeDtypeStruct((plan.half, plan.joined), BF16),
+            jax.ShapeDtypeStruct((2 * plan.half, plan.joined), BF16),
             jax.ShapeDtypeStruct((plan.joined - plan.held, plan.held), BF16),
+            jax.ShapeDtypeStruct(piece.shape, piece.dtype),
         ),
-        in_specs=[VMEM, VMEM],
+        in_specs=[VMEM, VMEM, VMEM],
         out_specs=(VMEM, VMEM, VMEM),
-        compiler_params=pltpu.CompilerParams(vmem_limit_bytes=20 * 2**20),
+        compiler_params=pltpu.CompilerParams(vmem_limit_bytes=12 * 2**20),
         cost_estimate=pl.CostEstimate(flops=500_000_000, bytes_accessed=2_000_000, transcendentals=0),
         name="tables",
-    )(dec_taps, bp_taps)
+    )(dec_taps, bp_taps, piece)
 
 
 def make_series(plan, place_ref, pieces, tables_refs, held, even, odd, ahead, right):
@@ -138,29 +143,32 @@
     if plan.slot > plan.rows:
         for p in range(plan.lag_total):
             held[(p + 1) * plan.slot - 16 : (p + 1) * plan.slot, :] = jnp.zeros((16, plan.wide), BF16)
-    for p in range(plan.lag_total):
-        at = pl.multiple_of(lax.bitwise_xor(place, p) * plan.slot, 16)
-        held[pl.ds(at, plan.rows), :] = pieces[p][...]
-    filter_block(plan, tables_refs, held, even, odd, ahead)
-    lay_right(plan, place, even, odd, ahead, right)
-
-
-def filter_block(plan, tables_refs, held, even, odd, ahead):
-    even_ref, odd_ref, edge_ref = tables_refs
-    held[plan.held : plan.joined, :] = jnp.dot(
-        edge_ref[...], held[0 : plan.held, :], preferred_element_type=F32
-    ).astype(BF16)
+    places = [
+        pl.ds(pl.multiple_of(lax.bitwise_xor(place, p) * plan.slot, 16), plan.rows)
+        for p in range(plan.lag_total)
+    ]
+    for p, piece in enumerate(pieces):
+        held[places[p], :] = piece[...]
     for ref in (even, odd, ahead):
         ref[0 : plan.pad, :] = jnp.zeros((plan.pad, plan.wide), F32)
         ref[plan.pad + plan.half - SUB :, :] = jnp.zeros(
             (plan.padded - plan.pad - plan.half + SUB, plan.wide), F32
         )
+    filter_block(plan, tables_refs, held, even, odd, ahead)
+    lay_right(plan, place, even, odd, ahead, right)
+
+
+def filter_block(plan, tables_refs, held, even, odd, ahead):
+    band_ref, edge_ref = tables_refs
+    held[plan.held : plan.joined, :] = jnp.dot(
+        edge_ref[...], held[0 : plan.held, :], preferred_element_type=F32
+    ).astype(BF16)
     step = 2 * LANES
     for c in range(0, plan.wide, step):
         cols = slice(c, c + step)
         block = held[:, cols]
-        a = jnp.dot(even_ref[...], block, preferred_element_type=F32)
-        b = jnp.dot(odd_ref[...], block, preferred_element_type=F32)
+        both = jnp.dot(band_ref[...], block, preferred_element_type=F32)
+        a, b = both[0 : plan.half], both[plan.half :]
         power = jnp.sum(a * a + b * b, axis=0, keepdims=True) * (1.0 / plan.total)
         scale = lax.rsqrt(power + 1e-06)
         a = (a * scale).astype(BF16).astype(F32)
@@ -175,13 +183,23 @@
     for w in range(plan.windows):
         cols = slice(w * plan.channels, (w + 1) * plan.channels)
         rows = slice(w * plan.depth, (w + 1) * plan.depth)
-        for s in range(plan.shifts):
-            at = pl.ds(pl.multiple_of(base + s * SUB, SUB), plan.depth)
+        for first in range(2):
+            shifts = range(first, plan.shifts, 2)
+            height = plan.depth + 2 * SUB * (len(shifts) - 1)
+            at = pl.ds(pl.multiple_of(base + first * SUB, SUB), height)
             a, b, c = even[at, cols], odd[at, cols], ahead[at, cols]
-            to = slice(s * plan.channels, (s + 1) * plan.channels)
-            right[0, rows, to] = b.astype(BF16)
-            right[1, rows, to] = (a - b).astype(BF16)
-            right[2, rows, to] = (c - b).astype(BF16)
+            for k, value in enumerate((b, a - b, c - b)):
+                value = value.astype(BF16)
+                for n, s in enumerate(shifts):
+                    to = slice(s * plan.channels, (s + 1) * plan.channels)
+                    part = value[2 * SUB * n : 2 * SUB * n + plan.depth]
+                    over = max(0, rows.stop - max(rows.start, plan.even)) if k == 0 else 0
+                    if over < plan.depth:
+                        right[k, rows.start : rows.stop - over, to] = part[: plan.depth - over]
+                    if over:
+                        first_over = rows.stop - over - plan.even + plan.deep
+                        for other in (1, 2):
+                            right[other, first_over : first_over + over, to] = part[plan.depth - over :]
 
 
 def make_left(plan, even, odd, stacks, mixes, left):
@@ -192,15 +210,26 @@
                 plan.pad : plan.pad + plan.depth, w * plan.channels : (w + 1) * plan.channels
             ]
     for n, c in enumerate(range(0, plan.deep, LANES)):
-        mixed = mixes[n % 2]
+        mixed = mixes[n % len(mixes)]
         for delay in range(SUB):
             rows = slice(SUB - delay + c, SUB - delay + c + LANES)
             for e, stack in enumerate(stacks):
-                mixed[e, pl.ds(delay, plan.channels, stride=SUB), :] = stack[rows, :].T
+                mixed[e, pl.ds(delay, plan.channels, stride=PITCH), :] = stack[rows, :].T
         for r in range(0, plan.channels * SUB, LANES):
-            a, b = (mixed[e, r : r + LANES, :] for e in range(2))
+            a, b = (
+                jnp.concatenate(
+                    [mixed[e, i * PITCH : i * PITCH + SUB, :] for i in range(r // SUB, (r + LANES) // SUB)], axis=0
+                )
+                for e in range(2)
+            )
             for k, value in enumerate((a + b, a, b)):
-                left[k, r : r + LANES, c : c + LANES] = value.astype(BF16)
+                value = value.astype(BF16)
+                if k > 0 or c < plan.even:
+                    left[k, r : r + LANES, c : c + LANES] = value
+                else:
+                    for other in (1, 2):
+                        at = c - plan.even + plan.deep
+                        left[other, r : r + LANES, at : at + LANES] = value
 
 
 def correlate(plan, count, left, right, out_ref):
@@ -210,7 +239,8 @@
         cols = slice(c, c + step)
         rows = pl.ds(pl.multiple_of(pl.program_id(0) * count * SUB, count * SUB), count * SUB)
         both, even, odd = (
-            jnp.dot(left[k, rows, :], right[k, :, cols], preferred_element_type=F32) for k in range(3)
+            jnp.dot(left[k, rows, :deep], right[k, :deep, cols], preferred_element_type=F32)
+            for k, deep in enumerate((plan.even, plan.full, plan.full))
         )
         for parity, value in ((0, even), (1, odd)):
             value = (both + value) * factor
@@ -224,8 +254,8 @@
 
 def own_kernel(plan, place_ref, *refs):
     n = plan.lag_total
-    pieces, tabs, (left_ref, right_ref) = refs[:n], refs[n : n + 3], refs[n + 3 : n + 5]
-    held, even, odd, ahead, *rest = refs[n + 5 :]
+    pieces, tabs, (left_ref, right_ref) = refs[:n], refs[n : n + 2], refs[n + 2 : n + 4]
+    held, even, odd, ahead, *rest = refs[n + 4 :]
     make_series(plan, place_ref, pieces, tabs, held, even, odd, ahead, right_ref)
     make_left(plan, even, odd, rest[:2], rest[2:], left_ref)
 
@@ -236,8 +266,8 @@
 
 def other_kernel(plan, count, place_ref, *refs):
     n = plan.lag_total
-    pieces, tabs, left_ref, out_ref = refs[:n], refs[n : n + 3], refs[n + 3], refs[n + 5]
-    held, even, odd, ahead, right = refs[n + 6 :]
+    pieces, tabs, left_ref, out_ref = refs[:n], refs[n : n + 2], refs[n + 2], refs[n + 4]
+    held, even, odd, ahead, right = refs[n + 5 :]
 
     @pl.when(pl.program_id(0) == 0)
     def _():
@@ -254,14 +284,14 @@
     return pl.pallas_call(
         functools.partial(own_kernel, plan),
         out_shape=(
-            jax.ShapeDtypeStruct((3, plan.channels * SUB, plan.deep), BF16),
-            jax.ShapeDtypeStruct((3, plan.deep, plan.shifts * plan.channels), BF16),
+            jax.ShapeDtypeStruct((3, plan.channels * SUB, plan.full), BF16),
+            jax.ShapeDtypeStruct((3, plan.full, plan.shifts * plan.channels), BF16),
         ),
-        in_specs=[SMEM] + [VMEM] * (plan.lag_total + 3),
+        in_specs=[SMEM] + [VMEM] * (plan.lag_total + 2),
         out_specs=(VMEM, VMEM),
         scratch_shapes=series_scratch(plan)
         + [pltpu.VMEM((SUB + plan.deep, plan.channels), F32)] * 2
-        + [pltpu.VMEM((2, plan.channels * SUB, LANES), F32)] * 2,
+        + [pltpu.VMEM((2, plan.channels * PITCH, LANES), F32)],
         compiler_params=pltpu.CompilerParams(vmem_limit_bytes=33 * 2**20),
         cost_estimate=pl.CostEstimate(flops=100_000_000, bytes_accessed=2**18, transcendentals=0),
         name="prepare_own",
@@ -292,7 +322,7 @@
 
 def other_correlation(plan, count, pairs, distance, place, pieces, tabs, left, out):
     out_shape, out_spec, cost = correlation_parts(plan, count, pairs, distance)
-    in_specs = [SMEM] + [VMEM] * (plan.lag_total + 4) + [pl.BlockSpec(memory_space=pl.ANY)]
+    in_specs = [SMEM] + [VMEM] * (plan.lag_total + 3) + [pl.BlockSpec(memory_space=pl.ANY)]
     return pl.pallas_call(
         functools.partial(other_kernel, plan, count),
         grid=(plan.channels // count,),
@@ -300,7 +330,7 @@
         in_specs=in_specs,
         out_specs=out_spec,
         scratch_shapes=series_scratch(plan)
-        + [pltpu.VMEM((3, plan.deep, plan.shifts * plan.channels), BF16)],
+        + [pltpu.VMEM((3, plan.full, plan.shifts * plan.channels), BF16)],
         input_output_aliases={len(in_specs) - 1: 0},
         compiler_params=pltpu.CompilerParams(vmem_limit_bytes=30 * 2**20),
         cost_estimate=cost,
@@ -318,9 +348,8 @@
     return lax.ppermute(piece, "chan", [((i + distance) % count, i) for i in range(count)])
 
 
-def same_core(piece, start=None, stop=None):
-    masks = list(range(0, lax.axis_size("lag"), 2))[start:stop]
-    return [swap(piece, mask) if mask else piece for mask in masks]
+def same_core(piece):
+    return [swap(piece, mask) if mask else piece for mask in range(0, lax.axis_size("lag"), 2)]
 
 
 def both_cores(held):
@@ -332,23 +361,23 @@
     pairs = lax.axis_size("chan") // 2 + 1
     place = lax.axis_index("lag").astype(jnp.int32).reshape(1)
     dec_taps = decimation_taps.reshape(1, -1)
-    piece, kept = local_rows(plan, raw_samples, dec_taps)
-    tabs = tables(plan, dec_taps, bandpass_taps.reshape(1, -1))
+    piece = local_rows(plan, raw_samples, dec_taps)
+    *tabs, kept = tables(plan, dec_taps, bandpass_taps.reshape(1, -1), piece)
     count = 32
     own = same_core(piece)
-    far = [from_ahead(piece, distance) for distance in range(1, pairs)]
+    near = from_ahead(piece, 1)
     tabs, own[1:] = lax.optimization_barrier((tabs, own[1:]))
-    pieces, far[0] = lax.optimization_barrier((both_cores(own), far[0]))
+    pieces, near = lax.optimization_barrier((both_cores(own), near))
     left, right = prepare_own(plan, place, [kept, *pieces[1:]], tabs)
-    left, far = lax.optimization_barrier((left, far))
-    held = same_core(far[0])
-    early = same_core(far[1], stop=-1) if pairs > 2 else None
+    left, near, piece = lax.optimization_barrier((left, near, piece))
+    held = same_core(near)
+    far = {distance: from_ahead(piece, distance) for distance in range(2, pairs)}
     out = own_correlation(plan, count, pairs, left, right)
     for distance in range(1, pairs):
         out, held, far = lax.optimization_barrier((out, held, far))
         pieces = both_cores(held)
         if distance + 1 < pairs:
-            held = early + same_core(far[distance], start=-1) if distance == 1 else same_core(far[distance])
+            held = same_core(far[distance + 1])
         out = other_correlation(plan, count, pairs, distance, place, pieces, tabs, left, out)
     return out
 

time: 63.9 us -> 61.2 us (0.958)
  Pallas kernels: 38.6 us -> 35.4 us
    pallas_call x2, Pallas kernels: 21.4 us -> 19.8 us  [other_correlation(): pl.pallas_call(functools.partial(other_kernel, plan, count), grid=(plan.c...]
    pallas_call x1, Pallas kernels: 7 us -> 5.65 us  [prepare_own(): pl.pallas_call(functools.partial(own_kernel, plan), out_shape=(jax.ShapeD...]
  transfers between devices with their start and end apart: 23 -> 23, of which waited for: 5 -> 8; matrix products, arithmetic and copies ran while one was open for 0% -> 0% of each run, Pallas kernels for 41% -> 29%
where the time goes in v3:
time: 61.2 us; the launch traced here: 61 us
  Pallas kernels  35.4 us (58%)
  starting transfers between devices  20.8 us (34%)
  waiting for transfers between devices  2.51 us (4%)
  local copies, waits for them, and re-layouts  2.25 us (4%)
    pallas_call x2, Pallas kernels, other_correlation(): pl.pallas_call(functools.partial(other_kernel, plan, count), grid=(plan.c...  19.8 us
    ppermute x21, starting transfers between devices, swap(): return lax.ppermute(piece, 'lag', [(i ^ mask, i) for i in range(count)])  14.7 us
    pallas_call x1, Pallas kernels, own_correlation(): pl.pallas_call(functools.partial(first_kernel, plan, count), grid=(plan.c...  7.12 us
    ppermute x2, starting transfers between devices, from_ahead(): lax.ppermute(piece, 'chan', [((i + distance) % count, i) for i in range(c...  6.1 us
    pallas_call x1, Pallas kernels, prepare_own(): pl.pallas_call(functools.partial(own_kernel, plan), out_shape=(jax.ShapeD...  5.65 us
    unnamed x6, local copies, waits for them, and re-layouts  2.25 us
    ppermute x21, waiting for transfers between devices, swap(): return lax.ppermute(piece, 'lag', [(i ^ mask, i) for i in range(count)])  2.17 us
    pallas_call x1, Pallas kernels, local_rows(): pl.pallas_call(functools.partial(local_kernel, plan), out_shape=jax.Shape...  1.92 us
  transfers between devices with their start and end apart: 23, of which 8 were waited for; matrix products, arithmetic and copies ran while one was open for 0% of the time, Pallas kernels for 29%

profile of v3, /device:TPU:0, one launch (start us, length us, event | category | flops | bytes accessed | tf_op | source)
XLA Modules:
  0.0 61.0 jit_solution(14654101752247355428)
XLA Ops:
  0.0 1.9 %local_rows.1.piece_ref = bf16[72,1024]{1,0:T(8,128)(2,1)} custom-call(f32[1,16]{1,0:T(1,128)} %bitcast.4, bf16[100,8,128]{2,1,0:T(8,128)(2,1)} %bitcast.7), custom_call_target="tpu_custom_call" | custom-call | tf_op jit(solution)/shard_map/local_rows/pallas_call | solution.py:78
  1.9 3.9 %collective-permute-start.3 = (bf16[72,1024]{1,0:T(8,128)(2,1)}, bf16[72,1024]{1,0:T(8,128)(2,1)S(1)}, u32[]{:S(2)}, u32[]{:S(2)}) collective-permute-start(bf16[72,1024]{1,0:T(8,128)(2,1)} %local_rows.1.piece_ref), channel_id=1, source_target_pairs={{6,0},{7,1},{4,2},{5,3},{2,4},{3,5},{0,6},{1,7},{14,8},{15,9},{12,... | collective-permute-start | bytes 442376 | tf_op jit(solution)/shard_map/ppermute | solution.py:343
  5.8 0.5 collective-permute-start.2
  6.4 4.1 %collective-permute-start.7 = (bf16[72,1024]{1,0:T(8,128)(2,1)}, bf16[72,1024]{1,0:T(8,128)(2,1)S(1)}, u32[]{:S(2)}, u32[]{:S(2)}) collective-permute-start(bf16[72,1024]{1,0:T(8,128)(2,1)} %local_rows.1.piece_ref), channel_id=1, source_target_pairs={{8,0},{16,8},{24,16},{0,24},{9,1},{17,9},{25,17},{1,25},{10,2},{18... | collective-permute-start | bytes 442376 | tf_op jit(solution)/shard_map/ppermute | solution.py:348
  10.5 0.9 %copy-done = bf16[72,1024]{1,0:T(8,128)(2,1)S(1)} copy-done((bf16[72,1024]{1,0:T(8,128)(2,1)S(1)}, bf16[72,1024]{1,0:T(8,128)(2,1)}, u32[]{:S(2)}) %copy-start) | copy-done | bytes 147480
  11.4 0.7 %copy-done.1 = f32[16]{0:T(128)S(1)} copy-done((f32[16]{0:T(128)S(1)}, f32[16]{0:T(128)}, u32[]{:S(2)}) %copy-start.1) | copy-done | bytes 88
  12.1 0.7 %copy-done.2 = f32[65]{0:T(128)S(1)} copy-done((f32[65]{0:T(128)S(1)}, f32[65]{0:T(128)}, u32[]{:S(2)}) %copy-start.2) | copy-done | bytes 284
  12.7 0.9 %tables.1 = (bf16[400,704]{1,0:T(8,128)(2,1)S(1)}, bf16[64,640]{1,0:T(8,128)(2,1)S(1)}, bf16[72,1024]{1,0:T(8,128)(2,1)S(1)}) custom-call(f32[1,16]{1,0:T(1,128)S(1)} %bitcast.5, f32[1,65]{1,0:T(1,128)S(1)} %bitcast.6, bf16[72,1024]{1,0:T(8,128)(2,1)S(1)} %copy-done), custom_call_target="tpu_custom_call" | custom-call | flops 500000000 | bytes 2000000 | tf_op jit(solution)/shard_map/tables/pallas_call | solution.py:126
  13.6 0.5 collective-permute-start.4
  14.3 0.4 collective-permute-start.6
  14.7 0.5 collective-permute-done.4.refs_3_
  15.2 0.4 collective-permute-done.5.refs_5_
  15.6 0.2 collective-permute-done.6.refs_7_
  15.8 5.7 %prepare_own.1 = (bf16[3,1024,1792]{2,1,0:T(8,128)(2,1)S(1)}, bf16[3,1792,512]{2,1,0:T(8,128)(2,1)S(1)}) custom-call(s32[1]{0:T(128)} %bitcast.place_ref, bf16[72,1024]{1,0:T(8,128)(2,1)S(1)} %get-tuple-element.37.refs_0_, bf16[72,1024]{1,0:T(8,128)(2,1)S(1)} %collective-permute-done.refs_1_, bf16[72,1024]{1,0:T(8,128)(2,1)S(1)} %collective-permute-done.1.refs_2_, ...), custom_call_target="tpu_custom_call" | custom-call | flops 100000000 | bytes 262144 | tf_op jit(solution)/shard_map/prepare_own/pallas_call | solution.py:284
  21.4 2.5 %collective-permute-start.10 = (bf16[72,1024]{1,0:T(8,128)(2,1)S(1)}, bf16[72,1024]{1,0:T(8,128)(2,1)S(1)}, u32[]{:S(2)}, u32[]{:S(2)}) collective-permute-start(bf16[72,1024]{1,0:T(8,128)(2,1)S(1)} %collective-permute-done.7.refs_0_), channel_id=1, source_target_pairs={{6,0},{7,1},{4,2},{5,3},{2,4},{3,5},{0,6},{1,7},{14,8},{15,9},{12,... | collective-permute-start | bytes 442376 | tf_op jit(solution)/shard_map/ppermute | solution.py:343
  23.9 0.5 collective-permute-start.9
  24.4 0.5 collective-permute-start.8
  25.0 2.0 %collective-permute-start.11 = (bf16[72,1024]{1,0:T(8,128)(2,1)}, bf16[72,1024]{1,0:T(8,128)(2,1)S(1)}, u32[]{:S(2)}, u32[]{:S(2)}) collective-permute-start(bf16[72,1024]{1,0:T(8,128)(2,1)} %local_rows.1.piece_ref), channel_id=1, source_target_pairs={{16,0},{24,8},{0,16},{8,24},{17,1},{25,9},{1,17},{9,25},{18,2},{26... | collective-permute-start | bytes 442376 | tf_op jit(solution)/shard_map/ppermute | solution.py:348
  27.0 7.1 %own_correlation.1.refs_11_ = f32[128,3,64,128]{3,2,1,0:T(8,128)} custom-call(bf16[3,1024,1792]{2,1,0:T(8,128)(2,1)S(1)} %get-tuple-element.54.left_ref.refs_10_, bf16[3,1792,512]{2,1,0:T(8,128)(2,1)S(1)} %get-tuple-element.55.right_ref), custom_call_target="tpu_custom_call" | custom-call | flops 5234491392 | bytes 8388608 | tf_op jit(solution)/shard_map/own_correlation/pallas_call | solution.py:311
  34.1 0.3 collective-permute-done.11.refs_0_
  34.6 0.5 collective-permute-start.13
  35.1 0.4 collective-permute-start.15
  35.6 2.0 %collective-permute-start.18 = (bf16[72,1024]{1,0:T(8,128)(2,1)S(1)}, bf16[72,1024]{1,0:T(8,128)(2,1)S(1)}, u32[]{:S(2)}, u32[]{:S(2)}) collective-permute-start(bf16[72,1024]{1,0:T(8,128)(2,1)S(1)} %collective-permute-done.11.refs_0_), channel_id=1, source_target_pairs={{6,0},{7,1},{4,2},{5,3},{2,4},{3,5},{0,6},{1,7},{14,8},{15,9},{12,... | collective-permute-start | bytes 442376 | tf_op jit(solution)/shard_map/ppermute | solution.py:343
  37.6 0.9 %collective-permute-start.17 = (bf16[72,1024]{1,0:T(8,128)(2,1)S(1)}, bf16[72,1024]{1,0:T(8,128)(2,1)S(1)}, u32[]{:S(2)}, u32[]{:S(2)}) collective-permute-start(bf16[72,1024]{1,0:T(8,128)(2,1)S(1)} %collective-permute-done.11.refs_0_), channel_id=1, source_target_pairs={{4,0},{5,1},{6,2},{7,3},{0,4},{1,5},{2,6},{3,7},{12,8},{13,9},{14,... | collective-permute-start | bytes 442376 | tf_op jit(solution)/shard_map/ppermute | solution.py:343
  38.5 0.5 collective-permute-start.16
  39.1 9.9 %other_correlation.2.refs_11_ = f32[128,3,64,128]{3,2,1,0:T(8,128)} custom-call(s32[1]{0:T(128)} %bitcast.place_ref, bf16[72,1024]{1,0:T(8,128)(2,1)S(1)} %collective-permute-done.7.refs_0_, bf16[72,1024]{1,0:T(8,128)(2,1)S(1)} %collective-permute-done.12.refs_1_, ...), custom_call_target="tpu_custom_call", output_to_operand_aliasing={{}: (12, {})} | custom-call | flops 5234491392 | bytes 8388608 | tf_op jit(solution)/shard_map/other_correlation/pallas_call | solution.py:326
  49.0 0.5 collective-permute-start.20
  49.6 0.4 collective-permute-start.22
  50.1 0.3 collective-permute-done.19.refs_1_
  50.4 0.2 collective-permute-done.20.refs_3_
  50.6 0.3 collective-permute-done.21.refs_5_
  51.1 9.9 %other_correlation.3 = f32[128,3,64,128]{3,2,1,0:T(8,128)} custom-call(s32[1]{0:T(128)} %bitcast.place_ref, bf16[72,1024]{1,0:T(8,128)(2,1)S(1)} %collective-permute-done.11.refs_0_, bf16[72,1024]{1,0:T(8,128)(2,1)S(1)} %collective-permute-done.19.refs_1_, bf16[72,1024]{1,0:T(8,128)(2,1)S(1)} %collective-permute-done.16.refs_2_, ...), custom_call_target="tpu_custom_call", output_to_operand_aliasing={{}: (12, {})} | custom-call | flops 5234491392 | bytes 8388608 | tf_op jit(solution)/shard_map/other_correlation/pallas_call | solution.py:326
  (26 shorter events, 0.7 us)
Async XLA Ops:
  1.9 11.7 %collective-permute-start.3 = (bf16[72,1024]{1,0:T(8,128)(2,1)}, bf16[72,1024]{1,0:T(8,128)(2,1)S(1)}, u32[]{:S(2)}, u32[]{:S(2)}) collective-permute-start(bf16[72,1024]{1,0:T(8,128)(2,1)} %local_rows.1.piece_ref), channel_id=1, source_target_pairs={{6,0},{7,1},{4,2},{5,3},{2,4},{3,5},{0,6},{1,7},{14,8},{15,9},{12,... | collective-permute-start | bytes 442376 | tf_op jit(solution)/shard_map/ppermute | solution.py:343
  5.8 7.8 %collective-permute-start.2 = (bf16[72,1024]{1,0:T(8,128)(2,1)}, bf16[72,1024]{1,0:T(8,128)(2,1)S(1)}, u32[]{:S(2)}, u32[]{:S(2)}) collective-permute-start(bf16[72,1024]{1,0:T(8,128)(2,1)} %local_rows.1.piece_ref), channel_id=1, source_target_pairs={{4,0},{5,1},{6,2},{7,3},{0,4},{1,5},{2,6},{3,7},{12,8},{13,9},{14,... | collective-permute-start | bytes 442376 | tf_op jit(solution)/shard_map/ppermute | solution.py:343
  6.3 7.3 %collective-permute-start.1 = (bf16[72,1024]{1,0:T(8,128)(2,1)}, bf16[72,1024]{1,0:T(8,128)(2,1)S(1)}, u32[]{:S(2)}, u32[]{:S(2)}) collective-permute-start(bf16[72,1024]{1,0:T(8,128)(2,1)} %local_rows.1.piece_ref), channel_id=1, source_target_pairs={{2,0},{3,1},{0,2},{1,3},{6,4},{7,5},{4,6},{5,7},{10,8},{11,9},{8,1... | collective-permute-start | bytes 442376 | tf_op jit(solution)/shard_map/ppermute | solution.py:343
  6.4 8.3 %collective-permute-start.7 = (bf16[72,1024]{1,0:T(8,128)(2,1)}, bf16[72,1024]{1,0:T(8,128)(2,1)S(1)}, u32[]{:S(2)}, u32[]{:S(2)}) collective-permute-start(bf16[72,1024]{1,0:T(8,128)(2,1)} %local_rows.1.piece_ref), channel_id=1, source_target_pairs={{8,0},{16,8},{24,16},{0,24},{9,1},{17,9},{25,17},{1,25},{10,2},{18... | collective-permute-start | bytes 442376 | tf_op jit(solution)/shard_map/ppermute | solution.py:348
  10.5 4.2 %collective-permute-start = (bf16[72,1024]{1,0:T(8,128)(2,1)}, bf16[72,1024]{1,0:T(8,128)(2,1)S(1)}, u32[]{:S(2)}, u32[]{:S(2)}) collective-permute-start(bf16[72,1024]{1,0:T(8,128)(2,1)} %local_rows.1.piece_ref), channel_id=1, source_target_pairs={{1,0},{0,1},{3,2},{2,3},{5,4},{4,5},{7,6},{6,7},{9,8},{8,9},{11,10... | collective-permute-start | bytes 442376 | tf_op jit(solution)/shard_map/ppermute | solution.py:343
  10.5 0.9 %copy-start = (bf16[72,1024]{1,0:T(8,128)(2,1)S(1)}, bf16[72,1024]{1,0:T(8,128)(2,1)}, u32[]{:S(2)}) copy-start(bf16[72,1024]{1,0:T(8,128)(2,1)} %local_rows.1.piece_ref) | copy-start | bytes 442372
  11.4 0.7 %copy-start.1 = (f32[16]{0:T(128)S(1)}, f32[16]{0:T(128)}, u32[]{:S(2)}) copy-start(f32[16]{0:T(128)} %param.4) | copy-start | bytes 196
  12.1 0.7 %copy-start.2 = (f32[65]{0:T(128)S(1)}, f32[65]{0:T(128)}, u32[]{:S(2)}) copy-start(f32[65]{0:T(128)} %param.5) | copy-start | bytes 784
  13.6 1.6 %collective-permute-start.4 = (bf16[72,1024]{1,0:T(8,128)(2,1)S(1)}, bf16[72,1024]{1,0:T(8,128)(2,1)S(1)}, u32[]{:S(2)}, u32[]{:S(2)}) collective-permute-start(bf16[72,1024]{1,0:T(8,128)(2,1)S(1)} %collective-permute-done.1.refs_2_), channel_id=1, source_target_pairs={{1,0},{0,1},{3,2},{2,3},{5,4},{4,5},{7,6},{6,7},{9,8},{8,9},{11,10... | collective-permute-start | bytes 442376 | tf_op jit(solution)/shard_map/ppermute | solution.py:343
  14.2 1.4 %collective-permute-start.5 = (bf16[72,1024]{1,0:T(8,128)(2,1)S(1)}, bf16[72,1024]{1,0:T(8,128)(2,1)S(1)}, u32[]{:S(2)}, u32[]{:S(2)}) collective-permute-start(bf16[72,1024]{1,0:T(8,128)(2,1)S(1)} %collective-permute-done.2.refs_4_), channel_id=1, source_target_pairs={{1,0},{0,1},{3,2},{2,3},{5,4},{4,5},{7,6},{6,7},{9,8},{8,9},{11,10... | collective-permute-start | bytes 442376 | tf_op jit(solution)/shard_map/ppermute | solution.py:343
  14.3 1.5 %collective-permute-start.6 = (bf16[72,1024]{1,0:T(8,128)(2,1)S(1)}, bf16[72,1024]{1,0:T(8,128)(2,1)S(1)}, u32[]{:S(2)}, u32[]{:S(2)}) collective-permute-start(bf16[72,1024]{1,0:T(8,128)(2,1)S(1)} %collective-permute-done.3.refs_6_), channel_id=1, source_target_pairs={{1,0},{0,1},{3,2},{2,3},{5,4},{4,5},{7,6},{6,7},{9,8},{8,9},{11,10... | collective-permute-start | bytes 442376 | tf_op jit(solution)/shard_map/ppermute | solution.py:343
  21.4 13.0 %collective-permute-start.10 = (bf16[72,1024]{1,0:T(8,128)(2,1)S(1)}, bf16[72,1024]{1,0:T(8,128)(2,1)S(1)}, u32[]{:S(2)}, u32[]{:S(2)}) collective-permute-start(bf16[72,1024]{1,0:T(8,128)(2,1)S(1)} %collective-permute-done.7.refs_0_), channel_id=1, source_target_pairs={{6,0},{7,1},{4,2},{5,3},{2,4},{3,5},{0,6},{1,7},{14,8},{15,9},{12,... | collective-permute-start | bytes 442376 | tf_op jit(solution)/shard_map/ppermute | solution.py:343
  23.9 10.5 %collective-permute-start.9 = (bf16[72,1024]{1,0:T(8,128)(2,1)S(1)}, bf16[72,1024]{1,0:T(8,128)(2,1)S(1)}, u32[]{:S(2)}, u32[]{:S(2)}) collective-permute-start(bf16[72,1024]{1,0:T(8,128)(2,1)S(1)} %collective-permute-done.7.refs_0_), channel_id=1, source_target_pairs={{4,0},{5,1},{6,2},{7,3},{0,4},{1,5},{2,6},{3,7},{12,8},{13,9},{14,... | collective-permute-start | bytes 442376 | tf_op jit(solution)/shard_map/ppermute | solution.py:343
  24.4 10.0 %collective-permute-start.8 = (bf16[72,1024]{1,0:T(8,128)(2,1)S(1)}, bf16[72,1024]{1,0:T(8,128)(2,1)S(1)}, u32[]{:S(2)}, u32[]{:S(2)}) collective-permute-start(bf16[72,1024]{1,0:T(8,128)(2,1)S(1)} %collective-permute-done.7.refs_0_), channel_id=1, source_target_pairs={{2,0},{3,1},{0,2},{1,3},{6,4},{7,5},{4,6},{5,7},{10,8},{11,9},{8,1... | collective-permute-start | bytes 442376 | tf_op jit(solution)/shard_map/ppermute | solution.py:343
  25.0 9.5 %collective-permute-start.11 = (bf16[72,1024]{1,0:T(8,128)(2,1)}, bf16[72,1024]{1,0:T(8,128)(2,1)S(1)}, u32[]{:S(2)}, u32[]{:S(2)}) collective-permute-start(bf16[72,1024]{1,0:T(8,128)(2,1)} %local_rows.1.piece_ref), channel_id=1, source_target_pairs={{16,0},{24,8},{0,16},{8,24},{17,1},{25,9},{1,17},{9,25},{18,2},{26... | collective-permute-start | bytes 442376 | tf_op jit(solution)/shard_map/ppermute | solution.py:348
  34.5 3.1 %collective-permute-start.12 = (bf16[72,1024]{1,0:T(8,128)(2,1)S(1)}, bf16[72,1024]{1,0:T(8,128)(2,1)S(1)}, u32[]{:S(2)}, u32[]{:S(2)}) collective-permute-start(bf16[72,1024]{1,0:T(8,128)(2,1)S(1)} %collective-permute-done.7.refs_0_), channel_id=1, source_target_pairs={{1,0},{0,1},{3,2},{2,3},{5,4},{4,5},{7,6},{6,7},{9,8},{8,9},{11,10... | collective-permute-start | bytes 442376 | tf_op jit(solution)/shard_map/ppermute | solution.py:343
  34.6 4.0 %collective-permute-start.13 = (bf16[72,1024]{1,0:T(8,128)(2,1)S(1)}, bf16[72,1024]{1,0:T(8,128)(2,1)S(1)}, u32[]{:S(2)}, u32[]{:S(2)}) collective-permute-start(bf16[72,1024]{1,0:T(8,128)(2,1)S(1)} %collective-permute-done.8.refs_2_), channel_id=1, source_target_pairs={{1,0},{0,1},{3,2},{2,3},{5,4},{4,5},{7,6},{6,7},{9,8},{8,9},{11,10... | collective-permute-start | bytes 442376 | tf_op jit(solution)/shard_map/ppermute | solution.py:343
  35.0 4.0 %collective-permute-start.14 = (bf16[72,1024]{1,0:T(8,128)(2,1)S(1)}, bf16[72,1024]{1,0:T(8,128)(2,1)S(1)}, u32[]{:S(2)}, u32[]{:S(2)}) collective-permute-start(bf16[72,1024]{1,0:T(8,128)(2,1)S(1)} %collective-permute-done.9.refs_4_), channel_id=1, source_target_pairs={{1,0},{0,1},{3,2},{2,3},{5,4},{4,5},{7,6},{6,7},{9,8},{8,9},{11,10... | collective-permute-start | bytes 442376 | tf_op jit(solution)/shard_map/ppermute | solution.py:343
  35.1 3.9 %collective-permute-start.15 = (bf16[72,1024]{1,0:T(8,128)(2,1)S(1)}, bf16[72,1024]{1,0:T(8,128)(2,1)S(1)}, u32[]{:S(2)}, u32[]{:S(2)}) collective-permute-start(bf16[72,1024]{1,0:T(8,128)(2,1)S(1)} %collective-permute-done.10.refs_6_), channel_id=1, source_target_pairs={{1,0},{0,1},{3,2},{2,3},{5,4},{4,5},{7,6},{6,7},{9,8},{8,9},{11,10... | collective-permute-start | bytes 442376 | tf_op jit(solution)/shard_map/ppermute | solution.py:343
  35.6 13.4 %collective-permute-start.18 = (bf16[72,1024]{1,0:T(8,128)(2,1)S(1)}, bf16[72,1024]{1,0:T(8,128)(2,1)S(1)}, u32[]{:S(2)}, u32[]{:S(2)}) collective-permute-start(bf16[72,1024]{1,0:T(8,128)(2,1)S(1)} %collective-permute-done.11.refs_0_), channel_id=1, source_target_pairs={{6,0},{7,1},{4,2},{5,3},{2,4},{3,5},{0,6},{1,7},{14,8},{15,9},{12,... | collective-permute-start | bytes 442376 | tf_op jit(solution)/shard_map/ppermute | solution.py:343
  37.6 11.4 %collective-permute-start.17 = (bf16[72,1024]{1,0:T(8,128)(2,1)S(1)}, bf16[72,1024]{1,0:T(8,128)(2,1)S(1)}, u32[]{:S(2)}, u32[]{:S(2)}) collective-permute-start(bf16[72,1024]{1,0:T(8,128)(2,1)S(1)} %collective-permute-done.11.refs_0_), channel_id=1, source_target_pairs={{4,0},{5,1},{6,2},{7,3},{0,4},{1,5},{2,6},{3,7},{12,8},{13,9},{14,... | collective-permute-start | bytes 442376 | tf_op jit(solution)/shard_map/ppermute | solution.py:343
  38.5 10.4 %collective-permute-start.16 = (bf16[72,1024]{1,0:T(8,128)(2,1)S(1)}, bf16[72,1024]{1,0:T(8,128)(2,1)S(1)}, u32[]{:S(2)}, u32[]{:S(2)}) collective-permute-start(bf16[72,1024]{1,0:T(8,128)(2,1)S(1)} %collective-permute-done.11.refs_0_), channel_id=1, source_target_pairs={{2,0},{3,1},{0,2},{1,3},{6,4},{7,5},{4,6},{5,7},{10,8},{11,9},{8,1... | collective-permute-start | bytes 442376 | tf_op jit(solution)/shard_map/ppermute | solution.py:343
  49.0 1.4 %collective-permute-start.19 = (bf16[72,1024]{1,0:T(8,128)(2,1)S(1)}, bf16[72,1024]{1,0:T(8,128)(2,1)S(1)}, u32[]{:S(2)}, u32[]{:S(2)}) collective-permute-start(bf16[72,1024]{1,0:T(8,128)(2,1)S(1)} %collective-permute-done.11.refs_0_), channel_id=1, source_target_pairs={{1,0},{0,1},{3,2},{2,3},{5,4},{4,5},{7,6},{6,7},{9,8},{8,9},{11,10... | collective-permute-start | bytes 442376 | tf_op jit(solution)/shard_map/ppermute | solution.py:343
  49.0 1.6 %collective-permute-start.20 = (bf16[72,1024]{1,0:T(8,128)(2,1)S(1)}, bf16[72,1024]{1,0:T(8,128)(2,1)S(1)}, u32[]{:S(2)}, u32[]{:S(2)}) collective-permute-start(bf16[72,1024]{1,0:T(8,128)(2,1)S(1)} %collective-permute-done.16.refs_2_), channel_id=1, source_target_pairs={{1,0},{0,1},{3,2},{2,3},{5,4},{4,5},{7,6},{6,7},{9,8},{8,9},{11,10... | collective-permute-start | bytes 442376 | tf_op jit(solution)/shard_map/ppermute | solution.py:343
  49.5 1.4 %collective-permute-start.21 = (bf16[72,1024]{1,0:T(8,128)(2,1)S(1)}, bf16[72,1024]{1,0:T(8,128)(2,1)S(1)}, u32[]{:S(2)}, u32[]{:S(2)}) collective-permute-start(bf16[72,1024]{1,0:T(8,128)(2,1)S(1)} %collective-permute-done.17.refs_4_), channel_id=1, source_target_pairs={{1,0},{0,1},{3,2},{2,3},{5,4},{4,5},{7,6},{6,7},{9,8},{8,9},{11,10... | collective-permute-start | bytes 442376 | tf_op jit(solution)/shard_map/ppermute | solution.py:343
  49.6 1.5 %collective-permute-start.22 = (bf16[72,1024]{1,0:T(8,128)(2,1)S(1)}, bf16[72,1024]{1,0:T(8,128)(2,1)S(1)}, u32[]{:S(2)}, u32[]{:S(2)}) collective-permute-start(bf16[72,1024]{1,0:T(8,128)(2,1)S(1)} %collective-permute-done.18.refs_6_), channel_id=1, source_target_pairs={{1,0},{0,1},{3,2},{2,3},{5,4},{4,5},{7,6},{6,7},{9,8},{8,9},{11,10... | collective-permute-start | bytes 442376 | tf_op jit(solution)/shard_map/ppermute | solution.py:343

commit v4 on v3

--- a/solution.py
+++ b/solution.py
@@ -42,6 +42,7 @@
         self.full = 2 * self.deep - self.even
         self.lags = NLAG // lag_total
         self.shifts = self.lags // 2 // SUB
+        self.pitch = self.depth + 2 * SUB * (self.shifts // 2 - 1)
         self.held = lag_total * self.slot
         self.joined = self.held + ceil_to(lag_total * self.head, 16)
         self.pad = NLAG // 4
@@ -52,7 +53,7 @@
     return taps[0:1, index : index + 1].astype(BF16).astype(F32)
 
 
-def local_kernel(plan, taps_ref, raw_ref, out_ref, spread):
+def local_kernel(plan, taps_ref, bp_ref, raw_ref, out_ref, kept_ref, spread, both):
     row = lax.broadcasted_iota(jnp.int32, (plan.rows, plan.raw), 0)
     time = lax.broadcasted_iota(jnp.int32, (plan.rows, plan.raw), 1)
     tap = 2 * (row + plan.head) - time
@@ -69,24 +70,35 @@
     series = [
         spread[pl.ds(w, plan.raw, stride=plan.windows), :].astype(BF16) for w in range(plan.windows)
     ]
-    out_ref[...] = jnp.dot(
-        table, jnp.concatenate(series, axis=1), preferred_element_type=F32
-    ).astype(BF16)
-
-
-def local_rows(plan, raw, taps):
+    rows = jnp.dot(table, jnp.concatenate(series, axis=1), preferred_element_type=F32).astype(BF16)
+    out_ref[...] = rows
+    kept_ref[0 : plan.rows, :] = rows
+    both[...] = jnp.zeros((SUB, LANES), F32)
+    both[0:1, 0 : plan.dec_taps] = taps_ref[...]
+    both[1:2, 0 : plan.bp_taps] = bp_ref[...]
+    kept_ref[plan.rows :, 0:LANES] = both[...].astype(BF16)
+
+
+def local_rows(plan, raw, dec_taps, bp_taps):
     return pl.pallas_call(
         functools.partial(local_kernel, plan),
-        out_shape=jax.ShapeDtypeStruct((plan.rows, plan.wide), BF16),
-        in_specs=[VMEM, VMEM],
-        out_specs=VMEM,
-        scratch_shapes=[pltpu.VMEM((plan.raw * plan.windows, plan.channels), F32)],
+        out_shape=(
+            jax.ShapeDtypeStruct((plan.rows, plan.wide), BF16),
+            jax.ShapeDtypeStruct((plan.rows + SUB, plan.wide), BF16),
+        ),
+        in_specs=[VMEM, VMEM, VMEM],
+        out_specs=(VMEM, VMEM),
+        scratch_shapes=[
+            pltpu.VMEM((plan.raw * plan.windows, plan.channels), F32),
+            pltpu.VMEM((SUB, LANES), F32),
+        ],
         name="local_rows",
-    )(taps, jnp.transpose(raw, (2, 0, 1)))
-
-
-def table_kernel(plan, dec_ref, bp_ref, piece_ref, band_ref, edge_ref, kept_ref):
-    kept_ref[...] = piece_ref[...]
+    )(dec_taps, bp_taps, jnp.transpose(raw, (2, 0, 1)))
+
+
+def table_kernel(plan, rows_ref, band_ref, edge_ref, kept_ref):
+    kept_ref[...] = rows_ref[0 : plan.rows, :]
+    dec_ref, bp_ref = (rows_ref[plan.rows :, 0:LANES].astype(F32)[k : k + 1] for k in range(2))
     span = ceil_to(plan.total + plan.bp_taps, LANES)
     lane = lax.broadcasted_iota(jnp.int32, (1, span), 1)
     base = jnp.zeros((1, span), F32)
@@ -122,20 +134,20 @@
     edge_ref[...] = table.astype(BF16)
 
 
-def tables(plan, dec_taps, bp_taps, piece):
+def tables(plan, rows):
     return pl.pallas_call(
         functools.partial(table_kernel, plan),
         out_shape=(
             jax.ShapeDtypeStruct((2 * plan.half, plan.joined), BF16),
             jax.ShapeDtypeStruct((plan.joined - plan.held, plan.held), BF16),
-            jax.ShapeDtypeStruct(piece.shape, piece.dtype),
+            jax.ShapeDtypeStruct((plan.rows, plan.wide), BF16),
         ),
-        in_specs=[VMEM, VMEM, VMEM],
+        in_specs=[VMEM],
         out_specs=(VMEM, VMEM, VMEM),
         compiler_params=pltpu.CompilerParams(vmem_limit_bytes=12 * 2**20),
         cost_estimate=pl.CostEstimate(flops=500_000_000, bytes_accessed=2_000_000, transcendentals=0),
         name="tables",
-    )(dec_taps, bp_taps, piece)
+    )(rows)
 
 
 def make_series(plan, place_ref, pieces, tables_refs, held, even, odd, ahead, right):
@@ -182,24 +194,27 @@
     base = place * (plan.lags // 2)
     for w in range(plan.windows):
         cols = slice(w * plan.channels, (w + 1) * plan.channels)
-        rows = slice(w * plan.depth, (w + 1) * plan.depth)
         for first in range(2):
-            shifts = range(first, plan.shifts, 2)
-            height = plan.depth + 2 * SUB * (len(shifts) - 1)
-            at = pl.ds(pl.multiple_of(base + first * SUB, SUB), height)
+            at = pl.ds(pl.multiple_of(base + first * SUB, SUB), plan.pitch)
             a, b, c = even[at, cols], odd[at, cols], ahead[at, cols]
+            to = slice(first * plan.channels, (first + 1) * plan.channels)
             for k, value in enumerate((b, a - b, c - b)):
-                value = value.astype(BF16)
-                for n, s in enumerate(shifts):
-                    to = slice(s * plan.channels, (s + 1) * plan.channels)
-                    part = value[2 * SUB * n : 2 * SUB * n + plan.depth]
-                    over = max(0, rows.stop - max(rows.start, plan.even)) if k == 0 else 0
-                    if over < plan.depth:
-                        right[k, rows.start : rows.stop - over, to] = part[: plan.depth - over]
-                    if over:
-                        first_over = rows.stop - over - plan.even + plan.deep
-                        for other in (1, 2):
-                            right[other, first_over : first_over + over, to] = part[plan.depth - over :]
+                right[k, w * plan.pitch : (w + 1) * plan.pitch, to] = value.astype(BF16)
+
+
+def right_operand(plan, k, n, right):
+    def rows(k, low, high):
+        parts = []
+        for w in range(plan.windows):
+            start, stop = max(low, w * plan.depth), min(high, (w + 1) * plan.depth)
+            if start < stop:
+                at = w * (plan.pitch - plan.depth) + 2 * SUB * n
+                parts.append(right[k, at + start : at + stop, :])
+        return parts
+
+    if k == 0:
+        return jnp.concatenate(rows(0, 0, plan.even), axis=0)
+    return jnp.concatenate(rows(k, 0, plan.deep) + rows(0, plan.even, plan.deep), axis=0)
 
 
 def make_left(plan, even, odd, stacks, mixes, left):
@@ -234,19 +249,17 @@
 
 def correlate(plan, count, left, right, out_ref):
     factor = 1.0 / math.sqrt(plan.windows * plan.total)
-    step = min(2 * LANES, plan.shifts * plan.channels)
-    for c in range(0, plan.shifts * plan.channels, step):
-        cols = slice(c, c + step)
+    for n in range(plan.shifts // 2):
         rows = pl.ds(pl.multiple_of(pl.program_id(0) * count * SUB, count * SUB), count * SUB)
         both, even, odd = (
-            jnp.dot(left[k, rows, :deep], right[k, :deep, cols], preferred_element_type=F32)
+            jnp.dot(left[k, rows, :deep], right_operand(plan, k, n, right), preferred_element_type=F32)
             for k, deep in enumerate((plan.even, plan.full, plan.full))
         )
         for parity, value in ((0, even), (1, odd)):
             value = (both + value) * factor
-            for n in range(step // plan.channels):
-                s = c // plan.channels + n
-                part = value[:, n * plan.channels : (n + 1) * plan.channels]
+            for first in range(2):
+                s = 2 * n + first
+                part = value[:, first * plan.channels : (first + 1) * plan.channels]
                 out_ref[:, 0, pl.ds(2 * SUB * s + parity, SUB, stride=2), :] = part.reshape(
                     count, SUB, plan.channels
                 )
@@ -285,7 +298,7 @@
         functools.partial(own_kernel, plan),
         out_shape=(
             jax.ShapeDtypeStruct((3, plan.channels * SUB, plan.full), BF16),
-            jax.ShapeDtypeStruct((3, plan.full, plan.shifts * plan.channels), BF16),
+            jax.ShapeDtypeStruct((3, plan.windows * plan.pitch, 2 * plan.channels), BF16),
         ),
         in_specs=[SMEM] + [VMEM] * (plan.lag_total + 2),
         out_specs=(VMEM, VMEM),
@@ -330,7 +343,7 @@
         in_specs=in_specs,
         out_specs=out_spec,
         scratch_shapes=series_scratch(plan)
-        + [pltpu.VMEM((3, plan.full, plan.shifts * plan.channels), BF16)],
+        + [pltpu.VMEM((3, plan.windows * plan.pitch, 2 * plan.channels), BF16)],
         input_output_aliases={len(in_specs) - 1: 0},
         compiler_params=pltpu.CompilerParams(vmem_limit_bytes=30 * 2**20),
         cost_estimate=cost,
@@ -360,9 +373,10 @@
     plan = Plan(raw_samples.shape, lax.axis_size("lag"), decimation_taps.shape[0], bandpass_taps.shape[0])
     pairs = lax.axis_size("chan") // 2 + 1
     place = lax.axis_index("lag").astype(jnp.int32).reshape(1)
-    dec_taps = decimation_taps.reshape(1, -1)
-    piece = local_rows(plan, raw_samples, dec_taps)
-    *tabs, kept = tables(plan, dec_taps, bandpass_taps.reshape(1, -1), piece)
+    piece, kept = local_rows(
+        plan, raw_samples, decimation_taps.reshape(1, -1), bandpass_taps.reshape(1, -1)
+    )
+    *tabs, kept = tables(plan, kept)
     count = 32
     own = same_core(piece)
     near = from_ahead(piece, 1)

time: 61.2 us -> 60.6 us (level)
  local copies, waits for them, and re-layouts: 2.25 us -> 0.92 us
  waiting for transfers between devices: 2.51 us -> 3.49 us
    unnamed x6 -> x2, local copies, waits for them, and re-layouts: 2.25 us -> 0.92 us
    ppermute x21, waiting for transfers between devices: 2.17 us -> 3.49 us  [swap(): return lax.ppermute(piece, 'lag', [(i ^ mask, i) for i in range(count)])]
  transfers between devices with their start and end apart: 23 -> 23, of which waited for: 8 -> 9; matrix products, arithmetic and copies ran while one was open for 0% -> 0% of each run, Pallas kernels for 29% -> 29%
where the time goes in v4:
time: 60.6 us; the launch traced here: 60.5 us
  Pallas kernels  35.1 us (58%)
  starting transfers between devices  20.8 us (34%)
  waiting for transfers between devices  3.49 us (6%)
  local copies, waits for them, and re-layouts  0.92 us (2%)
    pallas_call x2, Pallas kernels, other_correlation(): pl.pallas_call(functools.partial(other_kernel, plan, count), grid=(plan.c...  19.6 us
    ppermute x21, starting transfers between devices, swap(): return lax.ppermute(piece, 'lag', [(i ^ mask, i) for i in range(count)])  14.2 us
    pallas_call x1, Pallas kernels, own_correlation(): pl.pallas_call(functools.partial(first_kernel, plan, count), grid=(plan.c...  7.12 us
    ppermute x2, starting transfers between devices, from_ahead(): lax.ppermute(piece, 'chan', [((i + distance) % count, i) for i in range(c...  6.67 us
    pallas_call x1, Pallas kernels, prepare_own(): pl.pallas_call(functools.partial(own_kernel, plan), out_shape=(jax.ShapeD...  5.53 us
    ppermute x21, waiting for transfers between devices, swap(): return lax.ppermute(piece, 'lag', [(i ^ mask, i) for i in range(count)])  3.49 us
    pallas_call x1, Pallas kernels, local_rows(): pl.pallas_call(functools.partial(local_kernel, plan), out_shape=(jax.Shap...  1.99 us
  transfers between devices with their start and end apart: 23, of which 9 were waited for; matrix products, arithmetic and copies ran while one was open for 0% of the time, Pallas kernels for 29%

profile of v4, /device:TPU:0, one launch (start us, length us, event | category | flops | bytes accessed | tf_op | source)
XLA Modules:
  0.0 60.5 jit_solution(16828099335161448865)
XLA Ops:
  0.0 2.0 %local_rows.1 = (bf16[72,1024]{1,0:T(8,128)(2,1)}, bf16[80,1024]{1,0:T(8,128)(2,1)}) custom-call(f32[1,16]{1,0:T(1,128)} %bitcast.5, f32[1,65]{1,0:T(1,128)} %bitcast.6, bf16[100,8,128]{2,1,0:T(8,128)(2,1)} %bitcast.4), custom_call_target="tpu_custom_call" | custom-call | tf_op jit(solution)/shard_map/local_rows/pallas_call | solution.py:83
  2.0 3.9 %collective-permute-start.3 = (bf16[72,1024]{1,0:T(8,128)(2,1)}, bf16[72,1024]{1,0:T(8,128)(2,1)S(1)}, u32[]{:S(2)}, u32[]{:S(2)}) collective-permute-start(bf16[72,1024]{1,0:T(8,128)(2,1)} %get-tuple-element.61), channel_id=1, source_target_pairs={{6,0},{7,1},{4,2},{5,3},{2,4},{3,5},{0,6},{1,7},{14,8},{15,9},{12,... | collective-permute-start | bytes 442376 | tf_op jit(solution)/shard_map/ppermute | solution.py:356
  5.9 0.5 collective-permute-start.2
  6.4 4.1 %collective-permute-start.7 = (bf16[72,1024]{1,0:T(8,128)(2,1)}, bf16[72,1024]{1,0:T(8,128)(2,1)S(1)}, u32[]{:S(2)}, u32[]{:S(2)}) collective-permute-start(bf16[72,1024]{1,0:T(8,128)(2,1)} %get-tuple-element.61), channel_id=1, source_target_pairs={{8,0},{16,8},{24,16},{0,24},{9,1},{17,9},{25,17},{1,25},{10,2},{18... | collective-permute-start | bytes 442376 | tf_op jit(solution)/shard_map/ppermute | solution.py:361
  10.5 0.9 %copy-done = bf16[80,1024]{1,0:T(8,128)(2,1)S(1)} copy-done((bf16[80,1024]{1,0:T(8,128)(2,1)S(1)}, bf16[80,1024]{1,0:T(8,128)(2,1)}, u32[]{:S(2)}) %copy-start) | copy-done | bytes 163864
  11.4 0.9 %tables.1 = (bf16[400,704]{1,0:T(8,128)(2,1)S(1)}, bf16[64,640]{1,0:T(8,128)(2,1)S(1)}, bf16[72,1024]{1,0:T(8,128)(2,1)S(1)}) custom-call(bf16[80,1024]{1,0:T(8,128)(2,1)S(1)} %copy-done), custom_call_target="tpu_custom_call" | custom-call | flops 500000000 | bytes 2000000 | tf_op jit(solution)/shard_map/tables/pallas_call | solution.py:138
  12.4 0.7 %collective-permute-done.2.refs_4_ = bf16[72,1024]{1,0:T(8,128)(2,1)S(1)} collective-permute-done((bf16[72,1024]{1,0:T(8,128)(2,1)}, bf16[72,1024]{1,0:T(8,128)(2,1)S(1)}, u32[]{:S(2)}, u32[]{:S(2)}) %collective-permute-start.2) | collective-permute-done | bytes 147488 | tf_op jit(solution)/shard_map/ppermute | solution.py:356
  13.1 0.3 collective-permute-done.1.refs_2_
  13.4 0.5 collective-permute-start.5
  13.9 0.8 %collective-permute-done.4.refs_3_ = bf16[72,1024]{1,0:T(8,128)(2,1)S(1)} collective-permute-done((bf16[72,1024]{1,0:T(8,128)(2,1)S(1)}, bf16[72,1024]{1,0:T(8,128)(2,1)S(1)}, u32[]{:S(2)}, u32[]{:S(2)}) %collective-permute-start.4) | collective-permute-done | bytes 147488 | tf_op jit(solution)/shard_map/ppermute | solution.py:356
  14.8 0.2 collective-permute-done.5.refs_5_
  15.0 0.3 collective-permute-done.6.refs_7_
  15.3 5.5 %prepare_own.1 = (bf16[3,1024,1792]{2,1,0:T(8,128)(2,1)S(1)}, bf16[3,1792,256]{2,1,0:T(8,128)(2,1)S(1)}) custom-call(s32[1]{0:T(128)} %bitcast.place_ref, bf16[72,1024]{1,0:T(8,128)(2,1)S(1)} %get-tuple-element.40.refs_0_, bf16[72,1024]{1,0:T(8,128)(2,1)S(1)} %collective-permute-done.refs_1_, bf16[72,1024]{1,0:T(8,128)(2,1)S(1)} %collective-permute-done.1.refs_2_, ...), custom_call_target="tpu_custom_call" | custom-call | flops 100000000 | bytes 262144 | tf_op jit(solution)/shard_map/prepare_own/pallas_call | solution.py:297
  20.8 1.8 %collective-permute-start.10 = (bf16[72,1024]{1,0:T(8,128)(2,1)S(1)}, bf16[72,1024]{1,0:T(8,128)(2,1)S(1)}, u32[]{:S(2)}, u32[]{:S(2)}) collective-permute-start(bf16[72,1024]{1,0:T(8,128)(2,1)S(1)} %collective-permute-done.7.refs_0_), channel_id=1, source_target_pairs={{6,0},{7,1},{4,2},{5,3},{2,4},{3,5},{0,6},{1,7},{14,8},{15,9},{12,... | collective-permute-start | bytes 442376 | tf_op jit(solution)/shard_map/ppermute | solution.py:356
  22.6 1.3 %collective-permute-start.9 = (bf16[72,1024]{1,0:T(8,128)(2,1)S(1)}, bf16[72,1024]{1,0:T(8,128)(2,1)S(1)}, u32[]{:S(2)}, u32[]{:S(2)}) collective-permute-start(bf16[72,1024]{1,0:T(8,128)(2,1)S(1)} %collective-permute-done.7.refs_0_), channel_id=1, source_target_pairs={{4,0},{5,1},{6,2},{7,3},{0,4},{1,5},{2,6},{3,7},{12,8},{13,9},{14,... | collective-permute-start | bytes 442376 | tf_op jit(solution)/shard_map/ppermute | solution.py:356
  23.8 0.5 collective-permute-start.8
  24.4 2.6 %collective-permute-start.11 = (bf16[72,1024]{1,0:T(8,128)(2,1)}, bf16[72,1024]{1,0:T(8,128)(2,1)S(1)}, u32[]{:S(2)}, u32[]{:S(2)}) collective-permute-start(bf16[72,1024]{1,0:T(8,128)(2,1)} %get-tuple-element.61), channel_id=1, source_target_pairs={{16,0},{24,8},{0,16},{8,24},{17,1},{25,9},{1,17},{9,25},{18,2},{26... | collective-permute-start | bytes 442376 | tf_op jit(solution)/shard_map/ppermute | solution.py:361
  26.9 7.1 %own_correlation.1.refs_11_ = f32[128,3,64,128]{3,2,1,0:T(8,128)} custom-call(bf16[3,1024,1792]{2,1,0:T(8,128)(2,1)S(1)} %get-tuple-element.58.left_ref.refs_10_, bf16[3,1792,256]{2,1,0:T(8,128)(2,1)S(1)} %get-tuple-element.59.right_ref), custom_call_target="tpu_custom_call" | custom-call | flops 5234491392 | bytes 8388608 | tf_op jit(solution)/shard_map/own_correlation/pallas_call | solution.py:324
  34.2 0.5 collective-permute-start.13
  34.7 0.1 collective-permute-start.14
  34.7 0.4 collective-permute-start.15
  35.2 1.7 %collective-permute-start.18 = (bf16[72,1024]{1,0:T(8,128)(2,1)S(1)}, bf16[72,1024]{1,0:T(8,128)(2,1)S(1)}, u32[]{:S(2)}, u32[]{:S(2)}) collective-permute-start(bf16[72,1024]{1,0:T(8,128)(2,1)S(1)} %collective-permute-done.11.refs_0_), channel_id=1, source_target_pairs={{6,0},{7,1},{4,2},{5,3},{2,4},{3,5},{0,6},{1,7},{14,8},{15,9},{12,... | collective-permute-start | bytes 442376 | tf_op jit(solution)/shard_map/ppermute | solution.py:356
  36.8 1.3 %collective-permute-start.17 = (bf16[72,1024]{1,0:T(8,128)(2,1)S(1)}, bf16[72,1024]{1,0:T(8,128)(2,1)S(1)}, u32[]{:S(2)}, u32[]{:S(2)}) collective-permute-start(bf16[72,1024]{1,0:T(8,128)(2,1)S(1)} %collective-permute-done.11.refs_0_), channel_id=1, source_target_pairs={{4,0},{5,1},{6,2},{7,3},{0,4},{1,5},{2,6},{3,7},{12,8},{13,9},{14,... | collective-permute-start | bytes 442376 | tf_op jit(solution)/shard_map/ppermute | solution.py:356
  38.1 0.5 collective-permute-start.16
  38.7 9.8 %other_correlation.2.refs_11_ = f32[128,3,64,128]{3,2,1,0:T(8,128)} custom-call(s32[1]{0:T(128)} %bitcast.place_ref, bf16[72,1024]{1,0:T(8,128)(2,1)S(1)} %collective-permute-done.7.refs_0_, bf16[72,1024]{1,0:T(8,128)(2,1)S(1)} %collective-permute-done.12.refs_1_, ...), custom_call_target="tpu_custom_call", output_to_operand_aliasing={{}: (12, {})} | custom-call | flops 5234491392 | bytes 8388608 | tf_op jit(solution)/shard_map/other_correlation/pallas_call | solution.py:339
  48.6 0.5 collective-permute-start.20
  49.1 0.4 collective-permute-start.22
  49.6 0.3 collective-permute-done.19.refs_1_
  49.9 0.2 collective-permute-done.20.refs_3_
  50.1 0.3 collective-permute-done.21.refs_5_
  50.4 0.2 collective-permute-done.22.refs_7_
  50.7 9.8 %other_correlation.3 = f32[128,3,64,128]{3,2,1,0:T(8,128)} custom-call(s32[1]{0:T(128)} %bitcast.place_ref, bf16[72,1024]{1,0:T(8,128)(2,1)S(1)} %collective-permute-done.11.refs_0_, bf16[72,1024]{1,0:T(8,128)(2,1)S(1)} %collective-permute-done.19.refs_1_, bf16[72,1024]{1,0:T(8,128)(2,1)S(1)} %collective-permute-done.16.refs_2_, ...), custom_call_target="tpu_custom_call", output_to_operand_aliasing={{}: (12, {})} | custom-call | flops 5234491392 | bytes 8388608 | tf_op jit(solution)/shard_map/other_correlation/pallas_call | solution.py:339
  (22 shorter events, 0.3 us)
Async XLA Ops:
  2.0 10.4 %collective-permute-start.3 = (bf16[72,1024]{1,0:T(8,128)(2,1)}, bf16[72,1024]{1,0:T(8,128)(2,1)S(1)}, u32[]{:S(2)}, u32[]{:S(2)}) collective-permute-start(bf16[72,1024]{1,0:T(8,128)(2,1)} %get-tuple-element.61), channel_id=1, source_target_pairs={{6,0},{7,1},{4,2},{5,3},{2,4},{3,5},{0,6},{1,7},{14,8},{15,9},{12,... | collective-permute-start | bytes 442376 | tf_op jit(solution)/shard_map/ppermute | solution.py:356
  5.9 7.2 %collective-permute-start.2 = (bf16[72,1024]{1,0:T(8,128)(2,1)}, bf16[72,1024]{1,0:T(8,128)(2,1)S(1)}, u32[]{:S(2)}, u32[]{:S(2)}) collective-permute-start(bf16[72,1024]{1,0:T(8,128)(2,1)} %get-tuple-element.61), channel_id=1, source_target_pairs={{4,0},{5,1},{6,2},{7,3},{0,4},{1,5},{2,6},{3,7},{12,8},{13,9},{14,... | collective-permute-start | bytes 442376 | tf_op jit(solution)/shard_map/ppermute | solution.py:356
  6.4 7.0 %collective-permute-start.1 = (bf16[72,1024]{1,0:T(8,128)(2,1)}, bf16[72,1024]{1,0:T(8,128)(2,1)S(1)}, u32[]{:S(2)}, u32[]{:S(2)}) collective-permute-start(bf16[72,1024]{1,0:T(8,128)(2,1)} %get-tuple-element.61), channel_id=1, source_target_pairs={{2,0},{3,1},{0,2},{1,3},{6,4},{7,5},{4,6},{5,7},{10,8},{11,9},{8,1... | collective-permute-start | bytes 442376 | tf_op jit(solution)/shard_map/ppermute | solution.py:356
  6.4 7.5 %collective-permute-start.7 = (bf16[72,1024]{1,0:T(8,128)(2,1)}, bf16[72,1024]{1,0:T(8,128)(2,1)S(1)}, u32[]{:S(2)}, u32[]{:S(2)}) collective-permute-start(bf16[72,1024]{1,0:T(8,128)(2,1)} %get-tuple-element.61), channel_id=1, source_target_pairs={{8,0},{16,8},{24,16},{0,24},{9,1},{17,9},{25,17},{1,25},{10,2},{18... | collective-permute-start | bytes 442376 | tf_op jit(solution)/shard_map/ppermute | solution.py:361
  10.5 3.4 %collective-permute-start = (bf16[72,1024]{1,0:T(8,128)(2,1)}, bf16[72,1024]{1,0:T(8,128)(2,1)S(1)}, u32[]{:S(2)}, u32[]{:S(2)}) collective-permute-start(bf16[72,1024]{1,0:T(8,128)(2,1)} %get-tuple-element.61), channel_id=1, source_target_pairs={{1,0},{0,1},{3,2},{2,3},{5,4},{4,5},{7,6},{6,7},{9,8},{8,9},{11,10... | collective-permute-start | bytes 442376 | tf_op jit(solution)/shard_map/ppermute | solution.py:356
  10.5 0.9 %copy-start = (bf16[80,1024]{1,0:T(8,128)(2,1)S(1)}, bf16[80,1024]{1,0:T(8,128)(2,1)}, u32[]{:S(2)}) copy-start(bf16[80,1024]{1,0:T(8,128)(2,1)} %get-tuple-element.39.rows_ref) | copy-start | bytes 491524
  13.4 1.4 %collective-permute-start.4 = (bf16[72,1024]{1,0:T(8,128)(2,1)S(1)}, bf16[72,1024]{1,0:T(8,128)(2,1)S(1)}, u32[]{:S(2)}, u32[]{:S(2)}) collective-permute-start(bf16[72,1024]{1,0:T(8,128)(2,1)S(1)} %collective-permute-done.1.refs_2_), channel_id=1, source_target_pairs={{1,0},{0,1},{3,2},{2,3},{5,4},{4,5},{7,6},{6,7},{9,8},{8,9},{11,10... | collective-permute-start | bytes 442376 | tf_op jit(solution)/shard_map/ppermute | solution.py:356
  13.4 1.6 %collective-permute-start.5 = (bf16[72,1024]{1,0:T(8,128)(2,1)S(1)}, bf16[72,1024]{1,0:T(8,128)(2,1)S(1)}, u32[]{:S(2)}, u32[]{:S(2)}) collective-permute-start(bf16[72,1024]{1,0:T(8,128)(2,1)S(1)} %collective-permute-done.2.refs_4_), channel_id=1, source_target_pairs={{1,0},{0,1},{3,2},{2,3},{5,4},{4,5},{7,6},{6,7},{9,8},{8,9},{11,10... | collective-permute-start | bytes 442376 | tf_op jit(solution)/shard_map/ppermute | solution.py:356
  13.9 1.4 %collective-permute-start.6 = (bf16[72,1024]{1,0:T(8,128)(2,1)S(1)}, bf16[72,1024]{1,0:T(8,128)(2,1)S(1)}, u32[]{:S(2)}, u32[]{:S(2)}) collective-permute-start(bf16[72,1024]{1,0:T(8,128)(2,1)S(1)} %collective-permute-done.3.refs_6_), channel_id=1, source_target_pairs={{1,0},{0,1},{3,2},{2,3},{5,4},{4,5},{7,6},{6,7},{9,8},{8,9},{11,10... | collective-permute-start | bytes 442376 | tf_op jit(solution)/shard_map/ppermute | solution.py:356
  20.8 13.3 %collective-permute-start.10 = (bf16[72,1024]{1,0:T(8,128)(2,1)S(1)}, bf16[72,1024]{1,0:T(8,128)(2,1)S(1)}, u32[]{:S(2)}, u32[]{:S(2)}) collective-permute-start(bf16[72,1024]{1,0:T(8,128)(2,1)S(1)} %collective-permute-done.7.refs_0_), channel_id=1, source_target_pairs={{6,0},{7,1},{4,2},{5,3},{2,4},{3,5},{0,6},{1,7},{14,8},{15,9},{12,... | collective-permute-start | bytes 442376 | tf_op jit(solution)/shard_map/ppermute | solution.py:356
  22.6 11.5 %collective-permute-start.9 = (bf16[72,1024]{1,0:T(8,128)(2,1)S(1)}, bf16[72,1024]{1,0:T(8,128)(2,1)S(1)}, u32[]{:S(2)}, u32[]{:S(2)}) collective-permute-start(bf16[72,1024]{1,0:T(8,128)(2,1)S(1)} %collective-permute-done.7.refs_0_), channel_id=1, source_target_pairs={{4,0},{5,1},{6,2},{7,3},{0,4},{1,5},{2,6},{3,7},{12,8},{13,9},{14,... | collective-permute-start | bytes 442376 | tf_op jit(solution)/shard_map/ppermute | solution.py:356
  23.8 10.2 %collective-permute-start.8 = (bf16[72,1024]{1,0:T(8,128)(2,1)S(1)}, bf16[72,1024]{1,0:T(8,128)(2,1)S(1)}, u32[]{:S(2)}, u32[]{:S(2)}) collective-permute-start(bf16[72,1024]{1,0:T(8,128)(2,1)S(1)} %collective-permute-done.7.refs_0_), channel_id=1, source_target_pairs={{2,0},{3,1},{0,2},{1,3},{6,4},{7,5},{4,6},{5,7},{10,8},{11,9},{8,1... | collective-permute-start | bytes 442376 | tf_op jit(solution)/shard_map/ppermute | solution.py:356
  24.4 9.7 %collective-permute-start.11 = (bf16[72,1024]{1,0:T(8,128)(2,1)}, bf16[72,1024]{1,0:T(8,128)(2,1)S(1)}, u32[]{:S(2)}, u32[]{:S(2)}) collective-permute-start(bf16[72,1024]{1,0:T(8,128)(2,1)} %get-tuple-element.61), channel_id=1, source_target_pairs={{16,0},{24,8},{0,16},{8,24},{17,1},{25,9},{1,17},{9,25},{18,2},{26... | collective-permute-start | bytes 442376 | tf_op jit(solution)/shard_map/ppermute | solution.py:361
  34.1 2.8 %collective-permute-start.12 = (bf16[72,1024]{1,0:T(8,128)(2,1)S(1)}, bf16[72,1024]{1,0:T(8,128)(2,1)S(1)}, u32[]{:S(2)}, u32[]{:S(2)}) collective-permute-start(bf16[72,1024]{1,0:T(8,128)(2,1)S(1)} %collective-permute-done.7.refs_0_), channel_id=1, source_target_pairs={{1,0},{0,1},{3,2},{2,3},{5,4},{4,5},{7,6},{6,7},{9,8},{8,9},{11,10... | collective-permute-start | bytes 442376 | tf_op jit(solution)/shard_map/ppermute | solution.py:356
  34.2 4.0 %collective-permute-start.13 = (bf16[72,1024]{1,0:T(8,128)(2,1)S(1)}, bf16[72,1024]{1,0:T(8,128)(2,1)S(1)}, u32[]{:S(2)}, u32[]{:S(2)}) collective-permute-start(bf16[72,1024]{1,0:T(8,128)(2,1)S(1)} %collective-permute-done.8.refs_2_), channel_id=1, source_target_pairs={{1,0},{0,1},{3,2},{2,3},{5,4},{4,5},{7,6},{6,7},{9,8},{8,9},{11,10... | collective-permute-start | bytes 442376 | tf_op jit(solution)/shard_map/ppermute | solution.py:356
  34.7 4.0 %collective-permute-start.14 = (bf16[72,1024]{1,0:T(8,128)(2,1)S(1)}, bf16[72,1024]{1,0:T(8,128)(2,1)S(1)}, u32[]{:S(2)}, u32[]{:S(2)}) collective-permute-start(bf16[72,1024]{1,0:T(8,128)(2,1)S(1)} %collective-permute-done.9.refs_4_), channel_id=1, source_target_pairs={{1,0},{0,1},{3,2},{2,3},{5,4},{4,5},{7,6},{6,7},{9,8},{8,9},{11,10... | collective-permute-start | bytes 442376 | tf_op jit(solution)/shard_map/ppermute | solution.py:356
  34.7 3.9 %collective-permute-start.15 = (bf16[72,1024]{1,0:T(8,128)(2,1)S(1)}, bf16[72,1024]{1,0:T(8,128)(2,1)S(1)}, u32[]{:S(2)}, u32[]{:S(2)}) collective-permute-start(bf16[72,1024]{1,0:T(8,128)(2,1)S(1)} %collective-permute-done.10.refs_6_), channel_id=1, source_target_pairs={{1,0},{0,1},{3,2},{2,3},{5,4},{4,5},{7,6},{6,7},{9,8},{8,9},{11,10... | collective-permute-start | bytes 442376 | tf_op jit(solution)/shard_map/ppermute | solution.py:356
  35.2 13.3 %collective-permute-start.18 = (bf16[72,1024]{1,0:T(8,128)(2,1)S(1)}, bf16[72,1024]{1,0:T(8,128)(2,1)S(1)}, u32[]{:S(2)}, u32[]{:S(2)}) collective-permute-start(bf16[72,1024]{1,0:T(8,128)(2,1)S(1)} %collective-permute-done.11.refs_0_), channel_id=1, source_target_pairs={{6,0},{7,1},{4,2},{5,3},{2,4},{3,5},{0,6},{1,7},{14,8},{15,9},{12,... | collective-permute-start | bytes 442376 | tf_op jit(solution)/shard_map/ppermute | solution.py:356
  36.8 11.6 %collective-permute-start.17 = (bf16[72,1024]{1,0:T(8,128)(2,1)S(1)}, bf16[72,1024]{1,0:T(8,128)(2,1)S(1)}, u32[]{:S(2)}, u32[]{:S(2)}) collective-permute-start(bf16[72,1024]{1,0:T(8,128)(2,1)S(1)} %collective-permute-done.11.refs_0_), channel_id=1, source_target_pairs={{4,0},{5,1},{6,2},{7,3},{0,4},{1,5},{2,6},{3,7},{12,8},{13,9},{14,... | collective-permute-start | bytes 442376 | tf_op jit(solution)/shard_map/ppermute | solution.py:356
  38.1 10.3 %collective-permute-start.16 = (bf16[72,1024]{1,0:T(8,128)(2,1)S(1)}, bf16[72,1024]{1,0:T(8,128)(2,1)S(1)}, u32[]{:S(2)}, u32[]{:S(2)}) collective-permute-start(bf16[72,1024]{1,0:T(8,128)(2,1)S(1)} %collective-permute-done.11.refs_0_), channel_id=1, source_target_pairs={{2,0},{3,1},{0,2},{1,3},{6,4},{7,5},{4,6},{5,7},{10,8},{11,9},{8,1... | collective-permute-start | bytes 442376 | tf_op jit(solution)/shard_map/ppermute | solution.py:356
  48.5 1.4 %collective-permute-start.19 = (bf16[72,1024]{1,0:T(8,128)(2,1)S(1)}, bf16[72,1024]{1,0:T(8,128)(2,1)S(1)}, u32[]{:S(2)}, u32[]{:S(2)}) collective-permute-start(bf16[72,1024]{1,0:T(8,128)(2,1)S(1)} %collective-permute-done.11.refs_0_), channel_id=1, source_target_pairs={{1,0},{0,1},{3,2},{2,3},{5,4},{4,5},{7,6},{6,7},{9,8},{8,9},{11,10... | collective-permute-start | bytes 442376 | tf_op jit(solution)/shard_map/ppermute | solution.py:356
  48.6 1.6 %collective-permute-start.20 = (bf16[72,1024]{1,0:T(8,128)(2,1)S(1)}, bf16[72,1024]{1,0:T(8,128)(2,1)S(1)}, u32[]{:S(2)}, u32[]{:S(2)}) collective-permute-start(bf16[72,1024]{1,0:T(8,128)(2,1)S(1)} %collective-permute-done.16.refs_2_), channel_id=1, source_target_pairs={{1,0},{0,1},{3,2},{2,3},{5,4},{4,5},{7,6},{6,7},{9,8},{8,9},{11,10... | collective-permute-start | bytes 442376 | tf_op jit(solution)/shard_map/ppermute | solution.py:356
  49.1 1.4 %collective-permute-start.21 = (bf16[72,1024]{1,0:T(8,128)(2,1)S(1)}, bf16[72,1024]{1,0:T(8,128)(2,1)S(1)}, u32[]{:S(2)}, u32[]{:S(2)}) collective-permute-start(bf16[72,1024]{1,0:T(8,128)(2,1)S(1)} %collective-permute-done.17.refs_4_), channel_id=1, source_target_pairs={{1,0},{0,1},{3,2},{2,3},{5,4},{4,5},{7,6},{6,7},{9,8},{8,9},{11,10... | collective-permute-start | bytes 442376 | tf_op jit(solution)/shard_map/ppermute | solution.py:356
  49.1 1.5 %collective-permute-start.22 = (bf16[72,1024]{1,0:T(8,128)(2,1)S(1)}, bf16[72,1024]{1,0:T(8,128)(2,1)S(1)}, u32[]{:S(2)}, u32[]{:S(2)}) collective-permute-start(bf16[72,1024]{1,0:T(8,128)(2,1)S(1)} %collective-permute-done.18.refs_6_), channel_id=1, source_target_pairs={{1,0},{0,1},{3,2},{2,3},{5,4},{4,5},{7,6},{6,7},{9,8},{8,9},{11,10... | collective-permute-start | bytes 442376 | tf_op jit(solution)/shard_map/ppermute | solution.py:356

commit v5 on v4

--- a/solution.py
+++ b/solution.py
@@ -377,7 +377,7 @@
         plan, raw_samples, decimation_taps.reshape(1, -1), bandpass_taps.reshape(1, -1)
     )
     *tabs, kept = tables(plan, kept)
-    count = 32
+    count = 64
     own = same_core(piece)
     near = from_ahead(piece, 1)
     tabs, own[1:] = lax.optimization_barrier((tabs, own[1:]))

time: 60.6 us -> 60.5 us (level)
  no operation moved by 1% of the time
where the time goes in v5:
time: 60.5 us; the launch traced here: 60.3 us
  Pallas kernels  35 us (58%)
  starting transfers between devices  20.8 us (34%)
  waiting for transfers between devices  3.49 us (6%)
  local copies, waits for them, and re-layouts  0.92 us (2%)
    pallas_call x2, Pallas kernels, other_correlation(): pl.pallas_call(functools.partial(other_kernel, plan, count), grid=(plan.c...  19.5 us
    ppermute x21, starting transfers between devices, swap(): return lax.ppermute(piece, 'lag', [(i ^ mask, i) for i in range(count)])  14.2 us
    pallas_call x1, Pallas kernels, own_correlation(): pl.pallas_call(functools.partial(first_kernel, plan, count), grid=(plan.c...  7.1 us
    ppermute x2, starting transfers between devices, from_ahead(): lax.ppermute(piece, 'chan', [((i + distance) % count, i) for i in range(c...  6.67 us
    pallas_call x1, Pallas kernels, prepare_own(): pl.pallas_call(functools.partial(own_kernel, plan), out_shape=(jax.ShapeD...  5.53 us
    ppermute x21, waiting for transfers between devices, swap(): return lax.ppermute(piece, 'lag', [(i ^ mask, i) for i in range(count)])  3.49 us
    pallas_call x1, Pallas kernels, local_rows(): pl.pallas_call(functools.partial(local_kernel, plan), out_shape=(jax.Shap...  1.99 us
  transfers between devices with their start and end apart: 23, of which 9 were waited for; matrix products, arithmetic and copies ran while one was open for 0% of the time, Pallas kernels for 29%

profile of v5, /device:TPU:0, one launch (start us, length us, event | category | flops | bytes accessed | tf_op | source)
XLA Modules:
  0.0 60.3 jit_solution(5712613571039380507)
XLA Ops:
  0.0 2.0 %local_rows.1 = (bf16[72,1024]{1,0:T(8,128)(2,1)}, bf16[80,1024]{1,0:T(8,128)(2,1)}) custom-call(f32[1,16]{1,0:T(1,128)} %bitcast.5, f32[1,65]{1,0:T(1,128)} %bitcast.6, bf16[100,8,128]{2,1,0:T(8,128)(2,1)} %bitcast.4), custom_call_target="tpu_custom_call" | custom-call | tf_op jit(solution)/shard_map/local_rows/pallas_call | solution.py:83
  2.0 3.9 %collective-permute-start.3 = (bf16[72,1024]{1,0:T(8,128)(2,1)}, bf16[72,1024]{1,0:T(8,128)(2,1)S(1)}, u32[]{:S(2)}, u32[]{:S(2)}) collective-permute-start(bf16[72,1024]{1,0:T(8,128)(2,1)} %get-tuple-element.61), channel_id=1, source_target_pairs={{6,0},{7,1},{4,2},{5,3},{2,4},{3,5},{0,6},{1,7},{14,8},{15,9},{12,... | collective-permute-start | bytes 442376 | tf_op jit(solution)/shard_map/ppermute | solution.py:356
  5.9 0.5 collective-permute-start.2
  6.4 4.1 %collective-permute-start.7 = (bf16[72,1024]{1,0:T(8,128)(2,1)}, bf16[72,1024]{1,0:T(8,128)(2,1)S(1)}, u32[]{:S(2)}, u32[]{:S(2)}) collective-permute-start(bf16[72,1024]{1,0:T(8,128)(2,1)} %get-tuple-element.61), channel_id=1, source_target_pairs={{8,0},{16,8},{24,16},{0,24},{9,1},{17,9},{25,17},{1,25},{10,2},{18... | collective-permute-start | bytes 442376 | tf_op jit(solution)/shard_map/ppermute | solution.py:361
  10.5 0.9 %copy-done = bf16[80,1024]{1,0:T(8,128)(2,1)S(1)} copy-done((bf16[80,1024]{1,0:T(8,128)(2,1)S(1)}, bf16[80,1024]{1,0:T(8,128)(2,1)}, u32[]{:S(2)}) %copy-start) | copy-done | bytes 163864
  11.4 0.9 %tables.1 = (bf16[400,704]{1,0:T(8,128)(2,1)S(1)}, bf16[64,640]{1,0:T(8,128)(2,1)S(1)}, bf16[72,1024]{1,0:T(8,128)(2,1)S(1)}) custom-call(bf16[80,1024]{1,0:T(8,128)(2,1)S(1)} %copy-done), custom_call_target="tpu_custom_call" | custom-call | flops 500000000 | bytes 2000000 | tf_op jit(solution)/shard_map/tables/pallas_call | solution.py:138
  12.4 0.7 %collective-permute-done.2.refs_4_ = bf16[72,1024]{1,0:T(8,128)(2,1)S(1)} collective-permute-done((bf16[72,1024]{1,0:T(8,128)(2,1)}, bf16[72,1024]{1,0:T(8,128)(2,1)S(1)}, u32[]{:S(2)}, u32[]{:S(2)}) %collective-permute-start.2) | collective-permute-done | bytes 147488 | tf_op jit(solution)/shard_map/ppermute | solution.py:356
  13.1 0.3 collective-permute-done.1.refs_2_
  13.4 0.5 collective-permute-start.5
  13.9 0.8 %collective-permute-done.4.refs_3_ = bf16[72,1024]{1,0:T(8,128)(2,1)S(1)} collective-permute-done((bf16[72,1024]{1,0:T(8,128)(2,1)S(1)}, bf16[72,1024]{1,0:T(8,128)(2,1)S(1)}, u32[]{:S(2)}, u32[]{:S(2)}) %collective-permute-start.4) | collective-permute-done | bytes 147488 | tf_op jit(solution)/shard_map/ppermute | solution.py:356
  14.8 0.2 collective-permute-done.5.refs_5_
  15.0 0.3 collective-permute-done.6.refs_7_
  15.3 5.5 %prepare_own.1 = (bf16[3,1024,1792]{2,1,0:T(8,128)(2,1)S(1)}, bf16[3,1792,256]{2,1,0:T(8,128)(2,1)S(1)}) custom-call(s32[1]{0:T(128)} %bitcast.place_ref, bf16[72,1024]{1,0:T(8,128)(2,1)S(1)} %get-tuple-element.40.refs_0_, bf16[72,1024]{1,0:T(8,128)(2,1)S(1)} %collective-permute-done.refs_1_, bf16[72,1024]{1,0:T(8,128)(2,1)S(1)} %collective-permute-done.1.refs_2_, ...), custom_call_target="tpu_custom_call" | custom-call | flops 100000000 | bytes 262144 | tf_op jit(solution)/shard_map/prepare_own/pallas_call | solution.py:297
  20.8 1.8 %collective-permute-start.10 = (bf16[72,1024]{1,0:T(8,128)(2,1)S(1)}, bf16[72,1024]{1,0:T(8,128)(2,1)S(1)}, u32[]{:S(2)}, u32[]{:S(2)}) collective-permute-start(bf16[72,1024]{1,0:T(8,128)(2,1)S(1)} %collective-permute-done.7.refs_0_), channel_id=1, source_target_pairs={{6,0},{7,1},{4,2},{5,3},{2,4},{3,5},{0,6},{1,7},{14,8},{15,9},{12,... | collective-permute-start | bytes 442376 | tf_op jit(solution)/shard_map/ppermute | solution.py:356
  22.6 1.3 %collective-permute-start.9 = (bf16[72,1024]{1,0:T(8,128)(2,1)S(1)}, bf16[72,1024]{1,0:T(8,128)(2,1)S(1)}, u32[]{:S(2)}, u32[]{:S(2)}) collective-permute-start(bf16[72,1024]{1,0:T(8,128)(2,1)S(1)} %collective-permute-done.7.refs_0_), channel_id=1, source_target_pairs={{4,0},{5,1},{6,2},{7,3},{0,4},{1,5},{2,6},{3,7},{12,8},{13,9},{14,... | collective-permute-start | bytes 442376 | tf_op jit(solution)/shard_map/ppermute | solution.py:356
  23.8 0.5 collective-permute-start.8
  24.4 2.6 %collective-permute-start.11 = (bf16[72,1024]{1,0:T(8,128)(2,1)}, bf16[72,1024]{1,0:T(8,128)(2,1)S(1)}, u32[]{:S(2)}, u32[]{:S(2)}) collective-permute-start(bf16[72,1024]{1,0:T(8,128)(2,1)} %get-tuple-element.61), channel_id=1, source_target_pairs={{16,0},{24,8},{0,16},{8,24},{17,1},{25,9},{1,17},{9,25},{18,2},{26... | collective-permute-start | bytes 442376 | tf_op jit(solution)/shard_map/ppermute | solution.py:361
  26.9 7.1 %own_correlation.1.refs_11_ = f32[128,3,64,128]{3,2,1,0:T(8,128)} custom-call(bf16[3,1024,1792]{2,1,0:T(8,128)(2,1)S(1)} %get-tuple-element.58.left_ref.refs_10_, bf16[3,1792,256]{2,1,0:T(8,128)(2,1)S(1)} %get-tuple-element.59.right_ref), custom_call_target="tpu_custom_call" | custom-call | flops 5234491392 | bytes 8388608 | tf_op jit(solution)/shard_map/own_correlation/pallas_call | solution.py:324
  34.2 0.5 collective-permute-start.13
  34.7 0.1 collective-permute-start.14
  34.7 0.4 collective-permute-start.15
  35.2 1.7 %collective-permute-start.18 = (bf16[72,1024]{1,0:T(8,128)(2,1)S(1)}, bf16[72,1024]{1,0:T(8,128)(2,1)S(1)}, u32[]{:S(2)}, u32[]{:S(2)}) collective-permute-start(bf16[72,1024]{1,0:T(8,128)(2,1)S(1)} %collective-permute-done.11.refs_0_), channel_id=1, source_target_pairs={{6,0},{7,1},{4,2},{5,3},{2,4},{3,5},{0,6},{1,7},{14,8},{15,9},{12,... | collective-permute-start | bytes 442376 | tf_op jit(solution)/shard_map/ppermute | solution.py:356
  36.8 1.3 %collective-permute-start.17 = (bf16[72,1024]{1,0:T(8,128)(2,1)S(1)}, bf16[72,1024]{1,0:T(8,128)(2,1)S(1)}, u32[]{:S(2)}, u32[]{:S(2)}) collective-permute-start(bf16[72,1024]{1,0:T(8,128)(2,1)S(1)} %collective-permute-done.11.refs_0_), channel_id=1, source_target_pairs={{4,0},{5,1},{6,2},{7,3},{0,4},{1,5},{2,6},{3,7},{12,8},{13,9},{14,... | collective-permute-start | bytes 442376 | tf_op jit(solution)/shard_map/ppermute | solution.py:356
  38.1 0.5 collective-permute-start.16
  38.7 9.7 %other_correlation.2.refs_11_ = f32[128,3,64,128]{3,2,1,0:T(8,128)} custom-call(s32[1]{0:T(128)} %bitcast.place_ref, bf16[72,1024]{1,0:T(8,128)(2,1)S(1)} %collective-permute-done.7.refs_0_, bf16[72,1024]{1,0:T(8,128)(2,1)S(1)} %collective-permute-done.12.refs_1_, ...), custom_call_target="tpu_custom_call", output_to_operand_aliasing={{}: (12, {})} | custom-call | flops 5234491392 | bytes 8388608 | tf_op jit(solution)/shard_map/other_correlation/pallas_call | solution.py:339
  48.5 0.5 collective-permute-start.20
  49.1 0.4 collective-permute-start.22
  49.5 0.3 collective-permute-done.19.refs_1_
  49.9 0.2 collective-permute-done.20.refs_3_
  50.1 0.3 collective-permute-done.21.refs_5_
  50.4 0.2 collective-permute-done.22.refs_7_
  50.6 9.7 %other_correlation.3 = f32[128,3,64,128]{3,2,1,0:T(8,128)} custom-call(s32[1]{0:T(128)} %bitcast.place_ref, bf16[72,1024]{1,0:T(8,128)(2,1)S(1)} %collective-permute-done.11.refs_0_, bf16[72,1024]{1,0:T(8,128)(2,1)S(1)} %collective-permute-done.19.refs_1_, bf16[72,1024]{1,0:T(8,128)(2,1)S(1)} %collective-permute-done.16.refs_2_, ...), custom_call_target="tpu_custom_call", output_to_operand_aliasing={{}: (12, {})} | custom-call | flops 5234491392 | bytes 8388608 | tf_op jit(solution)/shard_map/other_correlation/pallas_call | solution.py:339
  (22 shorter events, 0.3 us)
Async XLA Ops:
  2.0 10.4 %collective-permute-start.3 = (bf16[72,1024]{1,0:T(8,128)(2,1)}, bf16[72,1024]{1,0:T(8,128)(2,1)S(1)}, u32[]{:S(2)}, u32[]{:S(2)}) collective-permute-start(bf16[72,1024]{1,0:T(8,128)(2,1)} %get-tuple-element.61), channel_id=1, source_target_pairs={{6,0},{7,1},{4,2},{5,3},{2,4},{3,5},{0,6},{1,7},{14,8},{15,9},{12,... | collective-permute-start | bytes 442376 | tf_op jit(solution)/shard_map/ppermute | solution.py:356
  5.9 7.2 %collective-permute-start.2 = (bf16[72,1024]{1,0:T(8,128)(2,1)}, bf16[72,1024]{1,0:T(8,128)(2,1)S(1)}, u32[]{:S(2)}, u32[]{:S(2)}) collective-permute-start(bf16[72,1024]{1,0:T(8,128)(2,1)} %get-tuple-element.61), channel_id=1, source_target_pairs={{4,0},{5,1},{6,2},{7,3},{0,4},{1,5},{2,6},{3,7},{12,8},{13,9},{14,... | collective-permute-start | bytes 442376 | tf_op jit(solution)/shard_map/ppermute | solution.py:356
  6.4 7.0 %collective-permute-start.1 = (bf16[72,1024]{1,0:T(8,128)(2,1)}, bf16[72,1024]{1,0:T(8,128)(2,1)S(1)}, u32[]{:S(2)}, u32[]{:S(2)}) collective-permute-start(bf16[72,1024]{1,0:T(8,128)(2,1)} %get-tuple-element.61), channel_id=1, source_target_pairs={{2,0},{3,1},{0,2},{1,3},{6,4},{7,5},{4,6},{5,7},{10,8},{11,9},{8,1... | collective-permute-start | bytes 442376 | tf_op jit(solution)/shard_map/ppermute | solution.py:356
  6.4 7.5 %collective-permute-start.7 = (bf16[72,1024]{1,0:T(8,128)(2,1)}, bf16[72,1024]{1,0:T(8,128)(2,1)S(1)}, u32[]{:S(2)}, u32[]{:S(2)}) collective-permute-start(bf16[72,1024]{1,0:T(8,128)(2,1)} %get-tuple-element.61), channel_id=1, source_target_pairs={{8,0},{16,8},{24,16},{0,24},{9,1},{17,9},{25,17},{1,25},{10,2},{18... | collective-permute-start | bytes 442376 | tf_op jit(solution)/shard_map/ppermute | solution.py:361
  10.5 3.4 %collective-permute-start = (bf16[72,1024]{1,0:T(8,128)(2,1)}, bf16[72,1024]{1,0:T(8,128)(2,1)S(1)}, u32[]{:S(2)}, u32[]{:S(2)}) collective-permute-start(bf16[72,1024]{1,0:T(8,128)(2,1)} %get-tuple-element.61), channel_id=1, source_target_pairs={{1,0},{0,1},{3,2},{2,3},{5,4},{4,5},{7,6},{6,7},{9,8},{8,9},{11,10... | collective-permute-start | bytes 442376 | tf_op jit(solution)/shard_map/ppermute | solution.py:356
  10.5 0.9 %copy-start = (bf16[80,1024]{1,0:T(8,128)(2,1)S(1)}, bf16[80,1024]{1,0:T(8,128)(2,1)}, u32[]{:S(2)}) copy-start(bf16[80,1024]{1,0:T(8,128)(2,1)} %get-tuple-element.39.rows_ref) | copy-start | bytes 491524
  13.4 1.4 %collective-permute-start.4 = (bf16[72,1024]{1,0:T(8,128)(2,1)S(1)}, bf16[72,1024]{1,0:T(8,128)(2,1)S(1)}, u32[]{:S(2)}, u32[]{:S(2)}) collective-permute-start(bf16[72,1024]{1,0:T(8,128)(2,1)S(1)} %collective-permute-done.1.refs_2_), channel_id=1, source_target_pairs={{1,0},{0,1},{3,2},{2,3},{5,4},{4,5},{7,6},{6,7},{9,8},{8,9},{11,10... | collective-permute-start | bytes 442376 | tf_op jit(solution)/shard_map/ppermute | solution.py:356
  13.4 1.6 %collective-permute-start.5 = (bf16[72,1024]{1,0:T(8,128)(2,1)S(1)}, bf16[72,1024]{1,0:T(8,128)(2,1)S(1)}, u32[]{:S(2)}, u32[]{:S(2)}) collective-permute-start(bf16[72,1024]{1,0:T(8,128)(2,1)S(1)} %collective-permute-done.2.refs_4_), channel_id=1, source_target_pairs={{1,0},{0,1},{3,2},{2,3},{5,4},{4,5},{7,6},{6,7},{9,8},{8,9},{11,10... | collective-permute-start | bytes 442376 | tf_op jit(solution)/shard_map/ppermute | solution.py:356
  13.9 1.4 %collective-permute-start.6 = (bf16[72,1024]{1,0:T(8,128)(2,1)S(1)}, bf16[72,1024]{1,0:T(8,128)(2,1)S(1)}, u32[]{:S(2)}, u32[]{:S(2)}) collective-permute-start(bf16[72,1024]{1,0:T(8,128)(2,1)S(1)} %collective-permute-done.3.refs_6_), channel_id=1, source_target_pairs={{1,0},{0,1},{3,2},{2,3},{5,4},{4,5},{7,6},{6,7},{9,8},{8,9},{11,10... | collective-permute-start | bytes 442376 | tf_op jit(solution)/shard_map/ppermute | solution.py:356
  20.8 13.3 %collective-permute-start.10 = (bf16[72,1024]{1,0:T(8,128)(2,1)S(1)}, bf16[72,1024]{1,0:T(8,128)(2,1)S(1)}, u32[]{:S(2)}, u32[]{:S(2)}) collective-permute-start(bf16[72,1024]{1,0:T(8,128)(2,1)S(1)} %collective-permute-done.7.refs_0_), channel_id=1, source_target_pairs={{6,0},{7,1},{4,2},{5,3},{2,4},{3,5},{0,6},{1,7},{14,8},{15,9},{12,... | collective-permute-start | bytes 442376 | tf_op jit(solution)/shard_map/ppermute | solution.py:356
  22.6 11.5 %collective-permute-start.9 = (bf16[72,1024]{1,0:T(8,128)(2,1)S(1)}, bf16[72,1024]{1,0:T(8,128)(2,1)S(1)}, u32[]{:S(2)}, u32[]{:S(2)}) collective-permute-start(bf16[72,1024]{1,0:T(8,128)(2,1)S(1)} %collective-permute-done.7.refs_0_), channel_id=1, source_target_pairs={{4,0},{5,1},{6,2},{7,3},{0,4},{1,5},{2,6},{3,7},{12,8},{13,9},{14,... | collective-permute-start | bytes 442376 | tf_op jit(solution)/shard_map/ppermute | solution.py:356
  23.8 10.2 %collective-permute-start.8 = (bf16[72,1024]{1,0:T(8,128)(2,1)S(1)}, bf16[72,1024]{1,0:T(8,128)(2,1)S(1)}, u32[]{:S(2)}, u32[]{:S(2)}) collective-permute-start(bf16[72,1024]{1,0:T(8,128)(2,1)S(1)} %collective-permute-done.7.refs_0_), channel_id=1, source_target_pairs={{2,0},{3,1},{0,2},{1,3},{6,4},{7,5},{4,6},{5,7},{10,8},{11,9},{8,1... | collective-permute-start | bytes 442376 | tf_op jit(solution)/shard_map/ppermute | solution.py:356
  24.4 9.7 %collective-permute-start.11 = (bf16[72,1024]{1,0:T(8,128)(2,1)}, bf16[72,1024]{1,0:T(8,128)(2,1)S(1)}, u32[]{:S(2)}, u32[]{:S(2)}) collective-permute-start(bf16[72,1024]{1,0:T(8,128)(2,1)} %get-tuple-element.61), channel_id=1, source_target_pairs={{16,0},{24,8},{0,16},{8,24},{17,1},{25,9},{1,17},{9,25},{18,2},{26... | collective-permute-start | bytes 442376 | tf_op jit(solution)/shard_map/ppermute | solution.py:361
  34.1 2.8 %collective-permute-start.12 = (bf16[72,1024]{1,0:T(8,128)(2,1)S(1)}, bf16[72,1024]{1,0:T(8,128)(2,1)S(1)}, u32[]{:S(2)}, u32[]{:S(2)}) collective-permute-start(bf16[72,1024]{1,0:T(8,128)(2,1)S(1)} %collective-permute-done.7.refs_0_), channel_id=1, source_target_pairs={{1,0},{0,1},{3,2},{2,3},{5,4},{4,5},{7,6},{6,7},{9,8},{8,9},{11,10... | collective-permute-start | bytes 442376 | tf_op jit(solution)/shard_map/ppermute | solution.py:356
  34.2 4.0 %collective-permute-start.13 = (bf16[72,1024]{1,0:T(8,128)(2,1)S(1)}, bf16[72,1024]{1,0:T(8,128)(2,1)S(1)}, u32[]{:S(2)}, u32[]{:S(2)}) collective-permute-start(bf16[72,1024]{1,0:T(8,128)(2,1)S(1)} %collective-permute-done.8.refs_2_), channel_id=1, source_target_pairs={{1,0},{0,1},{3,2},{2,3},{5,4},{4,5},{7,6},{6,7},{9,8},{8,9},{11,10... | collective-permute-start | bytes 442376 | tf_op jit(solution)/shard_map/ppermute | solution.py:356
  34.7 4.0 %collective-permute-start.14 = (bf16[72,1024]{1,0:T(8,128)(2,1)S(1)}, bf16[72,1024]{1,0:T(8,128)(2,1)S(1)}, u32[]{:S(2)}, u32[]{:S(2)}) collective-permute-start(bf16[72,1024]{1,0:T(8,128)(2,1)S(1)} %collective-permute-done.9.refs_4_), channel_id=1, source_target_pairs={{1,0},{0,1},{3,2},{2,3},{5,4},{4,5},{7,6},{6,7},{9,8},{8,9},{11,10... | collective-permute-start | bytes 442376 | tf_op jit(solution)/shard_map/ppermute | solution.py:356
  34.7 3.9 %collective-permute-start.15 = (bf16[72,1024]{1,0:T(8,128)(2,1)S(1)}, bf16[72,1024]{1,0:T(8,128)(2,1)S(1)}, u32[]{:S(2)}, u32[]{:S(2)}) collective-permute-start(bf16[72,1024]{1,0:T(8,128)(2,1)S(1)} %collective-permute-done.10.refs_6_), channel_id=1, source_target_pairs={{1,0},{0,1},{3,2},{2,3},{5,4},{4,5},{7,6},{6,7},{9,8},{8,9},{11,10... | collective-permute-start | bytes 442376 | tf_op jit(solution)/shard_map/ppermute | solution.py:356
  35.2 13.2 %collective-permute-start.18 = (bf16[72,1024]{1,0:T(8,128)(2,1)S(1)}, bf16[72,1024]{1,0:T(8,128)(2,1)S(1)}, u32[]{:S(2)}, u32[]{:S(2)}) collective-permute-start(bf16[72,1024]{1,0:T(8,128)(2,1)S(1)} %collective-permute-done.11.refs_0_), channel_id=1, source_target_pairs={{6,0},{7,1},{4,2},{5,3},{2,4},{3,5},{0,6},{1,7},{14,8},{15,9},{12,... | collective-permute-start | bytes 442376 | tf_op jit(solution)/shard_map/ppermute | solution.py:356
  36.8 11.6 %collective-permute-start.17 = (bf16[72,1024]{1,0:T(8,128)(2,1)S(1)}, bf16[72,1024]{1,0:T(8,128)(2,1)S(1)}, u32[]{:S(2)}, u32[]{:S(2)}) collective-permute-start(bf16[72,1024]{1,0:T(8,128)(2,1)S(1)} %collective-permute-done.11.refs_0_), channel_id=1, source_target_pairs={{4,0},{5,1},{6,2},{7,3},{0,4},{1,5},{2,6},{3,7},{12,8},{13,9},{14,... | collective-permute-start | bytes 442376 | tf_op jit(solution)/shard_map/ppermute | solution.py:356
  38.1 10.3 %collective-permute-start.16 = (bf16[72,1024]{1,0:T(8,128)(2,1)S(1)}, bf16[72,1024]{1,0:T(8,128)(2,1)S(1)}, u32[]{:S(2)}, u32[]{:S(2)}) collective-permute-start(bf16[72,1024]{1,0:T(8,128)(2,1)S(1)} %collective-permute-done.11.refs_0_), channel_id=1, source_target_pairs={{2,0},{3,1},{0,2},{1,3},{6,4},{7,5},{4,6},{5,7},{10,8},{11,9},{8,1... | collective-permute-start | bytes 442376 | tf_op jit(solution)/shard_map/ppermute | solution.py:356
  48.4 1.4 %collective-permute-start.19 = (bf16[72,1024]{1,0:T(8,128)(2,1)S(1)}, bf16[72,1024]{1,0:T(8,128)(2,1)S(1)}, u32[]{:S(2)}, u32[]{:S(2)}) collective-permute-start(bf16[72,1024]{1,0:T(8,128)(2,1)S(1)} %collective-permute-done.11.refs_0_), channel_id=1, source_target_pairs={{1,0},{0,1},{3,2},{2,3},{5,4},{4,5},{7,6},{6,7},{9,8},{8,9},{11,10... | collective-permute-start | bytes 442376 | tf_op jit(solution)/shard_map/ppermute | solution.py:356
  48.5 1.6 %collective-permute-start.20 = (bf16[72,1024]{1,0:T(8,128)(2,1)S(1)}, bf16[72,1024]{1,0:T(8,128)(2,1)S(1)}, u32[]{:S(2)}, u32[]{:S(2)}) collective-permute-start(bf16[72,1024]{1,0:T(8,128)(2,1)S(1)} %collective-permute-done.16.refs_2_), channel_id=1, source_target_pairs={{1,0},{0,1},{3,2},{2,3},{5,4},{4,5},{7,6},{6,7},{9,8},{8,9},{11,10... | collective-permute-start | bytes 442376 | tf_op jit(solution)/shard_map/ppermute | solution.py:356
  49.0 1.4 %collective-permute-start.21 = (bf16[72,1024]{1,0:T(8,128)(2,1)S(1)}, bf16[72,1024]{1,0:T(8,128)(2,1)S(1)}, u32[]{:S(2)}, u32[]{:S(2)}) collective-permute-start(bf16[72,1024]{1,0:T(8,128)(2,1)S(1)} %collective-permute-done.17.refs_4_), channel_id=1, source_target_pairs={{1,0},{0,1},{3,2},{2,3},{5,4},{4,5},{7,6},{6,7},{9,8},{8,9},{11,10... | collective-permute-start | bytes 442376 | tf_op jit(solution)/shard_map/ppermute | solution.py:356
  49.1 1.5 %collective-permute-start.22 = (bf16[72,1024]{1,0:T(8,128)(2,1)S(1)}, bf16[72,1024]{1,0:T(8,128)(2,1)S(1)}, u32[]{:S(2)}, u32[]{:S(2)}) collective-permute-start(bf16[72,1024]{1,0:T(8,128)(2,1)S(1)} %collective-permute-done.18.refs_6_), channel_id=1, source_target_pairs={{1,0},{0,1},{3,2},{2,3},{5,4},{4,5},{7,6},{6,7},{9,8},{8,9},{11,10... | collective-permute-start | bytes 442376 | tf_op jit(solution)/shard_map/ppermute | solution.py:356
